TPU v7x, 128 devices: a whole 4x4x4 slice. The times are simulated.
128 devices in a mesh: scen: 16 (over y, x), veh: 8 (over z, core).
Axes of the slice: x: 4, y: 4, z: 4, core: 2. Of those that a mesh axis runs over, the one named last changes fastest.
Arguments:
- start_plan: bfloat16 [256, 7168, 128], P('scen', 'veh'), may hold values from -6 to 6
- linear_cost: bfloat16 [256, 7168, 128], P('scen', 'veh'), may hold values from -12 to 12
- price: bfloat16 [256, 7168, 128], P('scen', 'veh'), may hold values from -6 to 6
- anchor: bfloat16 [16, 7168, 128], P(None, 'veh'), may hold values from -6 to 6
- hessian: bfloat16 [256, 128, 128], P('scen'), as said below
- usage_coef: bfloat16 [7168, 128], P('veh'), may hold values from -1.5 to 1.5
- crew_limit: float32 [256, 350], P('scen'), may hold values from -48 to 48
- crew_dual: float32 [256, 350], P('scen'), may hold values from 0 to 2
- crew_row: int32 [7168], P('veh'), may hold values from 0 to 349
- bundle_of: int32 [256, 1], replicated, may hold values from 0 to 15
- scen_weight: int32 [256], replicated, may hold values from 1 to 8
Outputs:
- new_plan: bfloat16 [256, 7168, 128], P('scen', 'veh')
- new_price: bfloat16 [256, 7168, 128], P('scen', 'veh')
- bundle_mean: bfloat16 [16, 7168, 128], P('scen', 'veh')
- new_dual: float32 [256, 350], P('scen')
- gap: float32 [], replicated
Inputs may be any that keep to these rules, and one draw needn't show every extreme that they name: `bundle_of`: every bundle holds one scenario or more. `hessian`: symmetric.
All inputs are finite; a program needn't handle non-finite values.
Results may differ from a plain program's by a relative error of at most 0.0013.
The roundings to bfloat16 on the way count: a program that leaves them out, or rounds other values in their place, can miss the bound.
Values sent between devices are 32-bit elements; how exact they have to be, the bound alone decides.
No kernel may reach another device: no remote copies, remote signals or barrier semaphores. Data moves between devices by JAX's collectives and lax.ppermute only.
A program may use at most 128 MiB of HBM per device.

v0:
```python
import jax
import jax.numpy as jnp
from jax import lax
from jax.sharding import PartitionSpec as P

ITERS = 12


penalty = 1.0
step_size = 0.02
dual_step = 0.02
highest = lax.Precision.HIGHEST


def shards(
    start_plan,
    linear_cost,
    price,
    anchor,
    hessian,
    usage_coef,
    crew_limit,
    crew_dual,
    crew_row,
    bundle_of,
    scen_weight,
):
    local_scen = start_plan.shape[0]
    bundle_count = anchor.shape[0]
    crew_count = crew_limit.shape[1]
    offset = lax.axis_index("scen") * local_scen
    all_bundles = bundle_of[:, 0]
    my_bundles = lax.dynamic_slice_in_dim(all_bundles, offset, local_scen)
    my_weights = lax.dynamic_slice_in_dim(scen_weight, offset, local_scen).astype(jnp.float32)
    bundle_ids = jnp.arange(bundle_count, dtype=jnp.int32)
    selector = (my_bundles[:, None] == bundle_ids[None, :]).astype(jnp.float32)
    anchored = jnp.einsum(
        "sb,bvi->svi", selector.astype(jnp.bfloat16), anchor, preferred_element_type=jnp.float32
    )
    linear_part = linear_cost.astype(jnp.float32) + price.astype(jnp.float32) - penalty * anchored
    coefficient = usage_coef.astype(jnp.float32)
    crew_map = (crew_row[:, None] == jnp.arange(crew_count, dtype=jnp.int32)[None, :]).astype(
        jnp.float32
    )

    def advance(index, state_pair):
        roster, multiplier = state_pair
        rounded = roster.astype(jnp.bfloat16)
        curvature = jnp.einsum("svi,sij->svj", rounded, hessian, preferred_element_type=jnp.float32)
        consumed = jnp.sum(roster * coefficient[None], axis=2)
        partial_use = jnp.dot(consumed, crew_map, precision=highest)
        usage = lax.psum(partial_use, "veh")
        updated = jnp.maximum(multiplier + dual_step * (usage - crew_limit), 0.0)
        per_vehicle = jnp.dot(multiplier, crew_map.T, precision=highest)
        gradient = (
            curvature + linear_part + penalty * roster + per_vehicle[:, :, None] * coefficient[None]
        )
        return (roster - step_size * gradient, updated)

    roster, multiplier = lax.fori_loop(
        0, ITERS, advance, (start_plan.astype(jnp.float32), crew_dual)
    )
    weighted_pick = selector * my_weights[:, None]
    every_weight = jnp.sum(
        (all_bundles[:, None] == bundle_ids[None, :]).astype(jnp.float32)
        * scen_weight.astype(jnp.float32)[:, None],
        axis=0,
    )
    owned_rows = bundle_count // lax.axis_size("scen")
    own_start = lax.axis_index("scen") * owned_rows
    partial_sums = jnp.einsum("sb,svi->bvi", weighted_pick, roster, precision=highest)
    totals = lax.psum(partial_sums, "scen")
    every_mean = totals / every_weight[:, None, None]
    own_mean = lax.dynamic_slice_in_dim(every_mean, own_start, owned_rows)
    mean_here = jnp.einsum("sb,bvi->svi", selector, every_mean, precision=highest)
    deviation = roster - mean_here
    new_price = (price.astype(jnp.float32) + penalty * deviation).astype(jnp.bfloat16)
    spread = jnp.sum(my_weights * jnp.sum(deviation * deviation, axis=(1, 2)))
    spread_total = lax.psum(spread, ("scen", "veh"))
    entries = start_plan.shape[1] * lax.axis_size("veh") * start_plan.shape[2]
    gap = jnp.sqrt(spread_total / (jnp.sum(scen_weight.astype(jnp.float32)) * entries))
    return (roster.astype(jnp.bfloat16), new_price, own_mean.astype(jnp.bfloat16), multiplier, gap)


def solution(mesh):
    return jax.shard_map(
        shards,
        mesh=mesh,
        in_specs=(
            P("scen", "veh", None),
            P("scen", "veh", None),
            P("scen", "veh", None),
            P(None, "veh", None),
            P("scen", None, None),
            P("veh", None),
            P("scen", None),
            P("scen", None),
            P("veh"),
            P(),
            P(),
        ),
        out_specs=(
            P("scen", "veh", None),
            P("scen", "veh", None),
            P("scen", "veh", None),
            P("scen", None),
            P(),
        ),
        check_vma=False,
    )
```

profile of v0, /device:TPU:0, one launch (start us, length us, event | category | flops | bytes accessed | tf_op | source)
XLA Modules:
  0.0 731.3 jit_solution(10766129550734030654)
XLA Ops:
  7.9 10.2 %fusion.12 = f32[16,896,128]{2,0,1:T(8,128)S(1)} fusion(bf16[16,896,128]{2,1,0:T(8,128)(2,1)} %param.14, bf16[16,896,128]{2,1,0:T(8,128)(2,1)} %param.15, bf16[16,896,128]{2,1,0:T(8,128)(2,1)} %param.16, s32[16]{0:T(128)S(1)} %dynamic-slice_bitcast_fusion), kind=kOutput, calls=%fused_computation.15 | convolution fusion | flops 66061056 | bytes 18350144 | tf_op jit(solution)/shard_map/sb,bvi->svi/dot_general | solution.py:37
  18.2 5.2 copy.28
  23.4 3.8 convert_element_type.42
  27.3 448.0 %while.13 = (s32[]{:T(128)}, f32[16,896,128]{2,1,0:T(8,128)}, f32[16,350]{1,0:T(8,128)S(1)}, bf16[16,128,128]{2,1,0:T(8,128)(2,1)S(1)}, f32[16,896,128]{2,1,0:T(...) while((s32[]{:T(128)}, f32[16,896,128]{2,1,0:T(8,128)}, ...), condition=%wide.region_3.0_spmd.clone, body=%wide.region_0.0_spmd.clone.sunk | while | flops 607967616 | bytes 75257976 | solution.py:60
  27.5 3.1 copy.59
  34.1 5.9 multiply_subtract_fusion.2
  40.9 27.0 %psum.25 = f32[16,350]{1,0:T(8,128)S(1)} all-reduce(f32[16,350]{1,0:T(8,128)S(1)} %fusion.51), channel_id=1, replica_groups=mesh['scen'=16,'veh'=8] {'veh'}, use_global_device_ids=true, to_apply=%region_2.0 | all-reduce | flops 5600 | bytes 44800 | tf_op jit(solution)/shard_map/while/body/eval_jaxpr/psum | solution.py:52
  67.9 3.1 copy.59
  74.5 5.9 multiply_subtract_fusion.2
  81.3 23.6 %psum.25 = f32[16,350]{1,0:T(8,128)S(1)} all-reduce(f32[16,350]{1,0:T(8,128)S(1)} %fusion.51), channel_id=1, replica_groups=mesh['scen'=16,'veh'=8] {'veh'}, use_global_device_ids=true, to_apply=%region_2.0 | all-reduce | flops 5600 | bytes 44800 | tf_op jit(solution)/shard_map/while/body/eval_jaxpr/psum | solution.py:52
  104.9 3.1 copy.59
  111.5 5.9 multiply_subtract_fusion.2
  118.3 23.6 %psum.25 = f32[16,350]{1,0:T(8,128)S(1)} all-reduce(f32[16,350]{1,0:T(8,128)S(1)} %fusion.51), channel_id=1, replica_groups=mesh['scen'=16,'veh'=8] {'veh'}, use_global_device_ids=true, to_apply=%region_2.0 | all-reduce | flops 5600 | bytes 44800 | tf_op jit(solution)/shard_map/while/body/eval_jaxpr/psum | solution.py:52
  142.0 3.1 copy.59
  148.5 5.9 multiply_subtract_fusion.2
  155.4 23.6 %psum.25 = f32[16,350]{1,0:T(8,128)S(1)} all-reduce(f32[16,350]{1,0:T(8,128)S(1)} %fusion.51), channel_id=1, replica_groups=mesh['scen'=16,'veh'=8] {'veh'}, use_global_device_ids=true, to_apply=%region_2.0 | all-reduce | flops 5600 | bytes 44800 | tf_op jit(solution)/shard_map/while/body/eval_jaxpr/psum | solution.py:52
  179.0 3.1 copy.59
  185.6 5.9 multiply_subtract_fusion.2
  192.4 23.6 %psum.25 = f32[16,350]{1,0:T(8,128)S(1)} all-reduce(f32[16,350]{1,0:T(8,128)S(1)} %fusion.51), channel_id=1, replica_groups=mesh['scen'=16,'veh'=8] {'veh'}, use_global_device_ids=true, to_apply=%region_2.0 | all-reduce | flops 5600 | bytes 44800 | tf_op jit(solution)/shard_map/while/body/eval_jaxpr/psum | solution.py:52
  216.1 3.1 copy.59
  222.6 5.9 multiply_subtract_fusion.2
  229.5 23.6 %psum.25 = f32[16,350]{1,0:T(8,128)S(1)} all-reduce(f32[16,350]{1,0:T(8,128)S(1)} %fusion.51), channel_id=1, replica_groups=mesh['scen'=16,'veh'=8] {'veh'}, use_global_device_ids=true, to_apply=%region_2.0 | all-reduce | flops 5600 | bytes 44800 | tf_op jit(solution)/shard_map/while/body/eval_jaxpr/psum | solution.py:52
  253.1 3.1 copy.59
  259.7 5.9 multiply_subtract_fusion.2
  266.5 23.6 %psum.25 = f32[16,350]{1,0:T(8,128)S(1)} all-reduce(f32[16,350]{1,0:T(8,128)S(1)} %fusion.51), channel_id=1, replica_groups=mesh['scen'=16,'veh'=8] {'veh'}, use_global_device_ids=true, to_apply=%region_2.0 | all-reduce | flops 5600 | bytes 44800 | tf_op jit(solution)/shard_map/while/body/eval_jaxpr/psum | solution.py:52
  290.1 3.1 copy.59
  296.7 5.9 multiply_subtract_fusion.2
  303.5 23.6 %psum.25 = f32[16,350]{1,0:T(8,128)S(1)} all-reduce(f32[16,350]{1,0:T(8,128)S(1)} %fusion.51), channel_id=1, replica_groups=mesh['scen'=16,'veh'=8] {'veh'}, use_global_device_ids=true, to_apply=%region_2.0 | all-reduce | flops 5600 | bytes 44800 | tf_op jit(solution)/shard_map/while/body/eval_jaxpr/psum | solution.py:52
  327.2 3.1 copy.59
  333.7 5.9 multiply_subtract_fusion.2
  340.6 23.6 %psum.25 = f32[16,350]{1,0:T(8,128)S(1)} all-reduce(f32[16,350]{1,0:T(8,128)S(1)} %fusion.51), channel_id=1, replica_groups=mesh['scen'=16,'veh'=8] {'veh'}, use_global_device_ids=true, to_apply=%region_2.0 | all-reduce | flops 5600 | bytes 44800 | tf_op jit(solution)/shard_map/while/body/eval_jaxpr/psum | solution.py:52
  364.2 3.1 copy.59
  370.8 5.9 multiply_subtract_fusion.2
  377.6 23.6 %psum.25 = f32[16,350]{1,0:T(8,128)S(1)} all-reduce(f32[16,350]{1,0:T(8,128)S(1)} %fusion.51), channel_id=1, replica_groups=mesh['scen'=16,'veh'=8] {'veh'}, use_global_device_ids=true, to_apply=%region_2.0 | all-reduce | flops 5600 | bytes 44800 | tf_op jit(solution)/shard_map/while/body/eval_jaxpr/psum | solution.py:52
  401.2 3.1 copy.59
  407.8 5.9 multiply_subtract_fusion.2
  414.6 23.6 %psum.25 = f32[16,350]{1,0:T(8,128)S(1)} all-reduce(f32[16,350]{1,0:T(8,128)S(1)} %fusion.51), channel_id=1, replica_groups=mesh['scen'=16,'veh'=8] {'veh'}, use_global_device_ids=true, to_apply=%region_2.0 | all-reduce | flops 5600 | bytes 44800 | tf_op jit(solution)/shard_map/while/body/eval_jaxpr/psum | solution.py:52
  438.3 3.1 copy.59
  444.8 5.9 multiply_subtract_fusion.2
  451.7 23.6 %psum.25 = f32[16,350]{1,0:T(8,128)S(1)} all-reduce(f32[16,350]{1,0:T(8,128)S(1)} %fusion.51), channel_id=1, replica_groups=mesh['scen'=16,'veh'=8] {'veh'}, use_global_device_ids=true, to_apply=%region_2.0 | all-reduce | flops 5600 | bytes 44800 | tf_op jit(solution)/shard_map/while/body/eval_jaxpr/psum | solution.py:52
  475.4 16.7 %fusion.14 = f32[16,896,128]{2,0,1:T(8,128)} fusion(f32[16,896,128]{2,1,0:T(8,128)} %get-tuple-element.48, f32[16]{0:T(128)S(1)} %dynamic-slice_convert_fusion.1, s32[16]{0:T(128)S(1)} %dynamic-slice_bitcast_fusion), kind=kOutput, calls=%fused_computation.18 | convolution fusion | flops 352322048 | bytes 14680192 | tf_op jit(solution)/shard_map/sb,svi->bvi/dot_general | solution.py:71
  492.2 5.6 convert_element_type.49
  499.2 123.3 %all-reduce.2.cloned.1.call-done = f32[16,896,128]{2,0,1:T(8,128)} async-done(((f32[16,896,128]{2,0,1:T(8,128)}), f32[16,896,128]{2,0,1:T(8,128)}) %all-reduce.2.cloned.1.call-update) | async-done | bytes 7340048 | tf_op jit(solution)/shard_map/psum | solution.py:72
  622.5 3.8 broadcast_divide_fusion
  626.7 24.6 %multiply_reduce_fusion.1 = (f32[16]{0:T(128)S(1)}, bf16[16,896,128]{2,0,1:T(8,128)(2,1)S(1)}) fusion(bf16[16,896,128]{2,1,0:T(8,128)(2,1)S(1)} %copy-done.2, f32[16,896,128]{2,0,1:T(8,128)S(1)} %broadcast_divide_fusion, s32[16]{0:T(128)S(1)} %dynamic-slice_bitcast_fusion, f32[16,896,128]{2,1,0:T(8,128)} %get-tuple-element.48), kind=kOutput, calls=%fused_computation.17 | convolution fusion | flops 363331840 | bytes 22020224 | tf_op jit(solution)/shard_map/sb,bvi->svi/dot_general | solution.py:75
  652.0 2.8 copy.32
  654.8 64.8 %psum.22 = f32[]{:T(128)} all-reduce(f32[]{:T(128)} %multiply_reduce_fusion.2), channel_id=1, replica_groups=mesh['scen'=16,'veh'=8] {'scen','veh'}, use_global_device_ids=true, to_apply=%region_8.0 | all-reduce | flops 1 | bytes 8 | tf_op jit(solution)/shard_map/psum | solution.py:79
  720.2 2.4 dynamic-slice_convert_fusion
  (104 shorter events, 56.5 us)
Async XLA Ops:
  7.2 615.4 %all-reduce.2.cloned.1.call-start = ((), (), s32[]{:S(2)}) async-start(), calls=%async_computation | async-start | bytes 14680064 | tf_op jit(solution)/shard_map/psum | solution.py:72
  18.2 5.2 copy-start.4
  23.4 3.8 copy-start.8
  23.4 3.8 copy-start.3
  23.4 3.9 copy-start.6
  23.4 3.9 copy-start.7
  23.4 3.9 copy-start.11
  27.3 448.0 %copy-start.9 = (s32[256]{0:T(256)S(1)}, s32[256]{0:T(256)}, u32[]{:S(2)}) copy-start(s32[256]{0:T(256)} %param.23) | copy-start | bytes 3076
  30.6 3.5 copy-start
  71.0 3.5 copy-start
  108.0 3.5 copy-start
  145.1 3.5 copy-start
  182.1 3.5 copy-start
  219.1 3.5 copy-start
  256.2 3.5 copy-start
  293.2 3.5 copy-start
  330.3 3.5 copy-start
  367.3 3.5 copy-start
  404.3 3.5 copy-start
  441.4 3.5 copy-start
  475.3 16.8 %copy-start.5 = (f32[16,350]{1,0:T(8,128)}, f32[16,350]{1,0:T(8,128)S(1)}, u32[]{:S(2)}) copy-start(f32[16,350]{1,0:T(8,128)S(1)} %get-tuple-element.93) | copy-start | bytes 67204
  492.2 6.9 copy-start.10
  622.5 4.1 copy-start.2
  626.7 24.6 %copy-start.1 = (f32[16,896,128]{2,0,1:T(8,128)}, f32[16,896,128]{2,0,1:T(8,128)S(1)}, u32[]{:S(2)}) copy-start(f32[16,896,128]{2,0,1:T(8,128)S(1)} %broadcast_divide_fusion) | copy-start | bytes 22020100
Sparse Core Ops, SparseCore 0:
  492.3 130.1 all-reduce.1
where the time goes:
time: 733 us; the launch traced here: 731 us
  blocking collectives  352 us (48%)
  matrix products  150 us (20%)
  waiting for transfers between devices  123 us (17%)
  local copies, waits for them, and re-layouts  49.3 us (7%)
  other arithmetic  39.9 us (5%)
  between operations  16.7 us (2%)
    psum x12, blocking collectives, advance(): usage = lax.psum(partial_use, 'veh')  287 us
    psum x1, waiting for transfers between devices, shards(): totals = lax.psum(partial_sums, 'scen')  123 us
    dot_general x12, matrix products, advance(): jnp.einsum('svi,sij->svj', rounded, hessian, preferred_element_type=jnp.f...  70.6 us
    psum x1, blocking collectives, shards(): spread_total = lax.psum(spread, ('scen', 'veh'))  64.8 us
    while x36, local copies, waits for them, and re-layouts  37.1 us
    reduce_sum x12, other arithmetic, advance(): consumed = jnp.sum(roster * coefficient[None], axis=2)  25.1 us
    dot_general x1, matrix products, shards(): jnp.einsum('sb,bvi->svi', selector, every_mean, precision=highest)  24.6 us
    dot_general x1, matrix products, shards(): jnp.einsum('sb,svi->bvi', weighted_pick, roster, precision=highest)  16.7 us
  transfers between devices with their start and end apart: 1, of which 1 were waited for; matrix products, arithmetic and copies ran while one was open for 1% of the time, Pallas kernels for 0%

commit v1 on v0

v1 whole, which is shorter than its diff:
```python
import functools

import jax
import jax.numpy as jnp
from jax import lax
from jax.experimental import pallas as pl
from jax.experimental.pallas import tpu as pltpu
from jax.sharding import PartitionSpec as P

ITERS = 12
penalty = 1.0
step_size = 0.02
dual_step = 0.02
keep = 1.0 - step_size * penalty
CREW_PAD = 384
LIMIT = 56 * 1024 * 1024
bf16 = jnp.bfloat16
f32 = jnp.float32

PAIR_A = {0: 1, 1: 0, 2: 3, 3: 2}
PAIR_B = {0: 3, 3: 0, 1: 2, 2: 1}


def split3(value):
    hi = value.astype(bf16)
    rest = value - hi.astype(f32)
    mid = rest.astype(bf16)
    low = (rest - mid.astype(f32)).astype(bf16)
    return jnp.concatenate([hi, mid, low], axis=0)


def exact_dot(left, right):
    rows = left.shape[0]
    out = jnp.dot(split3(left), right, preferred_element_type=f32)
    return out[:rows] + out[rows : 2 * rows] + out[2 * rows :]


def folded(value):
    return jnp.sum(value.reshape(-1, 8, value.shape[1]), axis=0)


def lane_chunks(width):
    chunks, start = [], 0
    while start < width:
        size = min(256, width - start)
        chunks.append(pl.ds(start, size))
        start += size
    return chunks


def first_kernel(
    bundles,
    start_ref,
    cost_ref,
    price_ref,
    anchor_ref,
    hess_ref,
    coef_ref,
    dual_ref,
    row_to_veh,
    veh_to_row,
    partial_ref,
    linear_ref,
    coef_t_ref,
    usage_ref,
    crew_scr,
    used_scr,
):
    s = pl.program_id(0)
    count = pl.num_programs(0)
    n = hess_ref.shape[-1]
    eye = (
        lax.broadcasted_iota(jnp.int32, (n, n), 0) == lax.broadcasted_iota(jnp.int32, (n, n), 1)
    ).astype(bf16)

    def turned(block):
        return lax.dot_general(eye, block, (((1,), (1,)), ((), ())), preferred_element_type=f32)

    @pl.when(s == 0)
    def _():
        crew_scr[:, 0, :] = step_size * exact_dot(dual_ref[...], row_to_veh[...])
        used_scr[...] = jnp.zeros_like(used_scr)
        for cols in lane_chunks(used_scr.shape[2]):
            c = turned(coef_ref[cols, :])
            coef_t_ref[:, cols] = c
            used_scr[48, :, cols] = folded(c * c)

    hess = hess_ref[0]
    for cols in lane_chunks(used_scr.shape[2]):
        c = coef_t_ref[:, cols]
        linear = step_size * (
            turned(cost_ref[0, cols, :])
            + turned(price_ref[0, cols, :])
            - penalty * turned(anchor_ref[0, cols, :])
        )
        linear_ref[0, :, cols] = linear
        x = turned(start_ref[0, cols, :])
        used_scr[s, :, cols] = folded(c * x)
        curve = jnp.dot(hess, x.astype(bf16), preferred_element_type=f32)
        x = (keep * x - linear) - step_size * curve - crew_scr[s, :, cols] * c
        used_scr[16 + s, :, cols] = folded(c * x)
        curve = jnp.dot(hess, x.astype(bf16), preferred_element_type=f32)
        x = (keep * x - linear) - step_size * curve
        used_scr[32 + s, :, cols] = folded(c * x)
        partial_ref[0, :, cols] = x

    @pl.when(s == count - 1)
    def _():
        usage_ref[...] = exact_dot(jnp.sum(used_scr[...], axis=1), veh_to_row[...])


def crew_update(usage, norms, limit, dual):
    one = jnp.maximum(dual + dual_step * (usage[0:16] - limit), 0.0)
    third = usage[32:48] - step_size * one * norms
    two = jnp.maximum(one + dual_step * (usage[16:32] - limit), 0.0)
    three = jnp.maximum(two + dual_step * (third - limit), 0.0)
    return one, two, three


def middle_kernel(
    partial_ref,
    linear_ref,
    hess_ref,
    coef_t_ref,
    use_a,
    use_b,
    norms_ref,
    limit_ref,
    dual_ref,
    row_to_veh,
    veh_to_row,
    next_ref,
    usage_ref,
    new_dual_ref,
    crew_scr,
    used_scr,
):
    s = pl.program_id(0)
    count = pl.num_programs(0)

    @pl.when(s == 0)
    def _():
        one, two, three = crew_update(
            use_a[0:48] + use_b[0:48], norms_ref[0:1], limit_ref[...], dual_ref[...]
        )
        new_dual_ref[...] = three
        crew_scr[:, 0, :] = step_size * exact_dot(
            jnp.concatenate([one, two, three], axis=0), row_to_veh[...]
        )

    hess = hess_ref[0]
    for cols in lane_chunks(used_scr.shape[2]):
        c = coef_t_ref[:, cols]
        linear = linear_ref[0, :, cols]
        x = partial_ref[0, :, cols] - crew_scr[s, :, cols] * c
        for k in (1, 2):
            curve = jnp.dot(hess, x.astype(bf16), preferred_element_type=f32)
            x = (keep * x - linear) - step_size * curve - crew_scr[16 * k + s, :, cols] * c
            used_scr[16 * (k - 1) + s, :, cols] = folded(c * x)
        curve = jnp.dot(hess, x.astype(bf16), preferred_element_type=f32)
        x = (keep * x - linear) - step_size * curve
        used_scr[32 + s, :, cols] = folded(c * x)
        next_ref[0, :, cols] = x

    @pl.when(s == count - 1)
    def _():
        usage_ref[...] = exact_dot(jnp.sum(used_scr[...], axis=1), veh_to_row[...])


def last_kernel(
    slots,
    factors,
    partial_ref,
    linear_ref,
    hess_ref,
    coef_t_ref,
    use_a,
    use_b,
    norms_ref,
    limit_ref,
    dual_ref,
    row_to_veh,
    plan_ref,
    roster_ref,
    sum_a,
    sum_b,
    spread_ref,
    new_dual_ref,
    crew_scr,
):
    s = pl.program_id(0)
    rows = sum_a.shape[1]

    @pl.when(s == 0)
    def _():
        one, two, three = crew_update(
            use_a[0:48] + use_b[0:48], norms_ref[0:1], limit_ref[...], dual_ref[...]
        )
        new_dual_ref[...] = three
        crew_scr[:, 0, :] = step_size * exact_dot(
            jnp.concatenate([one, two], axis=0), row_to_veh[...]
        )
        sum_a[...] = jnp.zeros_like(sum_a)
        sum_b[...] = jnp.zeros_like(sum_b)
        spread_ref[...] = jnp.zeros_like(spread_ref)

    hess = hess_ref[0]
    for cols in lane_chunks(crew_scr.shape[2]):
        c = coef_t_ref[:, cols]
        x = partial_ref[0, :, cols] - crew_scr[s, :, cols] * c
        curve = jnp.dot(hess, x.astype(bf16), preferred_element_type=f32)
        x = (
            (keep * x - linear_ref[0, :, cols])
            - step_size * curve
            - crew_scr[16 + s, :, cols] * c
        )
        turned = x.T
        roster_ref[0, cols, :] = turned
        plan_ref[0, cols, :] = turned.astype(bf16)

    weight, merge, inverse = factors[0, s], factors[1, s], factors[2, s]
    for side, sums in enumerate((sum_a, sum_b)):
        slot = slots[side, s]
        part = 112
        for start in range(0, rows, part):
            x = roster_ref[0, side * rows + start : side * rows + start + part, :]
            held = sums[slot, start : start + part, :]
            gap = held * inverse - x
            squares = gap * gap * merge
            spread_ref[...] += jnp.sum(squares.reshape(part // 8, 8, 128), axis=0)
            sums[slot, start : start + part, :] = held + weight * x


def price_kernel(slots, roster_ref, price_ref, mean_a, mean_b, out_ref):
    s = pl.program_id(0)
    rows = mean_a.shape[1]
    for side, means in enumerate((mean_a, mean_b)):
        slot = slots[side, s]
        part = 112
        for start in range(0, rows, part):
            here = slice(side * rows + start, side * rows + start + part)
            deviation = roster_ref[0, here, :] - means[slot, start : start + part, :]
            out_ref[0, here, :] = (
                price_ref[0, here, :].astype(f32) + penalty * deviation
            ).astype(bf16)


def veh_pairs(kind):
    if kind == "core":
        return [(i, i ^ 1) for i in range(8)]
    return [(z * 2 + c, kind[z] * 2 + c) for z in range(4) for c in range(2)]


def scen_pairs(pair, axis):
    out = []
    for y in range(4):
        for x in range(4):
            to = (y * 4 + pair[x]) if axis == "x" else (pair[y] * 4 + x)
            out.append((y * 4 + x, to))
    return out


def usage_exchange(value):
    value = value + lax.ppermute(value, "veh", veh_pairs("core"))
    value = value + lax.ppermute(value, "veh", veh_pairs(PAIR_A))
    return value, lax.ppermute(value, "veh", veh_pairs(PAIR_B))


def sum_everywhere(value):
    a, b = usage_exchange(value)
    value = a + b
    for axis in ("x", "y"):
        for pair in (PAIR_A, PAIR_B):
            value = value + lax.ppermute(value, "scen", scen_pairs(pair, axis))
    return value


def shift(value, axis, by):
    pairs = []
    for y in range(4):
        for x in range(4):
            to = (y * 4 + (x + by) % 4) if axis == "x" else (((y + by) % 4) * 4 + x)
            pairs.append((y * 4 + x, to))
    return lax.ppermute(value, "scen", pairs)


def merged(parts):
    total, weight = parts[0]
    spread = jnp.zeros((8, 128), f32)
    for other, other_weight in parts[1:]:
        both = weight + other_weight
        factor = jnp.where(both > 0, weight * other_weight / jnp.maximum(both, 1.0), 0.0)
        gap = total / jnp.maximum(weight, 1.0) - other / jnp.maximum(other_weight, 1.0)
        spread = spread + jnp.sum((gap * gap * factor).reshape(-1, 8, 128), axis=0)
        total, weight = total + other, both
    return total, weight, spread


def reduce_half(sums, weight, first, second):
    def w(ef, df):
        return weight(ef, 0)[df][:, None, None]

    up = shift(sums[2][:, 0], first, 1)
    down = shift(sums[2][:, 1], first, -1)
    up, _, s1 = merged([(sums[1][:, 0], w(0, 1)), (up, w(3, 1))])
    down, _, s2 = merged([(sums[3][:, 1], w(0, 3)), (down, w(1, 3))])
    up = shift(jnp.stack([up, sums[1][:, 1]], axis=1), first, 1)
    down = shift(jnp.stack([sums[3][:, 0], down], axis=1), first, -1)
    w0, w1, w2, w3 = (w(e, 0) for e in range(4))
    mine, mine_w, s3 = merged(
        [
            (sums[0], w0[:, None]),
            (up, jnp.stack([w3 + w2, w3], axis=1)),
            (down, jnp.stack([w1, w1 + w2], axis=1)),
        ]
    )
    arrived = [(mine[0], mine_w[0])]
    for by in (1, 3, 2):
        from_row = sum(weight(e, (4 - by) % 4)[0, 0] for e in range(4))
        arrived.append((shift(mine[by], second, by), from_row))
    own, _, s4 = merged(arrived)
    return own, s1 + s2 + s3 + s4


def gather_half(own, first, second):
    row = {0: own}
    for by in (1, 3, 2):
        row[by] = shift(own, second, -by)
    row = jnp.stack([row[k] for k in range(4)], axis=1)
    third = shift(row, first, 1)
    one = shift(row, first, -1)
    two_a = shift(third[0], first, 1)
    two_b = shift(one[1], first, -1)
    two = jnp.stack([two_a, two_b], axis=0)
    return jnp.stack([row, one, two, third], axis=0).transpose(0, 2, 1, 3, 4)


def shards(
    start_plan,
    linear_cost,
    price,
    anchor,
    hessian,
    usage_coef,
    crew_limit,
    crew_dual,
    crew_row,
    bundle_of,
    scen_weight,
):
    count, vehicles, n = start_plan.shape
    crews = crew_limit.shape[1]
    bundle_count = anchor.shape[0]
    me = lax.axis_index("scen")
    my_y, my_x = me // 4, me % 4
    all_bundles = bundle_of[:, 0]
    my_bundles = lax.dynamic_slice_in_dim(all_bundles, me * count, count)
    all_weights = scen_weight.astype(f32)
    my_weights = lax.dynamic_slice_in_dim(all_weights, me * count, count)

    pad = ((0, 0), (0, CREW_PAD - crews))
    limit = jnp.pad(crew_limit, pad)
    dual = jnp.pad(crew_dual, pad)
    crew_ids = jnp.arange(CREW_PAD, dtype=jnp.int32)
    row_to_veh = (crew_ids[:, None] == crew_row[None, :]).astype(bf16)
    veh_to_row = (crew_row[:, None] == crew_ids[None, :]).astype(bf16)

    def per_scen(*shape):
        return pl.BlockSpec((1, *shape), lambda s, *_: (s, 0, 0))

    def whole(*shape):
        return pl.BlockSpec(shape, lambda s, *_: (0,) * len(shape))

    params = pltpu.CompilerParams(
        dimension_semantics=("arbitrary",), vmem_limit_bytes=LIMIT
    )
    tall = jax.ShapeDtypeStruct((count, n, vehicles), f32)
    flat_block = per_scen(vehicles, n)
    tall_block = per_scen(n, vehicles)

    partial, linear, coef_t, usage = pl.pallas_call(
        first_kernel,
        grid_spec=pltpu.PrefetchScalarGridSpec(
            num_scalar_prefetch=1,
            grid=(count,),
            in_specs=[
                flat_block,
                flat_block,
                flat_block,
                pl.BlockSpec((1, vehicles, n), lambda s, b: (b[s], 0, 0)),
                per_scen(n, n),
                whole(vehicles, n),
                whole(count, CREW_PAD),
                whole(CREW_PAD, vehicles),
                whole(vehicles, CREW_PAD),
            ],
            out_specs=[tall_block, tall_block, whole(n, vehicles), whole(56, CREW_PAD)],
            scratch_shapes=[pltpu.VMEM((16, 1, vehicles), f32), pltpu.VMEM((56, 8, vehicles), f32)],
        ),
        out_shape=[
            tall,
            tall,
            jax.ShapeDtypeStruct((n, vehicles), f32),
            jax.ShapeDtypeStruct((56, CREW_PAD), f32),
        ],
        compiler_params=params,
        name="first_steps",
    )(
        my_bundles,
        start_plan,
        linear_cost,
        price,
        anchor,
        hessian,
        usage_coef,
        dual,
        row_to_veh,
        veh_to_row,
    )

    use_a, use_b = usage_exchange(usage)
    norms = use_a[48:56] + use_b[48:56]
    crew_specs = [whole(8, CREW_PAD), whole(count, CREW_PAD), whole(count, CREW_PAD)]
    for _ in range(3):
        partial, usage, dual = pl.pallas_call(
            middle_kernel,
            grid=(count,),
            in_specs=[
                tall_block,
                tall_block,
                per_scen(n, n),
                whole(n, vehicles),
                whole(*use_a.shape),
                whole(*use_a.shape),
                *crew_specs,
                whole(CREW_PAD, vehicles),
                whole(vehicles, CREW_PAD),
            ],
            out_specs=[tall_block, whole(48, CREW_PAD), whole(count, CREW_PAD)],
            out_shape=[
                tall,
                jax.ShapeDtypeStruct((48, CREW_PAD), f32),
                jax.ShapeDtypeStruct((count, CREW_PAD), f32),
            ],
            scratch_shapes=[pltpu.VMEM((48, 1, vehicles), f32), pltpu.VMEM((48, 8, vehicles), f32)],
            compiler_params=params,
            name="three_steps",
        )(partial, linear, hessian, coef_t, use_a, use_b, norms, limit, dual, row_to_veh, veh_to_row)
        use_a, use_b = usage_exchange(usage)

    rel_y = (my_bundles // 4 - my_y + 4) % 4
    rel_x = (my_bundles % 4 - my_x + 4) % 4
    slots = jnp.stack([rel_x * 4 + rel_y, rel_y * 4 + rel_x])
    same = my_bundles[:, None] == my_bundles[None, :]
    before = jnp.arange(count)[None, :] < jnp.arange(count)[:, None]
    held = jnp.sum(jnp.where(same & before, my_weights[None, :], 0.0), axis=1)
    factors = jnp.stack(
        [
            my_weights,
            held * my_weights / (held + my_weights),
            1.0 / jnp.maximum(held, 1.0),
        ]
    )
    half = vehicles // 2
    bundle_sums = jax.ShapeDtypeStruct((bundle_count, half, n), f32)
    plan, roster, sum_a, sum_b, spread, dual = pl.pallas_call(
        last_kernel,
        grid_spec=pltpu.PrefetchScalarGridSpec(
            num_scalar_prefetch=2,
            grid=(count,),
            in_specs=[
                tall_block,
                tall_block,
                per_scen(n, n),
                whole(n, vehicles),
                whole(*use_a.shape),
                whole(*use_a.shape),
                *crew_specs,
                whole(CREW_PAD, vehicles),
            ],
            out_specs=[
                flat_block,
                flat_block,
                whole(bundle_count, half, n),
                whole(bundle_count, half, n),
                whole(8, n),
                whole(count, CREW_PAD),
            ],
            scratch_shapes=[pltpu.VMEM((32, 1, vehicles), f32)],
        ),
        out_shape=[
            jax.ShapeDtypeStruct((count, vehicles, n), bf16),
            jax.ShapeDtypeStruct((count, vehicles, n), f32),
            bundle_sums,
            bundle_sums,
            jax.ShapeDtypeStruct((8, n), f32),
            jax.ShapeDtypeStruct((count, CREW_PAD), f32),
        ],
        compiler_params=params,
        name="last_step",
    )(slots, factors, partial, linear, hessian, coef_t, use_a, use_b, norms, limit, dual, row_to_veh)

    places = jnp.arange(16, dtype=jnp.int32)
    absolute = ((my_y + places // 4) % 4) * 4 + (my_x + places % 4) % 4
    owners = jnp.arange(all_bundles.shape[0], dtype=jnp.int32) // count
    rel_weights = jnp.sum(
        jnp.where(
            (owners[None, None, :] == absolute[:, None, None])
            & (all_bundles[None, None, :] == absolute[None, :, None]),
            all_weights[None, None, :],
            0.0,
        ),
        axis=2,
    ).reshape(4, 4, 4, 4)
    own_weight = jnp.sum(rel_weights[:, :, 0, 0])

    shape5 = (4, 4, 2, half // 2, n)
    own_a, spread_a = reduce_half(
        sum_a.reshape(shape5), lambda ex, ey: rel_weights[ey, ex].T, "x", "y"
    )
    own_b, spread_b = reduce_half(
        sum_b.reshape(shape5), lambda ey, ex: rel_weights[ey, ex], "y", "x"
    )
    own_a, own_b = own_a / own_weight, own_b / own_weight
    mean_a = gather_half(own_a, "x", "y").reshape(bundle_count, half, n)
    mean_b = gather_half(own_b, "y", "x").reshape(bundle_count, half, n)
    spread_total = jnp.sum(sum_everywhere(spread + spread_a + spread_b))
    entries = vehicles * lax.axis_size("veh") * n
    gap = jnp.sqrt(spread_total / (jnp.sum(all_weights) * entries))

    new_price = pl.pallas_call(
        price_kernel,
        grid_spec=pltpu.PrefetchScalarGridSpec(
            num_scalar_prefetch=1,
            grid=(count,),
            in_specs=[
                flat_block,
                flat_block,
                whole(bundle_count, half, n),
                whole(bundle_count, half, n),
            ],
            out_specs=[flat_block],
        ),
        out_shape=[jax.ShapeDtypeStruct((count, vehicles, n), bf16)],
        compiler_params=params,
        name="new_price",
    )(slots, roster, price, mean_a, mean_b)[0]

    own_mean = jnp.concatenate([own_a.reshape(half, n), own_b.reshape(half, n)], axis=0)
    return (plan, new_price, own_mean.astype(bf16)[None], dual[:, :crews], gap)


def solution(mesh):
    return jax.shard_map(
        shards,
        mesh=mesh,
        in_specs=(
            P("scen", "veh", None),
            P("scen", "veh", None),
            P("scen", "veh", None),
            P(None, "veh", None),
            P("scen", None, None),
            P("veh", None),
            P("scen", None),
            P("scen", None),
            P("veh"),
            P(),
            P(),
        ),
        out_specs=(
            P("scen", "veh", None),
            P("scen", "veh", None),
            P("scen", "veh", None),
            P("scen", None),
            P(),
        ),
        check_vma=False,
    )
```

time: 733 us -> 402 us (0.55)
  blocking collectives: 352 us -> 0 us
  matrix products: 150 us -> 0 us
  Pallas kernels: 0 us -> 137 us
  starting transfers between devices: 0.04 us -> 60.8 us
  waiting for transfers between devices: 123 us -> 84.4 us
  other arithmetic: 39.9 us -> 62.4 us
  local copies, waits for them, and re-layouts: 49.3 us -> 35.1 us
    psum x13 -> x0, blocking collectives: 352 us -> none  [the longest x12 287 us: advance(): usage = lax.psum(partial_use, 'veh')]
    dot_general x39 -> x0, matrix products: 150 us -> none  [the longest x12 70.6 us: advance(): jnp.einsum('svi,sij->svj', rounded, hessian, preferred_element_type=jnp.f...]
    pallas_call x0 -> x6, Pallas kernels: none -> 137 us  [the longest x3 68.9 us: shards(): pl.pallas_call(middle_kernel, grid=(count,), in_specs=[tall_block, tall_b...]
    psum x1 -> x0, waiting for transfers between devices: 123 us -> none  [shards(): totals = lax.psum(partial_sums, 'scen')]
    ppermute x0 -> x47, waiting for transfers between devices: none -> 84.4 us  [the longest x28 44.1 us: shift(): return lax.ppermute(value, 'scen', pairs)]
    ppermute x0 -> x47, starting transfers between devices: none -> 60.8 us  [the longest x28 41.1 us: shift(): return lax.ppermute(value, 'scen', pairs)]
    while x36 -> x0, local copies, waits for them, and re-layouts: 37.1 us -> none
    another operation x0 -> x15, other arithmetic: none -> 18.7 us  [the longest x6 9.94 us: gather_half(): return jnp.stack([row, one, two, third], axis=0).transpose(0, 2, 1, 3, 4)]
  transfers between devices with their start and end apart: 1 -> 47, of which waited for: 1 -> 28; matrix products, arithmetic and copies ran while one was open for 1% -> 17% of each run, Pallas kernels for 0% -> 0%
where the time goes in v1:
time: 402 us; the launch traced here: 398 us
  Pallas kernels  137 us (34%)
  waiting for transfers between devices  84.4 us (21%)
  other arithmetic  62.4 us (16%)
  starting transfers between devices  60.8 us (15%)
  local copies, waits for them, and re-layouts  35.1 us (9%)
  between operations  18.7 us (5%)
    pallas_call x3, Pallas kernels, shards(): pl.pallas_call(middle_kernel, grid=(count,), in_specs=[tall_block, tall_b...  68.9 us
    ppermute x28, waiting for transfers between devices, shift(): return lax.ppermute(value, 'scen', pairs)  44.1 us
    ppermute x28, starting transfers between devices, shift(): return lax.ppermute(value, 'scen', pairs)  41.1 us
    pallas_call x1, Pallas kernels, shards(): pl.pallas_call(first_kernel, grid_spec=pltpu.PrefetchScalarGridSpec(num_s...  32.5 us
    pallas_call x1, Pallas kernels, shards(): pl.pallas_call(last_kernel, grid_spec=pltpu.PrefetchScalarGridSpec(num_sc...  21.1 us
    reduce_sum x14, other arithmetic, merged(): spread = spread + jnp.sum((gap * gap * factor).reshape(-1, 8, 128), axis=0)  17.8 us
    ppermute x5, waiting for transfers between devices, usage_exchange(): value = value + lax.ppermute(value, 'veh', veh_pairs(PAIR_A))  16.8 us
    pallas_call x1, Pallas kernels, shards(): pl.pallas_call(price_kernel, grid_spec=pltpu.PrefetchScalarGridSpec(num_s...  14.5 us
  transfers between devices with their start and end apart: 47, of which 28 were waited for; matrix products, arithmetic and copies ran while one was open for 17% of the time, Pallas kernels for 0%

profile of v1, /device:TPU:0, one launch (start us, length us, event | category | flops | bytes accessed | tf_op | source)
XLA Modules:
  0.0 398.4 jit_solution(5638903928255741238)
XLA Ops:
  6.7 32.5 %first_steps.1 = (f32[16,128,896]{2,1,0:T(8,128)}, f32[16,128,896]{2,1,0:T(8,128)}, f32[128,896]{1,0:T(8,128)}, f32[56,384]{1,0:T(8,128)}) custom-call(s32[16]{0:T(128)} %fusion.26.bundles, bf16[16,896,128]{2,1,0:T(8,128)(2,1)} %start_ref.1, bf16[16,896,128]{2,1,0:T(8,128)(2,1)} %cost_ref.1, bf16[16,896,128]{2,1,0:T(8,128)(2,1)} %price_ref.3, ...), custom_call_target="tpu_custom_call" | custom-call | tf_op jit(solution)/shard_map/first_steps/pallas_call | solution.py:381
  56.7 2.1 collective-permute-start.1
  59.3 2.5 collective-permute-done.1
  61.9 4.0 collective-permute-start.2
  76.1 23.0 %three_steps.3 = (f32[16,128,896]{2,1,0:T(8,128)}, f32[48,384]{1,0:T(8,128)}, f32[16,384]{1,0:T(8,128)}) custom-call(f32[16,128,896]{2,1,0:T(8,128)} %get-tuple-element.24.partial_ref, f32[16,128,896]{2,1,0:T(8,128)} %get-tuple-element.25.linear_ref, bf16[16,128,128]{2,1,0:T(8,128)(2,1)} %hess_ref.9, f32[128,896]{1,0:T(8,128)} %get-tuple-element.26.coef_t_ref, ...), custom_call_target="tpu_custom_call" | custom-call | tf_op jit(solution)/shard_map/three_steps/pallas_call | solution.py:425
  102.4 3.6 collective-permute-done.4
  106.3 5.3 %collective-permute-done.5.use_b = f32[48,384]{1,0:T(8,128)S(1)} collective-permute-done((f32[48,384]{1,0:T(8,128)S(1)}, f32[48,384]{1,0:T(8,128)S(1)}, u32[]{:S(2)}, u32[]{:S(2)}) %collective-permute-start.5) | collective-permute-done | bytes 73760 | tf_op jit(solution)/shard_map/ppermute | solution.py:266
  112.2 23.0 %three_steps.4 = (f32[16,128,896]{2,1,0:T(8,128)}, f32[48,384]{1,0:T(8,128)}, f32[16,384]{1,0:T(8,128)}) custom-call(f32[16,128,896]{2,1,0:T(8,128)} %get-tuple-element.28.partial_ref, f32[16,128,896]{2,1,0:T(8,128)} %get-tuple-element.25.linear_ref, bf16[16,128,128]{2,1,0:T(8,128)(2,1)} %hess_ref.9, f32[128,896]{1,0:T(8,128)} %get-tuple-element.26.coef_t_ref, ...), custom_call_target="tpu_custom_call" | custom-call | tf_op jit(solution)/shard_map/three_steps/pallas_call | solution.py:425
  137.9 4.2 %collective-permute-done.7 = f32[48,384]{1,0:T(8,128)S(1)} collective-permute-done((f32[48,384]{1,0:T(8,128)S(1)}, f32[48,384]{1,0:T(8,128)S(1)}, u32[]{:S(2)}, u32[]{:S(2)}) %collective-permute-start.7) | collective-permute-done | bytes 73760 | tf_op jit(solution)/shard_map/ppermute | solution.py:265
  148.6 23.0 %three_steps.5 = (f32[16,128,896]{2,1,0:T(8,128)}, f32[48,384]{1,0:T(8,128)}, f32[16,384]{1,0:T(8,128)}) custom-call(f32[16,128,896]{2,1,0:T(8,128)} %get-tuple-element.31.partial_ref, f32[16,128,896]{2,1,0:T(8,128)} %get-tuple-element.25.linear_ref, bf16[16,128,128]{2,1,0:T(8,128)(2,1)} %hess_ref.9, f32[128,896]{1,0:T(8,128)} %get-tuple-element.26.coef_t_ref, ...), custom_call_target="tpu_custom_call" | custom-call | tf_op jit(solution)/shard_map/three_steps/pallas_call | solution.py:425
  174.7 3.8 collective-permute-done.10
  178.5 2.4 collective-permute-start.11
  181.4 2.7 collective-permute-done.11.use_b
  184.7 21.1 %last_step.1 = (bf16[16,896,128]{2,1,0:T(8,128)(2,1)}, f32[16,896,128]{2,1,0:T(8,128)}, f32[16,448,128]{2,1,0:T(8,128)}, f32[16,448,128]{2,1,0:T(8,128)}, f32[8,128]{1,0:T(8,128)}, /*index=5*/f32[16,384]{1,0:T(8,128)}) custom-call(s32[2,16]{1,0:T(2,128)} %pad_add_fusion.slots, f32[3,16]{1,0:T(4,128)} %pad_maximum_fusion.9.factors, ...), custom_call_target="tpu_custom_call" | custom-call | tf_op jit(solution)/shard_map/last_step/pallas_call | solution.py:466
  205.8 3.8 fusion.33
  216.6 4.7 %collective-permute-done.26 = f32[4,224,128]{2,1,0:T(8,128)S(1)} collective-permute-done((f32[4,224,128]{2,1,0:T(8,128)S(1)}, f32[4,224,128]{2,1,0:T(8,128)S(1)}, u32[]{:S(2)}, u32[]{:S(2)}) %collective-permute-start.26) | collective-permute-done | bytes 458784 | tf_op jit(solution)/shard_map/ppermute | solution.py:284
  223.9 2.9 collective-permute-start.29
  236.2 6.0 %collective-permute-done.27 = f32[4,2,224,128]{3,2,1,0:T(8,128)} collective-permute-done((f32[4,2,224,128]{3,2,1,0:T(8,128)S(1)}, f32[4,2,224,128]{3,2,1,0:T(8,128)}, u32[]{:S(2)}, u32[]{:S(2)}) %collective-permute-start.27) | collective-permute-done | bytes 917536 | tf_op jit(solution)/shard_map/ppermute | solution.py:284
  243.6 3.2 multiply_multiply_fusion
  250.2 1.8 collective-permute-start.32
  252.1 3.1 collective-permute-done.15
  255.1 3.2 multiply_multiply_fusion.2
  261.3 4.0 %collective-permute-start.33 = (f32[2,224,128]{2,1,0:T(8,128)S(1)}, f32[2,224,128]{2,1,0:T(8,128)S(1)}, u32[]{:S(2)}, u32[]{:S(2)}) collective-permute-start(f32[2,224,128]{2,1,0:T(8,128)S(1)} %get-tuple-element.75), channel_id=1, source_target_pairs={{0,24},{8,0},{16,8},{24,16},{32,56},{40,32},{48,40},{56,48},{64,88... | collective-permute-start | bytes 688136 | tf_op jit(solution)/shard_map/ppermute | solution.py:284
  267.5 3.2 collective-permute-start.17
  273.1 2.2 collective-permute-done.35
  278.5 3.1 collective-permute-done.18
  281.6 2.8 fusion.31
  287.0 2.2 collective-permute-start.36
  289.2 3.8 collective-permute-done.19
  293.0 12.2 %collective-permute-done.20 = f32[2,224,128]{2,1,0:T(8,128)S(1)} collective-permute-done((f32[2,224,128]{2,1,0:T(8,128)S(1)}, f32[2,224,128]{2,1,0:T(8,128)S(1)}, u32[]{:S(2)}, u32[]{:S(2)}) %collective-permute-start.20) | collective-permute-done | bytes 229408 | tf_op jit(solution)/shard_map/ppermute | solution.py:284
  305.3 3.1 collective-permute-done.21
  310.6 2.5 collective-permute-start.22
  319.0 2.0 reduce_sum.183
  321.0 2.0 reduce_sum.184
  323.0 2.0 reduce_sum.176
  325.0 2.0 reduce_sum.177
  333.8 2.7 collective-permute-done.41
  336.5 2.4 collective-permute-start.42
  338.9 2.5 collective-permute-done.42
  341.7 3.3 collective-permute-done.43
  344.9 3.2 collective-permute-start.44
  355.4 3.0 collective-permute-start.39
  360.2 2.6 collective-permute-start.25
  368.1 2.6 collective-permute-done.46
  372.1 2.4 collective-permute-done.24
  375.6 3.8 pad_maximum_fusion.1
  379.4 3.4 pad_maximum_fusion
  382.8 14.5 %new_price.1 = bf16[16,896,128]{2,1,0:T(8,128)(2,1)} custom-call(s32[2,16]{1,0:T(2,128)} %pad_add_fusion.slots, f32[16,896,128]{2,1,0:T(8,128)} %get-tuple-element.38.roster_ref, bf16[16,896,128]{2,1,0:T(8,128)(2,1)} %price_ref.3, f32[16,448,128]{2,1,0:T(8,128)} %bitcast.331, f32[16,448,128]{2,1,0:T(8,128)} %bitcast.330), custom_call_target="tpu_custom_call" | custom-call | tf_op jit(solution)/shard_map/new_price/pallas_call | solution.py:531
  (269 shorter events, 104.4 us)
Async XLA Ops:
  6.7 59.1 %copy-start.18 = (f32[16,350]{1,0:T(8,128)S(1)}, f32[16,350]{1,0:T(8,128)}, u32[]{:S(2)}) copy-start(f32[16,350]{1,0:T(8,128)} %param.17) | copy-start | bytes 67204
  39.2 16.6 %collective-permute-start = (f32[56,384]{1,0:T(8,128)}, f32[56,384]{1,0:T(8,128)S(1)}, u32[]{:S(2)}, u32[]{:S(2)}) collective-permute-start(f32[56,384]{1,0:T(8,128)} %get-tuple-element.27), channel_id=1, source_target_pairs={{0,1},{1,0},{2,3},{3,2},{4,5},{5,4},{6,7},{7,6},{8,9},{9,8},{10,11... | collective-permute-start | bytes 258056 | tf_op jit(solution)/shard_map/ppermute | solution.py:264
  56.7 5.2 %collective-permute-start.1 = (f32[56,384]{1,0:T(8,128)S(1)}, f32[56,384]{1,0:T(8,128)S(1)}, u32[]{:S(2)}, u32[]{:S(2)}) collective-permute-start(f32[56,384]{1,0:T(8,128)S(1)} %add.760), channel_id=1, source_target_pairs={{0,2},{1,3},{2,0},{3,1},{4,6},{5,7},{6,4},{7,5},{8,10},{9,11},{10,... | collective-permute-start | bytes 258056 | tf_op jit(solution)/shard_map/ppermute | solution.py:265
  61.9 13.5 %collective-permute-start.2 = (f32[56,384]{1,0:T(8,128)S(1)}, f32[56,384]{1,0:T(8,128)S(1)}, u32[]{:S(2)}, u32[]{:S(2)}) collective-permute-start(f32[56,384]{1,0:T(8,128)S(1)} %add.761.use_a), channel_id=1, source_target_pairs={{0,6},{1,7},{2,4},{3,5},{4,2},{5,3},{6,0},{7,1},{8,14},{9,15},{10,... | collective-permute-start | bytes 258056 | tf_op jit(solution)/shard_map/ppermute | solution.py:266
  99.1 1.6 collective-permute-start.3
  101.5 4.4 %collective-permute-start.4 = (f32[48,384]{1,0:T(8,128)S(1)}, f32[48,384]{1,0:T(8,128)S(1)}, u32[]{:S(2)}, u32[]{:S(2)}) collective-permute-start(f32[48,384]{1,0:T(8,128)S(1)} %add.763), channel_id=1, source_target_pairs={{0,2},{1,3},{2,0},{3,1},{4,6},{5,7},{6,4},{7,5},{8,10},{9,11},{10,... | collective-permute-start | bytes 221192 | tf_op jit(solution)/shard_map/ppermute | solution.py:265
  106.0 5.6 %collective-permute-start.5 = (f32[48,384]{1,0:T(8,128)S(1)}, f32[48,384]{1,0:T(8,128)S(1)}, u32[]{:S(2)}, u32[]{:S(2)}) collective-permute-start(f32[48,384]{1,0:T(8,128)S(1)} %add.764.use_a), channel_id=1, source_target_pairs={{0,6},{1,7},{2,4},{3,5},{4,2},{5,3},{6,0},{7,1},{8,14},{9,15},{10,... | collective-permute-start | bytes 221192 | tf_op jit(solution)/shard_map/ppermute | solution.py:266
  135.2 1.6 collective-permute-start.6
  137.7 4.4 %collective-permute-start.7 = (f32[48,384]{1,0:T(8,128)S(1)}, f32[48,384]{1,0:T(8,128)S(1)}, u32[]{:S(2)}, u32[]{:S(2)}) collective-permute-start(f32[48,384]{1,0:T(8,128)S(1)} %add.765), channel_id=1, source_target_pairs={{0,2},{1,3},{2,0},{3,1},{4,6},{5,7},{6,4},{7,5},{8,10},{9,11},{10,... | collective-permute-start | bytes 221192 | tf_op jit(solution)/shard_map/ppermute | solution.py:265
  142.1 5.8 %collective-permute-start.8 = (f32[48,384]{1,0:T(8,128)S(1)}, f32[48,384]{1,0:T(8,128)S(1)}, u32[]{:S(2)}, u32[]{:S(2)}) collective-permute-start(f32[48,384]{1,0:T(8,128)S(1)} %add.766.use_a), channel_id=1, source_target_pairs={{0,6},{1,7},{2,4},{3,5},{4,2},{5,3},{6,0},{7,1},{8,14},{9,15},{10,... | collective-permute-start | bytes 221192 | tf_op jit(solution)/shard_map/ppermute | solution.py:266
  171.6 1.6 collective-permute-start.9
  174.0 4.4 %collective-permute-start.10 = (f32[48,384]{1,0:T(8,128)S(1)}, f32[48,384]{1,0:T(8,128)S(1)}, u32[]{:S(2)}, u32[]{:S(2)}) collective-permute-start(f32[48,384]{1,0:T(8,128)S(1)} %add.767), channel_id=1, source_target_pairs={{0,2},{1,3},{2,0},{3,1},{4,6},{5,7},{6,4},{7,5},{8,10},{9,11},{10,... | collective-permute-start | bytes 221192 | tf_op jit(solution)/shard_map/ppermute | solution.py:265
  178.5 5.6 %collective-permute-start.11 = (f32[48,384]{1,0:T(8,128)S(1)}, f32[48,384]{1,0:T(8,128)S(1)}, u32[]{:S(2)}, u32[]{:S(2)}) collective-permute-start(f32[48,384]{1,0:T(8,128)S(1)} %add.768.use_a), channel_id=1, source_target_pairs={{0,6},{1,7},{2,4},{3,5},{4,2},{5,3},{6,0},{7,1},{8,14},{9,15},{10,... | collective-permute-start | bytes 221192 | tf_op jit(solution)/shard_map/ppermute | solution.py:266
  209.7 11.6 %collective-permute-start.26 = (f32[4,224,128]{2,1,0:T(8,128)S(1)}, f32[4,224,128]{2,1,0:T(8,128)S(1)}, u32[]{:S(2)}, u32[]{:S(2)}) collective-permute-start(f32[4,224,128]{2,1,0:T(8,128)S(1)} %get-tuple-element.112), channel_id=1, source_target_pairs={{0,32},{8,40},{16,48},{24,56},{32,64},{40,72},{48,80},{56,88},{64,... | collective-permute-start | bytes 1376264 | tf_op jit(solution)/shard_map/ppermute | solution.py:284
  211.4 10.6 %collective-permute-start.28 = (f32[4,224,128]{2,1,0:T(8,128)S(1)}, f32[4,224,128]{2,1,0:T(8,128)S(1)}, u32[]{:S(2)}, u32[]{:S(2)}) collective-permute-start(f32[4,224,128]{2,1,0:T(8,128)S(1)} %get-tuple-element.113), channel_id=1, source_target_pairs={{0,96},{8,104},{16,112},{24,120},{32,0},{40,8},{48,16},{56,24},{64... | collective-permute-start | bytes 1376264 | tf_op jit(solution)/shard_map/ppermute | solution.py:284
  213.2 13.6 %collective-permute-start.12 = (f32[4,224,128]{2,1,0:T(8,128)S(1)}, f32[4,224,128]{2,1,0:T(8,128)S(1)}, u32[]{:S(2)}, u32[]{:S(2)}) collective-permute-start(f32[4,224,128]{2,1,0:T(8,128)S(1)} %get-tuple-element.119), channel_id=1, source_target_pairs={{0,8},{8,16},{16,24},{24,0},{32,40},{40,48},{48,56},{56,32},{64,72... | collective-permute-start | bytes 1376264 | tf_op jit(solution)/shard_map/ppermute | solution.py:284
  214.8 15.5 %collective-permute-start.14 = (f32[4,224,128]{2,1,0:T(8,128)S(1)}, f32[4,224,128]{2,1,0:T(8,128)S(1)}, u32[]{:S(2)}, u32[]{:S(2)}) collective-permute-start(f32[4,224,128]{2,1,0:T(8,128)S(1)} %get-tuple-element.120), channel_id=1, source_target_pairs={{0,24},{8,0},{16,8},{24,16},{32,56},{40,32},{48,40},{56,48},{64,88... | collective-permute-start | bytes 1376264 | tf_op jit(solution)/shard_map/ppermute | solution.py:284
  221.6 20.6 %collective-permute-start.27 = (f32[4,2,224,128]{3,2,1,0:T(8,128)S(1)}, f32[4,2,224,128]{3,2,1,0:T(8,128)}, u32[]{:S(2)}, u32[]{:S(2)}) collective-permute-start(f32[4,2,224,128]{3,2,1,0:T(8,128)S(1)} %pad_maximum_fusion.5), channel_id=1, source_target_pairs={{0,32},{8,40},{16,48},{24,56},{32,64},{40,72},{48,80},{56,88},{64,... | collective-permute-start | bytes 2752520 | tf_op jit(solution)/shard_map/ppermute | solution.py:284
  223.9 19.7 %collective-permute-start.29 = (f32[4,2,224,128]{3,2,1,0:T(8,128)}, f32[4,2,224,128]{3,2,1,0:T(8,128)}, u32[]{:S(2)}, u32[]{:S(2)}) collective-permute-start(f32[4,2,224,128]{3,2,1,0:T(8,128)} %pad_maximum_fusion.6), channel_id=1, source_target_pairs={{0,96},{8,104},{16,112},{24,120},{32,0},{40,8},{48,16},{56,24},{64... | collective-permute-start | bytes 2752520 | tf_op jit(solution)/shard_map/ppermute | solution.py:284
  228.8 23.3 %collective-permute-start.13 = (f32[4,2,224,128]{3,2,1,0:T(8,128)}, f32[4,2,224,128]{3,2,1,0:T(8,128)}, u32[]{:S(2)}, u32[]{:S(2)}) collective-permute-start(f32[4,2,224,128]{3,2,1,0:T(8,128)} %pad_maximum_fusion.2), channel_id=1, source_target_pairs={{0,8},{8,16},{16,24},{24,0},{32,40},{40,48},{48,56},{56,32},{64,72... | collective-permute-start | bytes 2752520 | tf_op jit(solution)/shard_map/ppermute | solution.py:284
  232.2 22.9 %collective-permute-start.15 = (f32[4,2,224,128]{3,2,1,0:T(8,128)}, f32[4,2,224,128]{3,2,1,0:T(8,128)}, u32[]{:S(2)}, u32[]{:S(2)}) collective-permute-start(f32[4,2,224,128]{3,2,1,0:T(8,128)} %pad_maximum_fusion.3), channel_id=1, source_target_pairs={{0,24},{8,0},{16,8},{24,16},{32,56},{40,32},{48,40},{56,48},{64,88... | collective-permute-start | bytes 2752520 | tf_op jit(solution)/shard_map/ppermute | solution.py:284
  246.9 11.4 %collective-permute-start.30 = (f32[2,224,128]{2,1,0:T(8,128)S(1)}, f32[2,224,128]{2,1,0:T(8,128)S(1)}, u32[]{:S(2)}, u32[]{:S(2)}) collective-permute-start(f32[2,224,128]{2,1,0:T(8,128)S(1)} %get-tuple-element.109), channel_id=1, source_target_pairs={{0,8},{8,16},{16,24},{24,0},{32,40},{40,48},{48,56},{56,32},{64,72... | collective-permute-start | bytes 688136 | tf_op jit(solution)/shard_map/ppermute | solution.py:284
  248.5 9.8 %collective-permute-start.31 = (f32[2,224,128]{2,1,0:T(8,128)S(1)}, f32[2,224,128]{2,1,0:T(8,128)S(1)}, u32[]{:S(2)}, u32[]{:S(2)}) collective-permute-start(f32[2,224,128]{2,1,0:T(8,128)S(1)} %get-tuple-element.111), channel_id=1, source_target_pairs={{0,24},{8,0},{16,8},{24,16},{32,56},{40,32},{48,40},{56,48},{64,88... | collective-permute-start | bytes 688136 | tf_op jit(solution)/shard_map/ppermute | solution.py:284
  250.2 9.4 %collective-permute-start.32 = (f32[2,224,128]{2,1,0:T(8,128)S(1)}, f32[2,224,128]{2,1,0:T(8,128)S(1)}, u32[]{:S(2)}, u32[]{:S(2)}) collective-permute-start(f32[2,224,128]{2,1,0:T(8,128)S(1)} %get-tuple-element.110), channel_id=1, source_target_pairs={{0,16},{8,24},{16,0},{24,8},{32,48},{40,56},{48,32},{56,40},{64,80... | collective-permute-start | bytes 688136 | tf_op jit(solution)/shard_map/ppermute | solution.py:284
  261.3 10.1 %collective-permute-start.33 = (f32[2,224,128]{2,1,0:T(8,128)S(1)}, f32[2,224,128]{2,1,0:T(8,128)S(1)}, u32[]{:S(2)}, u32[]{:S(2)}) collective-permute-start(f32[2,224,128]{2,1,0:T(8,128)S(1)} %get-tuple-element.75), channel_id=1, source_target_pairs={{0,24},{8,0},{16,8},{24,16},{32,56},{40,32},{48,40},{56,48},{64,88... | collective-permute-start | bytes 688136 | tf_op jit(solution)/shard_map/ppermute | solution.py:284
  265.3 7.8 %collective-permute-start.34 = (f32[2,224,128]{2,1,0:T(8,128)S(1)}, f32[2,224,128]{2,1,0:T(8,128)S(1)}, u32[]{:S(2)}, u32[]{:S(2)}) collective-permute-start(f32[2,224,128]{2,1,0:T(8,128)S(1)} %get-tuple-element.75), channel_id=1, source_target_pairs={{0,16},{8,24},{16,0},{24,8},{32,48},{40,56},{48,32},{56,40},{64,80... | collective-permute-start | bytes 688136 | tf_op jit(solution)/shard_map/ppermute | solution.py:284
  266.6 8.7 %collective-permute-start.35 = (f32[2,224,128]{2,1,0:T(8,128)S(1)}, f32[2,224,128]{2,1,0:T(8,128)S(1)}, u32[]{:S(2)}, u32[]{:S(2)}) collective-permute-start(f32[2,224,128]{2,1,0:T(8,128)S(1)} %get-tuple-element.75), channel_id=1, source_target_pairs={{0,8},{8,16},{16,24},{24,0},{32,40},{40,48},{48,56},{56,32},{64,72... | collective-permute-start | bytes 688136 | tf_op jit(solution)/shard_map/ppermute | solution.py:284
  267.5 11.0 %collective-permute-start.16 = (f32[2,224,128]{2,1,0:T(8,128)}, f32[2,224,128]{2,1,0:T(8,128)}, u32[]{:S(2)}, u32[]{:S(2)}) collective-permute-start(f32[2,224,128]{2,1,0:T(8,128)} %get-tuple-element.116), channel_id=1, source_target_pairs={{0,32},{8,40},{16,48},{24,56},{32,64},{40,72},{48,80},{56,88},{64,... | collective-permute-start | bytes 688136 | tf_op jit(solution)/shard_map/ppermute | solution.py:284
  267.5 11.0 %collective-permute-start.17 = (f32[2,224,128]{2,1,0:T(8,128)}, f32[2,224,128]{2,1,0:T(8,128)}, u32[]{:S(2)}, u32[]{:S(2)}) collective-permute-start(f32[2,224,128]{2,1,0:T(8,128)} %get-tuple-element.118), channel_id=1, source_target_pairs={{0,96},{8,104},{16,112},{24,120},{32,0},{40,8},{48,16},{56,24},{64... | collective-permute-start | bytes 688136 | tf_op jit(solution)/shard_map/ppermute | solution.py:284
  271.3 10.3 %collective-permute-start.18 = (f32[2,224,128]{2,1,0:T(8,128)}, f32[2,224,128]{2,1,0:T(8,128)}, u32[]{:S(2)}, u32[]{:S(2)}) collective-permute-start(f32[2,224,128]{2,1,0:T(8,128)} %get-tuple-element.117), channel_id=1, source_target_pairs={{0,64},{8,72},{16,80},{24,88},{32,96},{40,104},{48,112},{56,120},{... | collective-permute-start | bytes 688136 | tf_op jit(solution)/shard_map/ppermute | solution.py:284
  278.5 73.0 %collective-permute-start.37 = (f32[2,4,224,128]{3,2,0,1:T(8,128)}, f32[2,4,224,128]{3,2,0,1:T(8,128)}, u32[]{:S(2)}, u32[]{:S(2)}) collective-permute-start(f32[2,4,224,128]{3,2,0,1:T(8,128)} %copy.86), channel_id=1, source_target_pairs={{0,32},{8,40},{16,48},{24,56},{32,64},{40,72},{48,80},{56,88},{64,... | collective-permute-start | bytes 2752520 | tf_op jit(solution)/shard_map/ppermute | solution.py:284
  284.5 8.5 %collective-permute-start.19 = (f32[2,224,128]{2,1,0:T(8,128)S(1)}, f32[2,224,128]{2,1,0:T(8,128)S(1)}, u32[]{:S(2)}, u32[]{:S(2)}) collective-permute-start(f32[2,224,128]{2,1,0:T(8,128)S(1)} %get-tuple-element.73), channel_id=1, source_target_pairs={{0,96},{8,104},{16,112},{24,120},{32,0},{40,8},{48,16},{56,24},{64... | collective-permute-start | bytes 688136 | tf_op jit(solution)/shard_map/ppermute | solution.py:284
  284.6 20.7 %collective-permute-start.20 = (f32[2,224,128]{2,1,0:T(8,128)S(1)}, f32[2,224,128]{2,1,0:T(8,128)S(1)}, u32[]{:S(2)}, u32[]{:S(2)}) collective-permute-start(f32[2,224,128]{2,1,0:T(8,128)S(1)} %get-tuple-element.73), channel_id=1, source_target_pairs={{0,64},{8,72},{16,80},{24,88},{32,96},{40,104},{48,112},{56,120},{... | collective-permute-start | bytes 688136 | tf_op jit(solution)/shard_map/ppermute | solution.py:284
  285.5 22.8 %collective-permute-start.21 = (f32[2,224,128]{2,1,0:T(8,128)S(1)}, f32[2,224,128]{2,1,0:T(8,128)S(1)}, u32[]{:S(2)}, u32[]{:S(2)}) collective-permute-start(f32[2,224,128]{2,1,0:T(8,128)S(1)} %get-tuple-element.73), channel_id=1, source_target_pairs={{0,32},{8,40},{16,48},{24,56},{32,64},{40,72},{48,80},{56,88},{64,... | collective-permute-start | bytes 688136 | tf_op jit(solution)/shard_map/ppermute | solution.py:284
  287.0 66.6 %collective-permute-start.36 = (f32[2,4,224,128]{3,2,1,0:T(8,128)S(1)}, f32[2,4,224,128]{3,2,1,0:T(8,128)}, u32[]{:S(2)}, u32[]{:S(2)}) collective-permute-start(f32[2,4,224,128]{3,2,1,0:T(8,128)S(1)} %get-tuple-element.108), channel_id=1, source_target_pairs={{0,96},{8,104},{16,112},{24,120},{32,0},{40,8},{48,16},{56,24},{64... | collective-permute-start | bytes 2752520 | tf_op jit(solution)/shard_map/ppermute | solution.py:284
  310.6 47.8 %collective-permute-start.22 = (f32[2,4,224,128]{3,2,1,0:T(8,128)}, f32[2,4,224,128]{3,2,1,0:T(8,128)}, u32[]{:S(2)}, u32[]{:S(2)}) collective-permute-start(f32[2,4,224,128]{3,2,1,0:T(8,128)} %copy.76), channel_id=1, source_target_pairs={{0,24},{8,0},{16,8},{24,16},{32,56},{40,32},{48,40},{56,48},{64,88... | collective-permute-start | bytes 2752520 | tf_op jit(solution)/shard_map/ppermute | solution.py:284
  330.8 31.9 %collective-permute-start.23 = (f32[2,4,224,128]{3,2,0,1:T(8,128)}, f32[2,4,224,128]{3,2,0,1:T(8,128)S(1)}, u32[]{:S(2)}, u32[]{:S(2)}) collective-permute-start(f32[2,4,224,128]{3,2,0,1:T(8,128)} %copy-done), channel_id=1, source_target_pairs={{0,8},{8,16},{16,24},{24,0},{32,40},{40,48},{48,56},{56,32},{64,72... | collective-permute-start | bytes 2752520 | tf_op jit(solution)/shard_map/ppermute | solution.py:284
  331.6 1.2 collective-permute-start.40
  332.9 3.6 collective-permute-start.41
  336.5 4.8 %collective-permute-start.42 = (f32[8,128]{1,0:T(8,128)S(1)}, f32[8,128]{1,0:T(8,128)S(1)}, u32[]{:S(2)}, u32[]{:S(2)}) collective-permute-start(f32[8,128]{1,0:T(8,128)S(1)} %add.860), channel_id=1, source_target_pairs={{0,6},{1,7},{2,4},{3,5},{4,2},{5,3},{6,0},{7,1},{8,14},{9,15},{10,... | collective-permute-start | bytes 12296 | tf_op jit(solution)/shard_map/ppermute | solution.py:266
  341.3 3.6 collective-permute-start.43
  344.9 4.8 %collective-permute-start.44 = (f32[8,128]{1,0:T(8,128)S(1)}, f32[8,128]{1,0:T(8,128)S(1)}, u32[]{:S(2)}, u32[]{:S(2)}) collective-permute-start(f32[8,128]{1,0:T(8,128)S(1)} %add.862), channel_id=1, source_target_pairs={{0,24},{8,16},{16,8},{24,0},{32,56},{40,48},{48,40},{56,32},{64,88... | collective-permute-start | bytes 12296 | tf_op jit(solution)/shard_map/ppermute | solution.py:274
  349.8 16.0 %collective-permute-start.45 = (f32[8,128]{1,0:T(8,128)S(1)}, f32[8,128]{1,0:T(8,128)S(1)}, u32[]{:S(2)}, u32[]{:S(2)}) collective-permute-start(f32[8,128]{1,0:T(8,128)S(1)} %add.863), channel_id=1, source_target_pairs={{0,32},{8,40},{16,48},{24,56},{32,0},{40,8},{48,16},{56,24},{64,96... | collective-permute-start | bytes 12296 | tf_op jit(solution)/shard_map/ppermute | solution.py:274
  353.3 18.6 %collective-permute-start.38 = (f32[4,224,128]{2,1,0:T(8,128)}, f32[4,224,128]{2,1,0:T(8,128)S(1)}, u32[]{:S(2)}, u32[]{:S(2)}) collective-permute-start(f32[4,224,128]{2,1,0:T(8,128)} %slice_bitcast_fusion.1), channel_id=1, source_target_pairs={{0,32},{8,40},{16,48},{24,56},{32,64},{40,72},{48,80},{56,88},{64,... | collective-permute-start | bytes 1376264 | tf_op jit(solution)/shard_map/ppermute | solution.py:284
  355.4 16.6 %collective-permute-start.39 = (f32[4,224,128]{2,1,0:T(8,128)}, f32[4,224,128]{2,1,0:T(8,128)S(1)}, u32[]{:S(2)}, u32[]{:S(2)}) collective-permute-start(f32[4,224,128]{2,1,0:T(8,128)} %slice_bitcast_fusion), channel_id=1, source_target_pairs={{0,96},{8,104},{16,112},{24,120},{32,0},{40,8},{48,16},{56,24},{64... | collective-permute-start | bytes 1376264 | tf_op jit(solution)/shard_map/ppermute | solution.py:284
  360.2 11.9 %collective-permute-start.25 = (f32[4,224,128]{2,1,0:T(8,128)}, f32[4,224,128]{2,1,0:T(8,128)S(1)}, u32[]{:S(2)}, u32[]{:S(2)}) collective-permute-start(f32[4,224,128]{2,1,0:T(8,128)} %slice_bitcast_fusion.6), channel_id=1, source_target_pairs={{0,24},{8,0},{16,8},{24,16},{32,56},{40,32},{48,40},{56,48},{64,88... | collective-permute-start | bytes 1376264 | tf_op jit(solution)/shard_map/ppermute | solution.py:284
  364.5 10.0 %collective-permute-start.24 = (f32[4,224,128]{2,1,0:T(8,128)}, f32[4,224,128]{2,1,0:T(8,128)}, u32[]{:S(2)}, u32[]{:S(2)}) collective-permute-start(f32[4,224,128]{2,1,0:T(8,128)} %slice_bitcast_fusion.7), channel_id=1, source_target_pairs={{0,8},{8,16},{16,24},{24,0},{32,40},{40,48},{48,56},{56,32},{64,72... | collective-permute-start | bytes 1376264 | tf_op jit(solution)/shard_map/ppermute | solution.py:284
  365.8 4.9 %collective-permute-start.46 = (f32[8,128]{1,0:T(8,128)S(1)}, f32[8,128]{1,0:T(8,128)S(1)}, u32[]{:S(2)}, u32[]{:S(2)}) collective-permute-start(f32[8,128]{1,0:T(8,128)S(1)} %add.864), channel_id=1, source_target_pairs={{0,96},{8,104},{16,112},{24,120},{32,64},{40,72},{48,80},{56,88},{... | collective-permute-start | bytes 12296 | tf_op jit(solution)/shard_map/ppermute | solution.py:274
  (38 other events, 543.6 us)

commit v2 on v1

v2 whole, which is shorter than its diff:
```python
import functools

import jax
import jax.numpy as jnp
import numpy as np
from jax import lax
from jax.experimental import pallas as pl
from jax.experimental.pallas import tpu as pltpu
from jax.sharding import PartitionSpec as P

ITERS = 12
penalty = 1.0
step_size = 0.02
dual_step = 0.02
keep = 1.0 - step_size * penalty
CREW_PAD = 384
LIMIT = 14 * 1024 * 1024
bf16 = jnp.bfloat16
f32 = jnp.float32

PAIR_A = {0: 1, 1: 0, 2: 3, 3: 2}
PAIR_B = {0: 3, 3: 0, 1: 2, 2: 1}


def split3(value):
    hi = value.astype(bf16)
    rest = value - hi.astype(f32)
    mid = rest.astype(bf16)
    low = (rest - mid.astype(f32)).astype(bf16)
    return jnp.concatenate([hi, mid, low], axis=0)


def exact_dot(left, right):
    rows = left.shape[0]
    out = jnp.dot(split3(left), right, preferred_element_type=f32)
    return out[:rows] + out[rows : 2 * rows] + out[2 * rows :]


def folded(value):
    return jnp.sum(value.reshape(-1, 8, value.shape[1]), axis=0)


def used_dot(used, row_to_veh):
    flat = jnp.sum(used, axis=1)
    rows = flat.shape[0]
    out = lax.dot_general(
        split3(flat), row_to_veh, (((1,), (1,)), ((), ())), preferred_element_type=f32
    )
    return out[:rows] + out[rows : 2 * rows] + out[2 * rows :]


def first_kernel(
    bundles,
    start_ref,
    cost_ref,
    price_ref,
    anchor_0,
    anchor_1,
    hess_ref,
    coef_ref,
    dual_ref,
    row_ref,
    partial_ref,
    linear_ref,
    coef_t_ref,
    row_to_veh,
    usage_ref,
    crew_scr,
    used_scr,
    block_scr,
):
    step = pl.program_id(0)
    count = pl.num_programs(0)
    n = hess_ref.shape[-1]

    @pl.when(step == 0)
    def _():
        block_scr[...] = jnp.zeros_like(block_scr)
        ids = lax.broadcasted_iota(jnp.int32, row_to_veh.shape, 0)
        row_to_veh[...] = (ids == row_ref[...]).astype(f32).astype(bf16)
        crew_scr[:, 0, :] = step_size * exact_dot(dual_ref[...], row_to_veh[...])
        used_scr[48:56] = jnp.zeros_like(used_scr[48:56])
        c = coef_ref[...].astype(f32).T
        coef_t_ref[...] = c
        used_scr[48] = folded(c * c)

    block_scr[0:n, 0:n] = hess_ref[0]
    block_scr[n:, n:] = hess_ref[1]
    both = block_scr[...]
    c = coef_t_ref[...]
    s = 2 * step
    xs = []
    for i, anchor_ref in enumerate((anchor_0, anchor_1)):
        linear = step_size * (
            cost_ref[i].astype(f32) + price_ref[i].astype(f32) - penalty * anchor_ref[0].astype(f32)
        )
        linear_ref[s + i] = linear.T
        x = start_ref[i].astype(f32).T
        used_scr[s + i] = folded(c * x)
        xs.append(x)
    for k in (1, 2):
        stacked = jnp.concatenate([x.astype(bf16) for x in xs], axis=0)
        curve = jnp.dot(both, stacked, preferred_element_type=f32)
        for i in range(2):
            x = (keep * xs[i] - linear_ref[s + i]) - step_size * curve[i * n : (i + 1) * n]
            if k < 2:
                x = x - crew_scr[s + i] * c
            used_scr[16 * k + s + i] = folded(c * x)
            xs[i] = x
    for i in range(2):
        partial_ref[s + i] = xs[i]

    @pl.when(step == count - 1)
    def _():
        usage_ref[...] = used_dot(used_scr[...], row_to_veh[...])


def crew_update(usage, norms, limit, dual):
    one = jnp.maximum(dual + dual_step * (usage[0:16] - limit), 0.0)
    third = usage[32:48] - step_size * one * norms
    two = jnp.maximum(one + dual_step * (usage[16:32] - limit), 0.0)
    three = jnp.maximum(two + dual_step * (third - limit), 0.0)
    return one, two, three


def middle_kernel(
    partial_ref,
    linear_ref,
    hess_ref,
    coef_t_ref,
    use_a,
    use_b,
    norms_ref,
    limit_ref,
    dual_ref,
    row_to_veh,
    next_ref,
    usage_ref,
    new_dual_ref,
    crew_scr,
    used_scr,
    block_scr,
):
    count = partial_ref.shape[0]
    n = hess_ref.shape[-1]
    one, two, three = crew_update(
        use_a[0:48] + use_b[0:48], norms_ref[0:1], limit_ref[...], dual_ref[...]
    )
    new_dual_ref[...] = three
    crew_scr[:, 0, :] = step_size * exact_dot(
        jnp.concatenate([one, two, three], axis=0), row_to_veh[...]
    )
    block_scr[...] = jnp.zeros_like(block_scr)

    def two_scenarios(pair, carry):
        s = 2 * pair
        block_scr[0:n, 0:n] = hess_ref[s]
        block_scr[n:, n:] = hess_ref[s + 1]
        both = block_scr[...]
        c = coef_t_ref[...]
        xs = [partial_ref[s + i] - crew_scr[s + i] * c for i in range(2)]
        for k in (1, 2, 3):
            stacked = jnp.concatenate([x.astype(bf16) for x in xs], axis=0)
            curve = jnp.dot(both, stacked, preferred_element_type=f32)
            for i in range(2):
                x = (keep * xs[i] - linear_ref[s + i]) - step_size * curve[i * n : (i + 1) * n]
                if k < 3:
                    x = x - crew_scr[16 * k + s + i] * c
                used_scr[16 * (k - 1) + s + i] = folded(c * x)
                xs[i] = x
        for i in range(2):
            next_ref[s + i] = xs[i]
        return carry

    lax.fori_loop(0, count // 2, two_scenarios, 0)
    usage_ref[...] = used_dot(used_scr[...], row_to_veh[...])


def last_kernel(
    slots,
    factors,
    partial_ref,
    linear_ref,
    hess_ref,
    coef_t_ref,
    use_a,
    use_b,
    norms_ref,
    limit_ref,
    dual_ref,
    row_to_veh,
    plan_ref,
    roster_ref,
    sum_a,
    sum_b,
    send_au,
    send_ad,
    send_bu,
    send_bd,
    spread_ref,
    new_dual_ref,
    crew_scr,
):
    s = pl.program_id(0)
    count = pl.num_programs(0)
    rows = sum_a.shape[1]

    @pl.when(s == 0)
    def _():
        one, two, three = crew_update(
            use_a[0:48] + use_b[0:48], norms_ref[0:1], limit_ref[...], dual_ref[...]
        )
        new_dual_ref[...] = three
        crew_scr[:, 0, :] = step_size * exact_dot(
            jnp.concatenate([one, two], axis=0), row_to_veh[...]
        )
        sum_a[...] = jnp.zeros_like(sum_a)
        sum_b[...] = jnp.zeros_like(sum_b)
        spread_ref[...] = jnp.zeros_like(spread_ref)

    c = coef_t_ref[...]
    x = partial_ref[s] - crew_scr[s] * c
    curve = jnp.dot(hess_ref[s], x.astype(bf16), preferred_element_type=f32)
    x = (keep * x - linear_ref[s]) - step_size * curve - crew_scr[16 + s] * c
    roster_ref[s] = x.T

    weight, merge, inverse = factors[0, s], factors[1, s], factors[2, s]
    part = 112
    spread = jnp.zeros((8, 128), f32)
    for side, sums in enumerate((sum_a, sum_b)):
        slot = slots[side, s]
        for start in range(0, rows, part):
            here = pl.ds(side * rows + start, part)
            x = roster_ref[s, here, :]
            plan_ref[0, here, :] = x.astype(bf16)
            held = sums[slot, start : start + part, :]
            gap = held * inverse - x
            spread = spread + merge * folded(gap * gap)
            sums[slot, start : start + part, :] = held + weight * x
    spread_ref[...] += spread

    @pl.when(s == count - 1)
    def _():
        for sums, up, down in ((sum_a, send_au, send_ad), (sum_b, send_bu, send_bd)):
            for k in range(4):
                up[k] = sums[8 + k, : rows // 2, :]
                down[k] = sums[8 + k, rows // 2 :, :]


def merge_into(total, weight, other, other_weight):
    weight = jnp.full((8, 128), weight, f32)
    other_weight = jnp.full((8, 128), other_weight, f32)
    both = weight + other_weight
    factor = jnp.where(both > 0, weight * other_weight / jnp.maximum(both, 1.0), 0.0)
    shape = total.shape
    total8, other8 = total.reshape(-1, 8, 128), other.reshape(-1, 8, 128)
    gap = total8 * (1.0 / jnp.maximum(weight, 1.0)) - other8 * (1.0 / jnp.maximum(other_weight, 1.0))
    return total + other, factor * jnp.sum(gap * gap, axis=0)


def forward_kernel(weights, sums, up_in, down_in, up_out, down_out, spread_ref):
    rows = sums.shape[1] // 2
    spread = jnp.zeros((8, 128), f32)
    for k in range(4):
        total, more = merge_into(sums[4 + k, :rows, :], weights[0, 4 + k], up_in[k], weights[12, 4 + k])
        spread += more
        up_out[0, k] = total
        up_out[1, k] = sums[4 + k, rows:, :]
        down_out[0, k] = sums[12 + k, :rows, :]
        total, more = merge_into(
            sums[12 + k, rows:, :], weights[0, 12 + k], down_in[k], weights[4, 12 + k]
        )
        spread += more
        down_out[1, k] = total
    spread_ref[...] = spread


def arrive_kernel(weights, sums, up_in, down_in, own, out_1, out_2, out_3, spread_ref):
    rows = sums.shape[1] // 2
    spread = jnp.zeros((8, 128), f32)
    for k, out in enumerate((own, out_1, out_2, out_3)):
        w0, w1, w2, w3 = (weights[4 * e, k] for e in range(4))
        for half in range(2):
            here = slice(half * rows, (half + 1) * rows)
            w_up, w_down = (w3 + w2, w1) if half == 0 else (w3, w1 + w2)
            total, more = merge_into(sums[k, here, :], w0, up_in[half, k], w_up)
            spread += more
            total, more = merge_into(total, w0 + w_up, down_in[half, k], w_down)
            spread += more
            out[here, :] = total
    spread_ref[...] = spread


def finish_kernel(weights, own, in_1, in_2, in_3, mean_ref, spread_ref):
    line = [sum(weights[4 * e + j, 0] for e in range(4)) for j in range(4)]
    total, weight = own[...], line[0]
    spread = jnp.zeros((8, 128), f32)
    for by, part in ((1, in_1), (3, in_3), (2, in_2)):
        total, more = merge_into(total, weight, part[...], line[4 - by])
        spread += more
        weight = weight + line[4 - by]
    mean_ref[...] = total / jnp.full((8, 128), weight, f32)[0:1]
    spread_ref[...] = spread


def price_kernel(slots, roster_ref, price_ref, spread_ref, weight_ref, *refs):
    means, out_ref, gap_ref = refs[:10], refs[10], refs[11]
    each = price_ref.shape[0]
    rows = means[3].shape[1]

    @pl.when(pl.program_id(0) == 0)
    def _():
        spread = jnp.sum(spread_ref[...], keepdims=True)
        gap_ref[...] = jnp.sqrt(spread / jnp.sum(weight_ref[...], keepdims=True))

    for i in range(each):
        s = pl.program_id(0) * each + i
        for side in range(2):
            slot = slots[side, s]
            first, second = slot // 4, slot % 4
            pack, one, third, two_low, two_high = means[side * 5 : side * 5 + 5]
            for k in range(4):

                @pl.when(first == k)
                def _():
                    for half in range(2):
                        if k == 2:
                            mean = (two_low, two_high)[half][second]
                        else:
                            mean = (pack, one, None, third)[k][half, second]
                        here = pl.ds((side * 2 + half) * rows, rows)
                        deviation = roster_ref[s, here, :] - mean
                        out_ref[i, here, :] = (
                            price_ref[i, here, :].astype(f32) + penalty * deviation
                        ).astype(bf16)


def veh_pairs(kind):
    if kind == "core":
        return [(i, i ^ 1) for i in range(8)]
    return [(z * 2 + c, kind[z] * 2 + c) for z in range(4) for c in range(2)]


def scen_pairs(pair, axis):
    out = []
    for y in range(4):
        for x in range(4):
            to = (y * 4 + pair[x]) if axis == "x" else (pair[y] * 4 + x)
            out.append((y * 4 + x, to))
    return out


def usage_exchange(value):
    value = value + lax.ppermute(value, "veh", veh_pairs("core"))
    value = value + lax.ppermute(value, "veh", veh_pairs(PAIR_A))
    return value, lax.ppermute(value, "veh", veh_pairs(PAIR_B))


def sum_everywhere(value):
    a, b = usage_exchange(value)
    value = a + b
    for axis in ("x", "y"):
        for pair in (PAIR_A, PAIR_B):
            value = value + lax.ppermute(value, "scen", scen_pairs(pair, axis))
    return value


def shift(value, axis, by):
    pairs = []
    for y in range(4):
        for x in range(4):
            to = (y * 4 + (x + by) % 4) if axis == "x" else (((y + by) % 4) * 4 + x)
            pairs.append((y * 4 + x, to))
    return lax.ppermute(value, "scen", pairs)


def vmem_spec():
    return pl.BlockSpec(memory_space=pltpu.VMEM)


def in_vmem(value):
    return pltpu.with_memory_space_constraint(value, pltpu.VMEM)


def in_hbm(value):
    return pltpu.with_memory_space_constraint(value, pltpu.HBM)


def local_call(body, weights, arrays, out_shapes, name):
    return pl.pallas_call(
        body,
        in_specs=[pl.BlockSpec(memory_space=pltpu.SMEM)] + [vmem_spec()] * len(arrays),
        out_specs=[vmem_spec()] * (len(out_shapes) + 1),
        out_shape=[pltpu.VMEM(shape, f32) for shape in out_shapes] + [pltpu.VMEM((8, 128), f32)],
        compiler_params=pltpu.CompilerParams(vmem_limit_bytes=LIMIT),
        name=name,
    )(weights, *[in_vmem(a) for a in arrays])


def gather_row(own, second):
    return {0: own, **{by: shift(own, second, -by) for by in (1, 3, 2)}}


def gather_half(row, first):
    rows = row[0].shape[0] // 2
    pack = jnp.stack([row[k].reshape(2, rows, -1) for k in range(4)], axis=1)
    third = shift(pack, first, 1)
    one = shift(pack, first, -1)
    two_low = shift(third[0], first, 1)
    two_high = shift(one[1], first, -1)
    return [pack, one, third, two_low, two_high]


def shards(
    start_plan,
    linear_cost,
    price,
    anchor,
    hessian,
    usage_coef,
    crew_limit,
    crew_dual,
    crew_row,
    bundle_of,
    scen_weight,
):
    count, vehicles, n = start_plan.shape
    crews = crew_limit.shape[1]
    bundle_count = anchor.shape[0]
    me = lax.axis_index("scen")
    all_bundles = bundle_of[:, 0]
    my_bundles = lax.dynamic_slice_in_dim(all_bundles, me * count, count)
    all_weights = scen_weight.astype(f32)
    my_weights = lax.dynamic_slice_in_dim(all_weights, me * count, count)

    pad = ((0, 0), (0, CREW_PAD - crews))
    limit = jnp.pad(crew_limit, pad)
    dual = jnp.pad(crew_dual, pad)
    def per_scen(*shape):
        return pl.BlockSpec((1, *shape), lambda s, *_: (s, 0, 0))

    def whole(*shape):
        return pl.BlockSpec(shape, lambda s, *_: (0,) * len(shape))

    params = pltpu.CompilerParams(
        dimension_semantics=("arbitrary",), vmem_limit_bytes=LIMIT
    )
    tall = pltpu.VMEM((count, n, vehicles), f32)
    flat_block = per_scen(vehicles, n)
    pair_block = pl.BlockSpec((2, vehicles, n), lambda s, *_: (s, 0, 0))
    vm = vmem_spec()

    partial, linear, coef_t, row_to_veh, usage = pl.pallas_call(
        first_kernel,
        grid_spec=pltpu.PrefetchScalarGridSpec(
            num_scalar_prefetch=1,
            grid=(count // 2,),
            in_specs=[
                pair_block,
                pair_block,
                pair_block,
                pl.BlockSpec((1, vehicles, n), lambda s, b: (b[2 * s], 0, 0)),
                pl.BlockSpec((1, vehicles, n), lambda s, b: (b[2 * s + 1], 0, 0)),
                pl.BlockSpec((2, n, n), lambda s, *_: (s, 0, 0)),
                whole(vehicles, n),
                whole(count, CREW_PAD),
                whole(1, vehicles),
            ],
            out_specs=[vm] * 5,
            scratch_shapes=[
                pltpu.VMEM((16, 1, vehicles), f32),
                pltpu.VMEM((56, 8, vehicles), f32),
                pltpu.VMEM((2 * n, 2 * n), bf16),
            ],
        ),
        out_shape=[
            tall,
            tall,
            pltpu.VMEM((n, vehicles), f32),
            pltpu.VMEM((CREW_PAD, vehicles), bf16),
            pltpu.VMEM((56, CREW_PAD), f32),
        ],
        compiler_params=params,
        name="first_steps",
    )(
        my_bundles,
        in_hbm(start_plan),
        in_hbm(linear_cost),
        in_hbm(price),
        in_hbm(anchor),
        in_hbm(anchor),
        hessian,
        usage_coef,
        dual,
        crew_row[None, :],
    )

    use_a, use_b = usage_exchange(usage)
    norms = use_a[48:56] + use_b[48:56]
    for _ in range(3):
        partial, usage, dual = pl.pallas_call(
            middle_kernel,
            in_specs=[vm] * 10,
            out_specs=[vm] * 3,
            out_shape=[
                tall,
                pltpu.VMEM((48, CREW_PAD), f32),
                pltpu.VMEM((count, CREW_PAD), f32),
            ],
            input_output_aliases={0: 0},
            scratch_shapes=[
                pltpu.VMEM((48, 1, vehicles), f32),
                pltpu.VMEM((48, 8, vehicles), f32),
                pltpu.VMEM((2 * n, 2 * n), bf16),
            ],
            compiler_params=pltpu.CompilerParams(vmem_limit_bytes=LIMIT),
            name="three_steps",
        )(
            *[
                in_vmem(a)
                for a in (
                    partial,
                    linear,
                    hessian,
                    coef_t,
                    use_a,
                    use_b,
                    norms,
                    limit,
                    dual,
                    row_to_veh,
                )
            ]
        )
        use_a, use_b = usage_exchange(usage)

    me_y, me_x = np.arange(16)[:, None] // 4, np.arange(16)[:, None] % 4
    it_y, it_x = np.arange(16)[None, :] // 4, np.arange(16)[None, :] % 4
    place_a = ((it_x - me_x) % 4) * 4 + (it_y - me_y) % 4
    place_b = ((it_y - me_y) % 4) * 4 + (it_x - me_x) % 4
    here = jnp.arange(16, dtype=jnp.int32) == me
    row_a = jnp.sum(jnp.where(here[:, None], place_a, 0), axis=0)
    row_b = jnp.sum(jnp.where(here[:, None], place_b, 0), axis=0)
    ids = jnp.arange(16, dtype=jnp.int32)
    hot = my_bundles[:, None] == ids[None, :]
    slots = jnp.stack(
        [jnp.sum(jnp.where(hot, row[None, :], 0), axis=1) for row in (row_a, row_b)]
    ).astype(jnp.int32)
    same = my_bundles[:, None] == my_bundles[None, :]
    before = jnp.arange(count)[None, :] < jnp.arange(count)[:, None]
    held = jnp.sum(jnp.where(same & before, my_weights[None, :], 0.0), axis=1)
    factors = jnp.stack(
        [
            my_weights,
            held * my_weights / (held + my_weights),
            1.0 / jnp.maximum(held, 1.0),
        ]
    )
    half = vehicles // 2
    bundle_sums = pltpu.VMEM((bundle_count, half, n), f32)
    quarter = pltpu.VMEM((4, half // 2, n), f32)
    plan, roster, sum_a, sum_b, up_a, down_a, up_b, down_b, spread, dual = pl.pallas_call(
        last_kernel,
        grid_spec=pltpu.PrefetchScalarGridSpec(
            num_scalar_prefetch=2,
            grid=(count,),
            in_specs=[vm] * 10,
            out_specs=[flat_block] + [vm] * 9,
            scratch_shapes=[pltpu.VMEM((32, 1, vehicles), f32)],
        ),
        out_shape=[
            jax.ShapeDtypeStruct((count, vehicles, n), bf16),
            pltpu.VMEM((count, vehicles, n), f32),
            bundle_sums,
            bundle_sums,
            quarter,
            quarter,
            quarter,
            quarter,
            pltpu.VMEM((8, n), f32),
            pltpu.VMEM((count, CREW_PAD), f32),
        ],
        compiler_params=params,
        name="last_step",
    )(
        slots,
        factors,
        *[
            in_vmem(a)
            for a in (
                partial,
                linear,
                hessian,
                coef_t,
                use_a,
                use_b,
                norms,
                limit,
                dual,
                row_to_veh,
            )
        ],
    )

    owners = jnp.arange(all_bundles.shape[0], dtype=jnp.int32) // count

    def weight_table(row):
        device = jnp.sum(jnp.where(owners[:, None] == ids[None, :], row[None, :], 0), axis=1)
        bundle = jnp.sum(jnp.where(all_bundles[:, None] == ids[None, :], row[None, :], 0), axis=1)
        return jnp.sum(
            jnp.where(
                (device[None, None, :] == ids[:, None, None])
                & (bundle[None, None, :] == ids[None, :, None]),
                all_weights[None, None, :],
                0.0,
            ),
            axis=2,
        )

    weights_a = weight_table(row_a)
    weights_b = weight_table(row_b)

    sides = (
        ("x", "y", weights_a, sum_a, up_a, down_a),
        ("y", "x", weights_b, sum_b, up_b, down_b),
    )
    flow = (2, 4, half // 2, n)
    flat = (half, n)
    moved = [(shift(up, f, 1), shift(down, f, -1)) for f, _, _, _, up, down in sides]
    moved = [
        local_call(forward_kernel, w, (sums, up, down), [flow, flow], "forward")
        for (_, _, w, sums, _, _), (up, down) in zip(sides, moved)
    ]
    spreads = [spread] + [m[2] for m in moved]
    moved = [(shift(m[0], side[0], 1), shift(m[1], side[0], -1)) for side, m in zip(sides, moved)]
    moved = [
        local_call(arrive_kernel, w, (sums, up, down), [flat] * 4, "arrive")
        for (_, _, w, sums, _, _), (up, down) in zip(sides, moved)
    ]
    spreads += [m[4] for m in moved]
    moved = [
        (m[0], *[shift(m[by], side[1], by) for by in (1, 2, 3)]) for side, m in zip(sides, moved)
    ]
    moved = [
        local_call(finish_kernel, side[2], m, [flat], "finish") for side, m in zip(sides, moved)
    ]
    spreads += [m[1] for m in moved]
    own_a, own_b = moved[0][0], moved[1][0]
    row_a, row_b = gather_row(own_a, "y"), gather_row(own_b, "x")
    row_a, row_b, spread = lax.optimization_barrier((row_a, row_b, sum(spreads)))
    means = gather_half(row_a, "x") + gather_half(row_b, "y")
    spread_total = sum_everywhere(spread)
    entries = vehicles * lax.axis_size("veh") * n

    each = 2
    new_price, gap = pl.pallas_call(
        price_kernel,
        grid_spec=pltpu.PrefetchScalarGridSpec(
            num_scalar_prefetch=1,
            grid=(count // each,),
            in_specs=[vm, pair_block] + [vm] * 12,
            out_specs=[pair_block, whole(1, 1)],
        ),
        out_shape=[
            jax.ShapeDtypeStruct((count, vehicles, n), bf16),
            jax.ShapeDtypeStruct((1, 1), f32),
        ],
        compiler_params=params,
        name="new_price",
    )(
        slots,
        in_vmem(roster),
        in_hbm(price),
        in_vmem(spread_total),
        in_vmem((all_weights * entries)[None, :]),
        *[in_vmem(m) for m in means],
    )

    own_mean = jnp.concatenate([own_a, own_b], axis=0)
    return (plan, new_price, own_mean.astype(bf16)[None], dual[:, :crews], gap[0, 0])


def solution(mesh):
    return jax.shard_map(
        shards,
        mesh=mesh,
        in_specs=(
            P("scen", "veh", None),
            P("scen", "veh", None),
            P("scen", "veh", None),
            P(None, "veh", None),
            P("scen", None, None),
            P("veh", None),
            P("scen", None),
            P("scen", None),
            P("veh"),
            P(),
            P(),
        ),
        out_specs=(
            P("scen", "veh", None),
            P("scen", "veh", None),
            P("scen", "veh", None),
            P("scen", None),
            P(),
        ),
        check_vma=False,
    )
```

time: 402 us -> 235 us (0.58)
  Pallas kernels: 137 us -> 66.5 us
  other arithmetic: 62.4 us -> 1.84 us
  local copies, waits for them, and re-layouts: 35.1 us -> 4.45 us
  between operations: 18.7 us -> 0.97 us
  starting transfers between devices: 60.8 us -> 71.3 us
  waiting for transfers between devices: 84.4 us -> 88.9 us
    pallas_call x3 -> x9, Pallas kernels: 68.9 us -> 35.4 us  [the longest x3 29.6 us: shards(): pl.pallas_call(middle_kernel, in_specs=[vm] * 10, out_specs=[vm] * 3, out...]
    pallas_call x1, Pallas kernels: 32.5 us -> 13 us  [shards(): pl.pallas_call(first_kernel, grid_spec=pltpu.PrefetchScalarGridSpec(num_s...]
    reduce_sum x18 -> x4, other arithmetic: 19.7 us -> 0.51 us  [the longest x1 0.18 us: shards(): jnp.sum(jnp.where(hot, row[None, :], 0), axis=1)]
    another operation x13 -> x3, other arithmetic: 18 us -> 0.16 us  [the longest x2 0.15 us: gather_half(): pack = jnp.stack([row[k].reshape(2, rows, -1) for k in range(4)], axis=1)]
    slice x30 -> x0, local copies, waits for them, and re-layouts: 16.8 us -> none  [the longest x24 12.8 us: reduce_half(): from_row = sum((weight(e, (4 - by) % 4)[0, 0] for e in range(4)))]
    ppermute x4, waiting for transfers between devices: 7.47 us -> 24.1 us  [sum_everywhere(): value = value + lax.ppermute(value, 'scen', scen_pairs(pair, axis))]
    ppermute x28, waiting for transfers between devices: 44.1 us -> 30.6 us  [shift(): return lax.ppermute(value, 'scen', pairs)]
    mul x8 -> x1, other arithmetic: 10.7 us -> 0.01 us  [shards(): all_weights * entries]
  transfers between devices with their start and end apart: 47 -> 47, of which waited for: 28 -> 26; matrix products, arithmetic and copies ran while one was open for 17% -> 1% of each run, Pallas kernels for 0% -> 2%
where the time goes in v2:
time: 235 us; the launch traced here: 234 us
  waiting for transfers between devices  88.9 us (38%)
  starting transfers between devices  71.3 us (30%)
  Pallas kernels  66.5 us (28%)
  local copies, waits for them, and re-layouts  4.45 us (2%)
    ppermute x28, starting transfers between devices, shift(): return lax.ppermute(value, 'scen', pairs)  46.8 us
    ppermute x28, waiting for transfers between devices, shift(): return lax.ppermute(value, 'scen', pairs)  30.6 us
    pallas_call x3, Pallas kernels, shards(): pl.pallas_call(middle_kernel, in_specs=[vm] * 10, out_specs=[vm] * 3, out...  29.6 us
    ppermute x4, waiting for transfers between devices, sum_everywhere(): value = value + lax.ppermute(value, 'scen', scen_pairs(pair, axis))  24.1 us
    ppermute x5, waiting for transfers between devices, usage_exchange(): value = value + lax.ppermute(value, 'veh', veh_pairs(PAIR_A))  19.2 us
    ppermute x5, starting transfers between devices, usage_exchange(): return (value, lax.ppermute(value, 'veh', veh_pairs(PAIR_B)))  17.1 us
    pallas_call x1, Pallas kernels, shards(): pl.pallas_call(first_kernel, grid_spec=pltpu.PrefetchScalarGridSpec(num_s...  13 us
    pallas_call x1, Pallas kernels, shards(): pl.pallas_call(last_kernel, grid_spec=pltpu.PrefetchScalarGridSpec(num_sc...  10.4 us
  transfers between devices with their start and end apart: 47, of which 26 were waited for; matrix products, arithmetic and copies ran while one was open for 1% of the time, Pallas kernels for 2%

profile of v2, /device:TPU:0, one launch (start us, length us, event | category | flops | bytes accessed | tf_op | source)
XLA Modules:
  0.0 233.9 jit_solution(11239148704905714836)
XLA Ops:
  4.8 13.0 %first_steps.1 = (f32[16,128,896]{2,1,0:T(8,128)S(1)}, f32[16,128,896]{2,1,0:T(8,128)S(1)}, f32[128,896]{1,0:T(8,128)S(1)}, bf16[384,896]{1,0:T(8,128)(2,1)S(1)}, f32[56,384]{1,0:T(8,128)S(1)}) custom-call(s32[16]{0:T(128)S(1)} %dynamic-slice_bitcast_fusion.bundles, bf16[16,896,128]{2,1,0:T(8,128)(2,1)} %start_ref.1, bf16[16,896,128]{2,1,0:T(8,128)(2,1)} %cost_ref.1, ...), custom_call_target="tpu_custom_call" | custom-call | tf_op jit(solution)/shard_map/first_steps/pallas_call | solution.py:453
  19.2 2.1 collective-permute-start.1
  21.3 2.7 %collective-permute-done.1 = f32[56,384]{1,0:T(8,128)S(1)} collective-permute-done((f32[56,384]{1,0:T(8,128)S(1)}, f32[56,384]{1,0:T(8,128)S(1)}, u32[]{:S(2)}, u32[]{:S(2)}) %collective-permute-start.1) | collective-permute-done | bytes 86048 | tf_op jit(solution)/shard_map/ppermute | solution.py:355
  24.1 3.9 %collective-permute-start.2 = (f32[56,384]{1,0:T(8,128)S(1)}, f32[56,384]{1,0:T(8,128)S(1)}, u32[]{:S(2)}, u32[]{:S(2)}) collective-permute-start(f32[56,384]{1,0:T(8,128)S(1)} %add.85.use_a), channel_id=1, source_target_pairs={{0,6},{1,7},{2,4},{3,5},{4,2},{5,3},{6,0},{7,1},{8,14},{9,15},{10,... | collective-permute-start | bytes 258056 | tf_op jit(solution)/shard_map/ppermute | solution.py:356
  28.2 2.3 collective-permute-done.2.use_b
  30.5 9.9 %three_steps.3 = (f32[16,128,896]{2,1,0:T(8,128)S(1)}, f32[48,384]{1,0:T(8,128)S(1)}, f32[16,384]{1,0:T(8,128)S(1)}) custom-call(f32[16,128,896]{2,1,0:T(8,128)S(1)} %get-tuple-element.60.partial_ref, f32[16,128,896]{2,1,0:T(8,128)S(1)} %get-tuple-element.61.linear_ref, bf16[16,128,128]{2,1,0:T(8,128)(2,1)S(1)} %copy-done.1, ...), custom_call_target="tpu_custom_call", output_to_operand_aliasing={{0}: (0, {})} | custom-call | tf_op jit(solution)/shard_map/three_steps/pallas_call | solution.py:501
  41.9 4.3 %collective-permute-done.4 = f32[48,384]{1,0:T(8,128)S(1)} collective-permute-done((f32[48,384]{1,0:T(8,128)S(1)}, f32[48,384]{1,0:T(8,128)S(1)}, u32[]{:S(2)}, u32[]{:S(2)}) %collective-permute-start.4) | collective-permute-done | bytes 73760 | tf_op jit(solution)/shard_map/ppermute | solution.py:355
  46.2 3.3 %collective-permute-start.5 = (f32[48,384]{1,0:T(8,128)S(1)}, f32[48,384]{1,0:T(8,128)S(1)}, u32[]{:S(2)}, u32[]{:S(2)}) collective-permute-start(f32[48,384]{1,0:T(8,128)S(1)} %add.88.use_a), channel_id=1, source_target_pairs={{0,6},{1,7},{2,4},{3,5},{4,2},{5,3},{6,0},{7,1},{8,14},{9,15},{10,... | collective-permute-start | bytes 221192 | tf_op jit(solution)/shard_map/ppermute | solution.py:356
  49.6 2.2 collective-permute-done.5.use_b
  51.9 9.9 %three_steps.4 = (f32[16,128,896]{2,1,0:T(8,128)S(1)}, f32[48,384]{1,0:T(8,128)S(1)}, f32[16,384]{1,0:T(8,128)S(1)}) custom-call(f32[16,128,896]{2,1,0:T(8,128)S(1)} %get-tuple-element.65.partial_ref, f32[16,128,896]{2,1,0:T(8,128)S(1)} %get-tuple-element.61.linear_ref, bf16[16,128,128]{2,1,0:T(8,128)(2,1)S(1)} %copy-done.1, ...), custom_call_target="tpu_custom_call", output_to_operand_aliasing={{0}: (0, {})} | custom-call | tf_op jit(solution)/shard_map/three_steps/pallas_call | solution.py:501
  63.3 4.2 %collective-permute-done.7 = f32[48,384]{1,0:T(8,128)S(1)} collective-permute-done((f32[48,384]{1,0:T(8,128)S(1)}, f32[48,384]{1,0:T(8,128)S(1)}, u32[]{:S(2)}, u32[]{:S(2)}) %collective-permute-start.7) | collective-permute-done | bytes 73760 | tf_op jit(solution)/shard_map/ppermute | solution.py:355
  67.5 3.3 %collective-permute-start.8 = (f32[48,384]{1,0:T(8,128)S(1)}, f32[48,384]{1,0:T(8,128)S(1)}, u32[]{:S(2)}, u32[]{:S(2)}) collective-permute-start(f32[48,384]{1,0:T(8,128)S(1)} %add.90.use_a), channel_id=1, source_target_pairs={{0,6},{1,7},{2,4},{3,5},{4,2},{5,3},{6,0},{7,1},{8,14},{9,15},{10,... | collective-permute-start | bytes 221192 | tf_op jit(solution)/shard_map/ppermute | solution.py:356
  71.0 2.2 collective-permute-done.8.use_b
  73.2 9.9 %three_steps.5 = (f32[16,128,896]{2,1,0:T(8,128)S(1)}, f32[48,384]{1,0:T(8,128)S(1)}, f32[16,384]{1,0:T(8,128)S(1)}) custom-call(f32[16,128,896]{2,1,0:T(8,128)S(1)} %get-tuple-element.68.partial_ref, f32[16,128,896]{2,1,0:T(8,128)S(1)} %get-tuple-element.61.linear_ref, bf16[16,128,128]{2,1,0:T(8,128)(2,1)S(1)} %copy-done.1, ...), custom_call_target="tpu_custom_call", output_to_operand_aliasing={{0}: (0, {})} | custom-call | tf_op jit(solution)/shard_map/three_steps/pallas_call | solution.py:501
  84.7 4.3 %collective-permute-done.10 = f32[48,384]{1,0:T(8,128)S(1)} collective-permute-done((f32[48,384]{1,0:T(8,128)S(1)}, f32[48,384]{1,0:T(8,128)S(1)}, u32[]{:S(2)}, u32[]{:S(2)}) %collective-permute-start.10) | collective-permute-done | bytes 73760 | tf_op jit(solution)/shard_map/ppermute | solution.py:355
  89.0 3.3 %collective-permute-start.11 = (f32[48,384]{1,0:T(8,128)S(1)}, f32[48,384]{1,0:T(8,128)S(1)}, u32[]{:S(2)}, u32[]{:S(2)}) collective-permute-start(f32[48,384]{1,0:T(8,128)S(1)} %add.92.use_a), channel_id=1, source_target_pairs={{0,6},{1,7},{2,4},{3,5},{4,2},{5,3},{6,0},{7,1},{8,14},{9,15},{10,... | collective-permute-start | bytes 221192 | tf_op jit(solution)/shard_map/ppermute | solution.py:356
  92.4 2.3 collective-permute-done.11.use_b
  94.7 10.4 %last_step.1 = (bf16[16,896,128]{2,1,0:T(8,128)(2,1)}, f32[16,896,128]{2,1,0:T(8,128)S(1)}, f32[16,448,128]{2,1,0:T(8,128)S(1)}, f32[16,448,128]{2,1,0:T(8,128)S...) custom-call(s32[2,16]{1,0:T(2,128)S(1)} %pad_add_fusion.slots, ...), custom_call_target="tpu_custom_call" | custom-call | tf_op jit(solution)/shard_map/last_step/pallas_call | solution.py:562
  106.5 1.9 collective-permute-start.23
  109.6 2.0 collective-permute-start.13
  111.8 5.0 %collective-permute-done.22.up_in = f32[4,224,128]{2,1,0:T(8,128)S(1)} collective-permute-done((f32[4,224,128]{2,1,0:T(8,128)S(1)}, f32[4,224,128]{2,1,0:T(8,128)S(1)}, u32[]{:S(2)}, u32[]{:S(2)}) %collective-permute-start.22) | collective-permute-done | bytes 458784 | tf_op jit(solution)/shard_map/ppermute | solution.py:374
  117.8 1.4 collective-permute-start.24
  119.2 1.9 collective-permute-start.25
  123.4 2.0 collective-permute-start.15
  125.4 13.2 %collective-permute-done.24.up_in = f32[2,4,224,128]{3,2,1,0:T(8,128)S(1)} collective-permute-done((f32[2,4,224,128]{3,2,1,0:T(8,128)S(1)}, f32[2,4,224,128]{3,2,1,0:T(8,128)S(1)}, u32[]{:S(2)}, u32[]{:S(2)}) %collective-permute-start.24) | collective-permute-done | bytes 917536 | tf_op jit(solution)/shard_map/ppermute | solution.py:374
  141.0 2.8 %collective-permute-start.27 = (f32[448,128]{1,0:T(8,128)S(1)}, f32[448,128]{1,0:T(8,128)S(1)}, u32[]{:S(2)}, u32[]{:S(2)}) collective-permute-start(f32[448,128]{1,0:T(8,128)S(1)} %get-tuple-element.93), channel_id=1, source_target_pairs={{0,16},{8,24},{16,0},{24,8},{32,48},{40,56},{48,32},{56,40},{64,80... | collective-permute-start | bytes 688136 | tf_op jit(solution)/shard_map/ppermute | solution.py:374
  143.8 1.6 collective-permute-start.28
  147.4 3.4 %collective-permute-start.17 = (f32[448,128]{1,0:T(8,128)S(1)}, f32[448,128]{1,0:T(8,128)S(1)}, u32[]{:S(2)}, u32[]{:S(2)}) collective-permute-start(f32[448,128]{1,0:T(8,128)S(1)} %get-tuple-element.83), channel_id=1, source_target_pairs={{0,64},{8,72},{16,80},{24,88},{32,96},{40,104},{48,112},{56,120},{... | collective-permute-start | bytes 688136 | tf_op jit(solution)/shard_map/ppermute | solution.py:374
  153.7 2.2 collective-permute-start.29
  156.4 1.9 collective-permute-start.31
  159.1 1.9 collective-permute-start.19
  161.0 1.8 collective-permute-start.20
  162.8 1.8 collective-permute-done.29
  165.9 2.3 collective-permute-done.31
  168.2 2.1 collective-permute-done.20
  170.3 3.4 %collective-permute-done.21 = f32[448,128]{1,0:T(8,128)S(1)} collective-permute-done((f32[448,128]{1,0:T(8,128)S(1)}, f32[448,128]{1,0:T(8,128)S(1)}, u32[]{:S(2)}, u32[]{:S(2)}) %collective-permute-start.21) | collective-permute-done | bytes 229408 | tf_op jit(solution)/shard_map/ppermute | solution.py:374
  173.9 3.2 %collective-permute-start.43 = (f32[2,4,224,128]{3,2,1,0:T(8,128)S(1)}, f32[2,4,224,128]{3,2,1,0:T(8,128)S(1)}, u32[]{:S(2)}, u32[]{:S(2)}) collective-permute-start(f32[2,4,224,128]{3,2,1,0:T(8,128)S(1)} %pad_maximum_fusion.1.refs_5_), channel_id=1, source_target_pairs={{0,96},{8,104},{16,112},{24,120},{32,0},{40,8},{48,16},{56,24},{64... | collective-permute-start | bytes 2752520 | tf_op jit(solution)/shard_map/ppermute | solution.py:374
  178.8 3.5 %collective-permute-done.33 = f32[8,128]{1,0:T(8,128)S(1)} collective-permute-done((f32[8,128]{1,0:T(8,128)S(1)}, f32[8,128]{1,0:T(8,128)S(1)}, u32[]{:S(2)}, u32[]{:S(2)}) %collective-permute-start.33) | collective-permute-done | bytes 4128 | tf_op jit(solution)/shard_map/ppermute | solution.py:355
  182.4 3.2 %collective-permute-start.34 = (f32[8,128]{1,0:T(8,128)S(1)}, f32[8,128]{1,0:T(8,128)S(1)}, u32[]{:S(2)}, u32[]{:S(2)}) collective-permute-start(f32[8,128]{1,0:T(8,128)S(1)} %add.100), channel_id=1, source_target_pairs={{0,6},{1,7},{2,4},{3,5},{4,2},{5,3},{6,0},{7,1},{8,14},{9,15},{10,... | collective-permute-start | bytes 12296 | tf_op jit(solution)/shard_map/ppermute | solution.py:356
  185.6 4.3 %collective-permute-start.39 = (f32[2,4,224,128]{3,2,1,0:T(8,128)S(1)}, f32[2,4,224,128]{3,2,1,0:T(8,128)S(1)}, u32[]{:S(2)}, u32[]{:S(2)}) collective-permute-start(f32[2,4,224,128]{3,2,1,0:T(8,128)S(1)} %pad_maximum_fusion.refs_0_), channel_id=1, source_target_pairs={{0,24},{8,0},{16,8},{24,16},{32,56},{40,32},{48,40},{56,48},{64,88... | collective-permute-start | bytes 2752520 | tf_op jit(solution)/shard_map/ppermute | solution.py:374
  189.9 17.1 %collective-permute-done.35 = f32[8,128]{1,0:T(8,128)S(1)} collective-permute-done((f32[8,128]{1,0:T(8,128)S(1)}, f32[8,128]{1,0:T(8,128)S(1)}, u32[]{:S(2)}, u32[]{:S(2)}) %collective-permute-start.35) | collective-permute-done | bytes 4128 | tf_op jit(solution)/shard_map/ppermute | solution.py:364
  207.0 3.7 %collective-permute-start.36 = (f32[8,128]{1,0:T(8,128)S(1)}, f32[8,128]{1,0:T(8,128)S(1)}, u32[]{:S(2)}, u32[]{:S(2)}) collective-permute-start(f32[8,128]{1,0:T(8,128)S(1)} %add.102), channel_id=1, source_target_pairs={{0,24},{8,16},{16,8},{24,0},{32,56},{40,48},{48,40},{56,32},{64,88... | collective-permute-start | bytes 12296 | tf_op jit(solution)/shard_map/ppermute | solution.py:364
  210.8 3.3 %collective-permute-start.46 = (f32[4,224,128]{2,1,0:T(8,128)S(1)}, f32[4,224,128]{2,1,0:T(8,128)S(1)}, u32[]{:S(2)}, u32[]{:S(2)}) collective-permute-start(f32[4,224,128]{2,1,0:T(8,128)S(1)} %slice_bitcast_fusion), channel_id=1, source_target_pairs={{0,96},{8,104},{16,112},{24,120},{32,0},{40,8},{48,16},{56,24},{64... | collective-permute-start | bytes 1376264 | tf_op jit(solution)/shard_map/ppermute | solution.py:374
  214.2 1.9 collective-permute-start.41
  216.1 1.4 collective-permute-start.42
  217.7 3.6 %collective-permute-done.37 = f32[8,128]{1,0:T(8,128)S(1)} collective-permute-done((f32[8,128]{1,0:T(8,128)S(1)}, f32[8,128]{1,0:T(8,128)S(1)}, u32[]{:S(2)}, u32[]{:S(2)}) %collective-permute-start.37) | collective-permute-done | bytes 4128 | tf_op jit(solution)/shard_map/ppermute | solution.py:364
  222.7 3.4 %collective-permute-done.38 = f32[8,128]{1,0:T(8,128)S(1)} collective-permute-done((f32[8,128]{1,0:T(8,128)S(1)}, f32[8,128]{1,0:T(8,128)S(1)}, u32[]{:S(2)}, u32[]{:S(2)}) %collective-permute-start.38) | collective-permute-done | bytes 4128 | tf_op jit(solution)/shard_map/ppermute | solution.py:364
  226.2 7.7 %new_price.1 = (bf16[16,896,128]{2,1,0:T(8,128)(2,1)}, f32[1,1]{1,0:T(1,128)}) custom-call(s32[2,16]{1,0:T(2,128)S(1)} %pad_add_fusion.slots, f32[16,896,128]{2,1,0:T(8,128)S(1)} %get-tuple-element.75.roster_ref, bf16[16,896,128]{2,1,0:T(8,128)(2,1)} %price_ref.3, f32[8,128]{1,0:T(8,128)S(1)} %add.105.spread_ref, f32[1,256]{1,0:T(1,128)S(1)} %bitcast.36, ...), custom_call_target="tpu_custom_call" | custom-call | tf_op jit(solution)/shard_map/new_price/pallas_call | solution.py:656
  (122 shorter events, 30.4 us)
Async XLA Ops:
  4.8 25.7 %copy-start.1 = (bf16[16,128,128]{2,1,0:T(8,128)(2,1)S(1)}, bf16[16,128,128]{2,1,0:T(8,128)(2,1)}, u32[]{:S(2)}) copy-start(bf16[16,128,128]{2,1,0:T(8,128)(2,1)} %hess_ref.9) | copy-start | bytes 1572868
  17.8 1.4 collective-permute-start
  19.2 4.9 %collective-permute-start.1 = (f32[56,384]{1,0:T(8,128)S(1)}, f32[56,384]{1,0:T(8,128)S(1)}, u32[]{:S(2)}, u32[]{:S(2)}) collective-permute-start(f32[56,384]{1,0:T(8,128)S(1)} %add.84), channel_id=1, source_target_pairs={{0,2},{1,3},{2,0},{3,1},{4,6},{5,7},{6,4},{7,5},{8,10},{9,11},{10,... | collective-permute-start | bytes 258056 | tf_op jit(solution)/shard_map/ppermute | solution.py:355
  24.1 6.4 %collective-permute-start.2 = (f32[56,384]{1,0:T(8,128)S(1)}, f32[56,384]{1,0:T(8,128)S(1)}, u32[]{:S(2)}, u32[]{:S(2)}) collective-permute-start(f32[56,384]{1,0:T(8,128)S(1)} %add.85.use_a), channel_id=1, source_target_pairs={{0,6},{1,7},{2,4},{3,5},{4,2},{5,3},{6,0},{7,1},{8,14},{9,15},{10,... | collective-permute-start | bytes 258056 | tf_op jit(solution)/shard_map/ppermute | solution.py:356
  40.4 1.3 collective-permute-start.3
  41.8 4.4 %collective-permute-start.4 = (f32[48,384]{1,0:T(8,128)S(1)}, f32[48,384]{1,0:T(8,128)S(1)}, u32[]{:S(2)}, u32[]{:S(2)}) collective-permute-start(f32[48,384]{1,0:T(8,128)S(1)} %add.87), channel_id=1, source_target_pairs={{0,2},{1,3},{2,0},{3,1},{4,6},{5,7},{6,4},{7,5},{8,10},{9,11},{10,... | collective-permute-start | bytes 221192 | tf_op jit(solution)/shard_map/ppermute | solution.py:355
  46.2 5.6 %collective-permute-start.5 = (f32[48,384]{1,0:T(8,128)S(1)}, f32[48,384]{1,0:T(8,128)S(1)}, u32[]{:S(2)}, u32[]{:S(2)}) collective-permute-start(f32[48,384]{1,0:T(8,128)S(1)} %add.88.use_a), channel_id=1, source_target_pairs={{0,6},{1,7},{2,4},{3,5},{4,2},{5,3},{6,0},{7,1},{8,14},{9,15},{10,... | collective-permute-start | bytes 221192 | tf_op jit(solution)/shard_map/ppermute | solution.py:356
  61.7 1.3 collective-permute-start.6
  63.1 4.4 %collective-permute-start.7 = (f32[48,384]{1,0:T(8,128)S(1)}, f32[48,384]{1,0:T(8,128)S(1)}, u32[]{:S(2)}, u32[]{:S(2)}) collective-permute-start(f32[48,384]{1,0:T(8,128)S(1)} %add.89), channel_id=1, source_target_pairs={{0,2},{1,3},{2,0},{3,1},{4,6},{5,7},{6,4},{7,5},{8,10},{9,11},{10,... | collective-permute-start | bytes 221192 | tf_op jit(solution)/shard_map/ppermute | solution.py:355
  67.5 5.6 %collective-permute-start.8 = (f32[48,384]{1,0:T(8,128)S(1)}, f32[48,384]{1,0:T(8,128)S(1)}, u32[]{:S(2)}, u32[]{:S(2)}) collective-permute-start(f32[48,384]{1,0:T(8,128)S(1)} %add.90.use_a), channel_id=1, source_target_pairs={{0,6},{1,7},{2,4},{3,5},{4,2},{5,3},{6,0},{7,1},{8,14},{9,15},{10,... | collective-permute-start | bytes 221192 | tf_op jit(solution)/shard_map/ppermute | solution.py:356
  83.1 1.5 collective-permute-start.9
  84.6 4.4 %collective-permute-start.10 = (f32[48,384]{1,0:T(8,128)S(1)}, f32[48,384]{1,0:T(8,128)S(1)}, u32[]{:S(2)}, u32[]{:S(2)}) collective-permute-start(f32[48,384]{1,0:T(8,128)S(1)} %add.91), channel_id=1, source_target_pairs={{0,2},{1,3},{2,0},{3,1},{4,6},{5,7},{6,4},{7,5},{8,10},{9,11},{10,... | collective-permute-start | bytes 221192 | tf_op jit(solution)/shard_map/ppermute | solution.py:355
  89.0 5.6 %collective-permute-start.11 = (f32[48,384]{1,0:T(8,128)S(1)}, f32[48,384]{1,0:T(8,128)S(1)}, u32[]{:S(2)}, u32[]{:S(2)}) collective-permute-start(f32[48,384]{1,0:T(8,128)S(1)} %add.92.use_a), channel_id=1, source_target_pairs={{0,6},{1,7},{2,4},{3,5},{4,2},{5,3},{6,0},{7,1},{8,14},{9,15},{10,... | collective-permute-start | bytes 221192 | tf_op jit(solution)/shard_map/ppermute | solution.py:356
  105.1 11.8 %collective-permute-start.22 = (f32[4,224,128]{2,1,0:T(8,128)S(1)}, f32[4,224,128]{2,1,0:T(8,128)S(1)}, u32[]{:S(2)}, u32[]{:S(2)}) collective-permute-start(f32[4,224,128]{2,1,0:T(8,128)S(1)} %get-tuple-element.87), channel_id=1, source_target_pairs={{0,32},{8,40},{16,48},{24,56},{32,64},{40,72},{48,80},{56,88},{64,... | collective-permute-start | bytes 1376264 | tf_op jit(solution)/shard_map/ppermute | solution.py:374
  106.5 10.4 %collective-permute-start.23 = (f32[4,224,128]{2,1,0:T(8,128)S(1)}, f32[4,224,128]{2,1,0:T(8,128)S(1)}, u32[]{:S(2)}, u32[]{:S(2)}) collective-permute-start(f32[4,224,128]{2,1,0:T(8,128)S(1)} %get-tuple-element.88), channel_id=1, source_target_pairs={{0,96},{8,104},{16,112},{24,120},{32,0},{40,8},{48,16},{56,24},{64... | collective-permute-start | bytes 1376264 | tf_op jit(solution)/shard_map/ppermute | solution.py:374
  108.3 12.8 %collective-permute-start.12 = (f32[4,224,128]{2,1,0:T(8,128)S(1)}, f32[4,224,128]{2,1,0:T(8,128)S(1)}, u32[]{:S(2)}, u32[]{:S(2)}) collective-permute-start(f32[4,224,128]{2,1,0:T(8,128)S(1)} %get-tuple-element.77), channel_id=1, source_target_pairs={{0,8},{8,16},{16,24},{24,0},{32,40},{40,48},{48,56},{56,32},{64,72... | collective-permute-start | bytes 1376264 | tf_op jit(solution)/shard_map/ppermute | solution.py:374
  109.6 11.5 %collective-permute-start.13 = (f32[4,224,128]{2,1,0:T(8,128)S(1)}, f32[4,224,128]{2,1,0:T(8,128)S(1)}, u32[]{:S(2)}, u32[]{:S(2)}) collective-permute-start(f32[4,224,128]{2,1,0:T(8,128)S(1)} %get-tuple-element.78), channel_id=1, source_target_pairs={{0,24},{8,0},{16,8},{24,16},{32,56},{40,32},{48,40},{56,48},{64,88... | collective-permute-start | bytes 1376264 | tf_op jit(solution)/shard_map/ppermute | solution.py:374
  117.8 20.7 %collective-permute-start.24 = (f32[2,4,224,128]{3,2,1,0:T(8,128)S(1)}, f32[2,4,224,128]{3,2,1,0:T(8,128)S(1)}, u32[]{:S(2)}, u32[]{:S(2)}) collective-permute-start(f32[2,4,224,128]{3,2,1,0:T(8,128)S(1)} %get-tuple-element.89), channel_id=1, source_target_pairs={{0,32},{8,40},{16,48},{24,56},{32,64},{40,72},{48,80},{56,88},{64,... | collective-permute-start | bytes 2752520 | tf_op jit(solution)/shard_map/ppermute | solution.py:374
  119.2 19.3 %collective-permute-start.25 = (f32[2,4,224,128]{3,2,1,0:T(8,128)S(1)}, f32[2,4,224,128]{3,2,1,0:T(8,128)S(1)}, u32[]{:S(2)}, u32[]{:S(2)}) collective-permute-start(f32[2,4,224,128]{3,2,1,0:T(8,128)S(1)} %get-tuple-element.90), channel_id=1, source_target_pairs={{0,96},{8,104},{16,112},{24,120},{32,0},{40,8},{48,16},{56,24},{64... | collective-permute-start | bytes 2752520 | tf_op jit(solution)/shard_map/ppermute | solution.py:374
  122.1 23.2 %collective-permute-start.14 = (f32[2,4,224,128]{3,2,1,0:T(8,128)S(1)}, f32[2,4,224,128]{3,2,1,0:T(8,128)S(1)}, u32[]{:S(2)}, u32[]{:S(2)}) collective-permute-start(f32[2,4,224,128]{3,2,1,0:T(8,128)S(1)} %get-tuple-element.79), channel_id=1, source_target_pairs={{0,8},{8,16},{16,24},{24,0},{32,40},{40,48},{48,56},{56,32},{64,72... | collective-permute-start | bytes 2752520 | tf_op jit(solution)/shard_map/ppermute | solution.py:374
  123.4 22.3 %collective-permute-start.15 = (f32[2,4,224,128]{3,2,1,0:T(8,128)S(1)}, f32[2,4,224,128]{3,2,1,0:T(8,128)S(1)}, u32[]{:S(2)}, u32[]{:S(2)}) collective-permute-start(f32[2,4,224,128]{3,2,1,0:T(8,128)S(1)} %get-tuple-element.80), channel_id=1, source_target_pairs={{0,24},{8,0},{16,8},{24,16},{32,56},{40,32},{48,40},{56,48},{64,88... | collective-permute-start | bytes 2752520 | tf_op jit(solution)/shard_map/ppermute | solution.py:374
  139.6 11.1 %collective-permute-start.26 = (f32[448,128]{1,0:T(8,128)S(1)}, f32[448,128]{1,0:T(8,128)S(1)}, u32[]{:S(2)}, u32[]{:S(2)}) collective-permute-start(f32[448,128]{1,0:T(8,128)S(1)} %get-tuple-element.92), channel_id=1, source_target_pairs={{0,8},{8,16},{16,24},{24,0},{32,40},{40,48},{48,56},{56,32},{64,72... | collective-permute-start | bytes 688136 | tf_op jit(solution)/shard_map/ppermute | solution.py:374
  141.0 11.9 %collective-permute-start.27 = (f32[448,128]{1,0:T(8,128)S(1)}, f32[448,128]{1,0:T(8,128)S(1)}, u32[]{:S(2)}, u32[]{:S(2)}) collective-permute-start(f32[448,128]{1,0:T(8,128)S(1)} %get-tuple-element.93), channel_id=1, source_target_pairs={{0,16},{8,24},{16,0},{24,8},{32,48},{40,56},{48,32},{56,40},{64,80... | collective-permute-start | bytes 688136 | tf_op jit(solution)/shard_map/ppermute | solution.py:374
  143.8 9.2 %collective-permute-start.28 = (f32[448,128]{1,0:T(8,128)S(1)}, f32[448,128]{1,0:T(8,128)S(1)}, u32[]{:S(2)}, u32[]{:S(2)}) collective-permute-start(f32[448,128]{1,0:T(8,128)S(1)} %get-tuple-element.94), channel_id=1, source_target_pairs={{0,24},{8,0},{16,8},{24,16},{32,56},{40,32},{48,40},{56,48},{64,88... | collective-permute-start | bytes 688136 | tf_op jit(solution)/shard_map/ppermute | solution.py:374
  146.8 9.6 %collective-permute-start.16 = (f32[448,128]{1,0:T(8,128)S(1)}, f32[448,128]{1,0:T(8,128)S(1)}, u32[]{:S(2)}, u32[]{:S(2)}) collective-permute-start(f32[448,128]{1,0:T(8,128)S(1)} %get-tuple-element.82), channel_id=1, source_target_pairs={{0,32},{8,40},{16,48},{24,56},{32,64},{40,72},{48,80},{56,88},{64,... | collective-permute-start | bytes 688136 | tf_op jit(solution)/shard_map/ppermute | solution.py:374
  147.4 10.9 %collective-permute-start.17 = (f32[448,128]{1,0:T(8,128)S(1)}, f32[448,128]{1,0:T(8,128)S(1)}, u32[]{:S(2)}, u32[]{:S(2)}) collective-permute-start(f32[448,128]{1,0:T(8,128)S(1)} %get-tuple-element.83), channel_id=1, source_target_pairs={{0,64},{8,72},{16,80},{24,88},{32,96},{40,104},{48,112},{56,120},{... | collective-permute-start | bytes 688136 | tf_op jit(solution)/shard_map/ppermute | solution.py:374
  150.8 7.5 %collective-permute-start.18 = (f32[448,128]{1,0:T(8,128)S(1)}, f32[448,128]{1,0:T(8,128)S(1)}, u32[]{:S(2)}, u32[]{:S(2)}) collective-permute-start(f32[448,128]{1,0:T(8,128)S(1)} %get-tuple-element.84), channel_id=1, source_target_pairs={{0,96},{8,104},{16,112},{24,120},{32,0},{40,8},{48,16},{56,24},{64... | collective-permute-start | bytes 688136 | tf_op jit(solution)/shard_map/ppermute | solution.py:374
  153.7 10.8 %collective-permute-start.29 = (f32[448,128]{1,0:T(8,128)S(1)}, f32[448,128]{1,0:T(8,128)S(1)}, u32[]{:S(2)}, u32[]{:S(2)}) collective-permute-start(f32[448,128]{1,0:T(8,128)S(1)} %get-tuple-element.108), channel_id=1, source_target_pairs={{0,24},{8,0},{16,8},{24,16},{32,56},{40,32},{48,40},{56,48},{64,88... | collective-permute-start | bytes 688136 | tf_op jit(solution)/shard_map/ppermute | solution.py:374
  156.0 9.9 %collective-permute-start.30 = (f32[448,128]{1,0:T(8,128)S(1)}, f32[448,128]{1,0:T(8,128)S(1)}, u32[]{:S(2)}, u32[]{:S(2)}) collective-permute-start(f32[448,128]{1,0:T(8,128)S(1)} %get-tuple-element.108), channel_id=1, source_target_pairs={{0,16},{8,24},{16,0},{24,8},{32,48},{40,56},{48,32},{56,40},{64,80... | collective-permute-start | bytes 688136 | tf_op jit(solution)/shard_map/ppermute | solution.py:374
  156.4 11.8 %collective-permute-start.31 = (f32[448,128]{1,0:T(8,128)S(1)}, f32[448,128]{1,0:T(8,128)S(1)}, u32[]{:S(2)}, u32[]{:S(2)}) collective-permute-start(f32[448,128]{1,0:T(8,128)S(1)} %get-tuple-element.108), channel_id=1, source_target_pairs={{0,8},{8,16},{16,24},{24,0},{32,40},{40,48},{48,56},{56,32},{64,72... | collective-permute-start | bytes 688136 | tf_op jit(solution)/shard_map/ppermute | solution.py:374
  159.1 9.1 %collective-permute-start.19 = (f32[448,128]{1,0:T(8,128)S(1)}, f32[448,128]{1,0:T(8,128)S(1)}, u32[]{:S(2)}, u32[]{:S(2)}) collective-permute-start(f32[448,128]{1,0:T(8,128)S(1)} %get-tuple-element.104), channel_id=1, source_target_pairs={{0,96},{8,104},{16,112},{24,120},{32,0},{40,8},{48,16},{56,24},{64... | collective-permute-start | bytes 688136 | tf_op jit(solution)/shard_map/ppermute | solution.py:374
  161.0 9.3 %collective-permute-start.20 = (f32[448,128]{1,0:T(8,128)S(1)}, f32[448,128]{1,0:T(8,128)S(1)}, u32[]{:S(2)}, u32[]{:S(2)}) collective-permute-start(f32[448,128]{1,0:T(8,128)S(1)} %get-tuple-element.104), channel_id=1, source_target_pairs={{0,64},{8,72},{16,80},{24,88},{32,96},{40,104},{48,112},{56,120},{... | collective-permute-start | bytes 688136 | tf_op jit(solution)/shard_map/ppermute | solution.py:374
  164.6 9.2 %collective-permute-start.21 = (f32[448,128]{1,0:T(8,128)S(1)}, f32[448,128]{1,0:T(8,128)S(1)}, u32[]{:S(2)}, u32[]{:S(2)}) collective-permute-start(f32[448,128]{1,0:T(8,128)S(1)} %get-tuple-element.104), channel_id=1, source_target_pairs={{0,32},{8,40},{16,48},{24,56},{32,64},{40,72},{48,80},{56,88},{64,... | collective-permute-start | bytes 688136 | tf_op jit(solution)/shard_map/ppermute | solution.py:374
  173.8 36.9 %collective-permute-start.44 = (f32[2,4,224,128]{3,2,1,0:T(8,128)S(1)}, f32[2,4,224,128]{3,2,1,0:T(8,128)S(1)}, u32[]{:S(2)}, u32[]{:S(2)}) collective-permute-start(f32[2,4,224,128]{3,2,1,0:T(8,128)S(1)} %pad_maximum_fusion.1.refs_5_), channel_id=1, source_target_pairs={{0,32},{8,40},{16,48},{24,56},{32,64},{40,72},{48,80},{56,88},{64,... | collective-permute-start | bytes 2752520 | tf_op jit(solution)/shard_map/ppermute | solution.py:374
  173.9 36.9 %collective-permute-start.43 = (f32[2,4,224,128]{3,2,1,0:T(8,128)S(1)}, f32[2,4,224,128]{3,2,1,0:T(8,128)S(1)}, u32[]{:S(2)}, u32[]{:S(2)}) collective-permute-start(f32[2,4,224,128]{3,2,1,0:T(8,128)S(1)} %pad_maximum_fusion.1.refs_5_), channel_id=1, source_target_pairs={{0,96},{8,104},{16,112},{24,120},{32,0},{40,8},{48,16},{56,24},{64... | collective-permute-start | bytes 2752520 | tf_op jit(solution)/shard_map/ppermute | solution.py:374
  177.2 37.0 %collective-permute-start.40 = (f32[2,4,224,128]{3,2,1,0:T(8,128)S(1)}, f32[2,4,224,128]{3,2,1,0:T(8,128)S(1)}, u32[]{:S(2)}, u32[]{:S(2)}) collective-permute-start(f32[2,4,224,128]{3,2,1,0:T(8,128)S(1)} %pad_maximum_fusion.refs_0_), channel_id=1, source_target_pairs={{0,8},{8,16},{16,24},{24,0},{32,40},{40,48},{48,56},{56,32},{64,72... | collective-permute-start | bytes 2752520 | tf_op jit(solution)/shard_map/ppermute | solution.py:374
  177.6 1.2 collective-permute-start.32
  178.7 3.6 %collective-permute-start.33 = (f32[8,128]{1,0:T(8,128)S(1)}, f32[8,128]{1,0:T(8,128)S(1)}, u32[]{:S(2)}, u32[]{:S(2)}) collective-permute-start(f32[8,128]{1,0:T(8,128)S(1)} %add.99), channel_id=1, source_target_pairs={{0,2},{1,3},{2,0},{3,1},{4,6},{5,7},{6,4},{7,5},{8,10},{9,11},{10,... | collective-permute-start | bytes 12296 | tf_op jit(solution)/shard_map/ppermute | solution.py:355
  182.4 7.5 %collective-permute-start.34 = (f32[8,128]{1,0:T(8,128)S(1)}, f32[8,128]{1,0:T(8,128)S(1)}, u32[]{:S(2)}, u32[]{:S(2)}) collective-permute-start(f32[8,128]{1,0:T(8,128)S(1)} %add.100), channel_id=1, source_target_pairs={{0,6},{1,7},{2,4},{3,5},{4,2},{5,3},{6,0},{7,1},{8,14},{9,15},{10,... | collective-permute-start | bytes 12296 | tf_op jit(solution)/shard_map/ppermute | solution.py:356
  185.6 30.5 %collective-permute-start.39 = (f32[2,4,224,128]{3,2,1,0:T(8,128)S(1)}, f32[2,4,224,128]{3,2,1,0:T(8,128)S(1)}, u32[]{:S(2)}, u32[]{:S(2)}) collective-permute-start(f32[2,4,224,128]{3,2,1,0:T(8,128)S(1)} %pad_maximum_fusion.refs_0_), channel_id=1, source_target_pairs={{0,24},{8,0},{16,8},{24,16},{32,56},{40,32},{48,40},{56,48},{64,88... | collective-permute-start | bytes 2752520 | tf_op jit(solution)/shard_map/ppermute | solution.py:374
  189.8 17.1 %collective-permute-start.35 = (f32[8,128]{1,0:T(8,128)S(1)}, f32[8,128]{1,0:T(8,128)S(1)}, u32[]{:S(2)}, u32[]{:S(2)}) collective-permute-start(f32[8,128]{1,0:T(8,128)S(1)} %add.101), channel_id=1, source_target_pairs={{0,8},{8,0},{16,24},{24,16},{32,40},{40,32},{48,56},{56,48},{64,72... | collective-permute-start | bytes 12296 | tf_op jit(solution)/shard_map/ppermute | solution.py:364
  207.0 10.6 %collective-permute-start.36 = (f32[8,128]{1,0:T(8,128)S(1)}, f32[8,128]{1,0:T(8,128)S(1)}, u32[]{:S(2)}, u32[]{:S(2)}) collective-permute-start(f32[8,128]{1,0:T(8,128)S(1)} %add.102), channel_id=1, source_target_pairs={{0,24},{8,16},{16,8},{24,0},{32,56},{40,48},{48,40},{56,32},{64,88... | collective-permute-start | bytes 12296 | tf_op jit(solution)/shard_map/ppermute | solution.py:364
  210.7 15.4 %collective-permute-start.45 = (f32[4,224,128]{2,1,0:T(8,128)S(1)}, f32[4,224,128]{2,1,0:T(8,128)S(1)}, u32[]{:S(2)}, u32[]{:S(2)}) collective-permute-start(f32[4,224,128]{2,1,0:T(8,128)S(1)} %slice_bitcast_fusion.1), channel_id=1, source_target_pairs={{0,32},{8,40},{16,48},{24,56},{32,64},{40,72},{48,80},{56,88},{64,... | collective-permute-start | bytes 1376264 | tf_op jit(solution)/shard_map/ppermute | solution.py:374
  210.8 15.3 %collective-permute-start.46 = (f32[4,224,128]{2,1,0:T(8,128)S(1)}, f32[4,224,128]{2,1,0:T(8,128)S(1)}, u32[]{:S(2)}, u32[]{:S(2)}) collective-permute-start(f32[4,224,128]{2,1,0:T(8,128)S(1)} %slice_bitcast_fusion), channel_id=1, source_target_pairs={{0,96},{8,104},{16,112},{24,120},{32,0},{40,8},{48,16},{56,24},{64... | collective-permute-start | bytes 1376264 | tf_op jit(solution)/shard_map/ppermute | solution.py:374
  214.2 12.0 %collective-permute-start.41 = (f32[4,224,128]{2,1,0:T(8,128)S(1)}, f32[4,224,128]{2,1,0:T(8,128)S(1)}, u32[]{:S(2)}, u32[]{:S(2)}) collective-permute-start(f32[4,224,128]{2,1,0:T(8,128)S(1)} %slice_bitcast_fusion.3), channel_id=1, source_target_pairs={{0,8},{8,16},{16,24},{24,0},{32,40},{40,48},{48,56},{56,32},{64,72... | collective-permute-start | bytes 1376264 | tf_op jit(solution)/shard_map/ppermute | solution.py:374
  216.1 10.0 %collective-permute-start.42 = (f32[4,224,128]{2,1,0:T(8,128)S(1)}, f32[4,224,128]{2,1,0:T(8,128)S(1)}, u32[]{:S(2)}, u32[]{:S(2)}) collective-permute-start(f32[4,224,128]{2,1,0:T(8,128)S(1)} %slice_bitcast_fusion.2), channel_id=1, source_target_pairs={{0,24},{8,0},{16,8},{24,16},{32,56},{40,32},{48,40},{56,48},{64,88... | collective-permute-start | bytes 1376264 | tf_op jit(solution)/shard_map/ppermute | solution.py:374
  217.6 3.7 %collective-permute-start.37 = (f32[8,128]{1,0:T(8,128)S(1)}, f32[8,128]{1,0:T(8,128)S(1)}, u32[]{:S(2)}, u32[]{:S(2)}) collective-permute-start(f32[8,128]{1,0:T(8,128)S(1)} %add.103), channel_id=1, source_target_pairs={{0,32},{8,40},{16,48},{24,56},{32,0},{40,8},{48,16},{56,24},{64,96... | collective-permute-start | bytes 12296 | tf_op jit(solution)/shard_map/ppermute | solution.py:364
  221.3 4.8 %collective-permute-start.38 = (f32[8,128]{1,0:T(8,128)S(1)}, f32[8,128]{1,0:T(8,128)S(1)}, u32[]{:S(2)}, u32[]{:S(2)}) collective-permute-start(f32[8,128]{1,0:T(8,128)S(1)} %add.104), channel_id=1, source_target_pairs={{0,96},{8,104},{16,112},{24,120},{32,64},{40,72},{48,80},{56,88},{... | collective-permute-start | bytes 12296 | tf_op jit(solution)/shard_map/ppermute | solution.py:364
  (8 other events, 101.2 us)

commit v3 on v2

--- a/solution.py
+++ b/solution.py
@@ -356,9 +356,7 @@
     return value, lax.ppermute(value, "veh", veh_pairs(PAIR_B))
 
 
-def sum_everywhere(value):
-    a, b = usage_exchange(value)
-    value = a + b
+def sum_over_scen(value):
     for axis in ("x", "y"):
         for pair in (PAIR_A, PAIR_B):
             value = value + lax.ppermute(value, "scen", scen_pairs(pair, axis))
@@ -401,11 +399,13 @@
     return {0: own, **{by: shift(own, second, -by) for by in (1, 3, 2)}}
 
 
-def gather_half(row, first):
+def gather_near(row, first):
     rows = row[0].shape[0] // 2
     pack = jnp.stack([row[k].reshape(2, rows, -1) for k in range(4)], axis=1)
-    third = shift(pack, first, 1)
-    one = shift(pack, first, -1)
+    return pack, shift(pack, first, -1), shift(pack, first, 1)
+
+
+def gather_far(pack, one, third, first):
     two_low = shift(third[0], first, 1)
     two_high = shift(one[1], first, -1)
     return [pack, one, third, two_low, two_high]
@@ -489,8 +489,8 @@
         in_hbm(price),
         in_hbm(anchor),
         in_hbm(anchor),
-        hessian,
-        usage_coef,
+        in_hbm(hessian),
+        in_hbm(usage_coef),
         dual,
         crew_row[None, :],
     )
@@ -647,9 +647,13 @@
     spreads += [m[1] for m in moved]
     own_a, own_b = moved[0][0], moved[1][0]
     row_a, row_b = gather_row(own_a, "y"), gather_row(own_b, "x")
-    row_a, row_b, spread = lax.optimization_barrier((row_a, row_b, sum(spreads)))
-    means = gather_half(row_a, "x") + gather_half(row_b, "y")
-    spread_total = sum_everywhere(spread)
+    row_a[1], row_b[1], spread = lax.optimization_barrier((row_a[1], row_b[1], sum(spreads)))
+    spread = sum(usage_exchange(spread))
+    row_a, row_b, spread = lax.optimization_barrier((row_a, row_b, spread))
+    near_a, near_b = gather_near(row_a, "x"), gather_near(row_b, "y")
+    near_b, spread = lax.optimization_barrier((near_b, spread))
+    spread_total = sum_over_scen(spread)
+    means = gather_far(*near_a, "x") + gather_far(*near_b, "y")
     entries = vehicles * lax.axis_size("veh") * n
 
     each = 2

time: 235 us -> 232 us (0.987)
  starting transfers between devices: 71.3 us -> 76.8 us
  waiting for transfers between devices: 88.9 us -> 83.5 us
    ppermute x4, waiting for transfers between devices: 24.1 us -> 9.54 us  [sum_over_scen(): value = value + lax.ppermute(value, 'scen', scen_pairs(pair, axis))]
    ppermute x28, waiting for transfers between devices: 30.6 us -> 38.3 us  [shift(): return lax.ppermute(value, 'scen', pairs)]
    ppermute x28, starting transfers between devices: 46.8 us -> 51.2 us  [shift(): return lax.ppermute(value, 'scen', pairs)]
where the time goes in v3:
time: 232 us; the launch traced here: 233 us
  waiting for transfers between devices  83.5 us (36%)
  starting transfers between devices  76.8 us (33%)
  Pallas kernels  66.9 us (29%)
  local copies, waits for them, and re-layouts  2.47 us (1%)
    ppermute x28, starting transfers between devices, shift(): return lax.ppermute(value, 'scen', pairs)  51.2 us
    ppermute x28, waiting for transfers between devices, shift(): return lax.ppermute(value, 'scen', pairs)  38.3 us
    pallas_call x3, Pallas kernels, shards(): pl.pallas_call(middle_kernel, in_specs=[vm] * 10, out_specs=[vm] * 3, out...  29.7 us
    ppermute x5, waiting for transfers between devices, usage_exchange(): value = value + lax.ppermute(value, 'veh', veh_pairs(PAIR_A))  19.1 us
    ppermute x5, starting transfers between devices, usage_exchange(): return (value, lax.ppermute(value, 'veh', veh_pairs(PAIR_B)))  17.1 us
    pallas_call x1, Pallas kernels, shards(): pl.pallas_call(first_kernel, grid_spec=pltpu.PrefetchScalarGridSpec(num_s...  13.3 us
    ppermute x5, waiting for transfers between devices, usage_exchange(): return (value, lax.ppermute(value, 'veh', veh_pairs(PAIR_B)))  10.6 us
    pallas_call x1, Pallas kernels, shards(): pl.pallas_call(last_kernel, grid_spec=pltpu.PrefetchScalarGridSpec(num_sc...  10.4 us
  transfers between devices with their start and end apart: 47, of which 26 were waited for; matrix products, arithmetic and copies ran while one was open for 1% of the time, Pallas kernels for 2%

profile of v3, /device:TPU:0, one launch (start us, length us, event | category | flops | bytes accessed | tf_op | source)
XLA Modules:
  0.0 232.5 jit_solution(12085148336681699433)
XLA Ops:
  2.8 13.3 %first_steps.1 = (f32[16,128,896]{2,1,0:T(8,128)S(1)}, f32[16,128,896]{2,1,0:T(8,128)S(1)}, f32[128,896]{1,0:T(8,128)S(1)}, bf16[384,896]{1,0:T(8,128)(2,1)S(1)}, f32[56,384]{1,0:T(8,128)S(1)}) custom-call(s32[16]{0:T(128)S(1)} %dynamic-slice_bitcast_fusion.bundles, bf16[16,896,128]{2,1,0:T(8,128)(2,1)} %start_ref.1, bf16[16,896,128]{2,1,0:T(8,128)(2,1)} %cost_ref.1, ...), custom_call_target="tpu_custom_call" | custom-call | tf_op jit(solution)/shard_map/first_steps/pallas_call | solution.py:453
  17.5 2.1 collective-permute-start.1
  19.7 2.7 %collective-permute-done.1 = f32[56,384]{1,0:T(8,128)S(1)} collective-permute-done((f32[56,384]{1,0:T(8,128)S(1)}, f32[56,384]{1,0:T(8,128)S(1)}, u32[]{:S(2)}, u32[]{:S(2)}) %collective-permute-start.1) | collective-permute-done | bytes 86048 | tf_op jit(solution)/shard_map/ppermute | solution.py:355
  22.5 3.9 %collective-permute-start.2 = (f32[56,384]{1,0:T(8,128)S(1)}, f32[56,384]{1,0:T(8,128)S(1)}, u32[]{:S(2)}, u32[]{:S(2)}) collective-permute-start(f32[56,384]{1,0:T(8,128)S(1)} %add.85.use_a), channel_id=1, source_target_pairs={{0,6},{1,7},{2,4},{3,5},{4,2},{5,3},{6,0},{7,1},{8,14},{9,15},{10,... | collective-permute-start | bytes 258056 | tf_op jit(solution)/shard_map/ppermute | solution.py:356
  26.6 2.3 collective-permute-done.2.use_b
  28.9 9.9 %three_steps.3 = (f32[16,128,896]{2,1,0:T(8,128)S(1)}, f32[48,384]{1,0:T(8,128)S(1)}, f32[16,384]{1,0:T(8,128)S(1)}) custom-call(f32[16,128,896]{2,1,0:T(8,128)S(1)} %get-tuple-element.67.partial_ref, f32[16,128,896]{2,1,0:T(8,128)S(1)} %get-tuple-element.68.linear_ref, bf16[16,128,128]{2,1,0:T(8,128)(2,1)S(1)} %copy-done, ...), custom_call_target="tpu_custom_call", output_to_operand_aliasing={{0}: (0, {})} | custom-call | tf_op jit(solution)/shard_map/three_steps/pallas_call | solution.py:501
  40.3 4.3 %collective-permute-done.4 = f32[48,384]{1,0:T(8,128)S(1)} collective-permute-done((f32[48,384]{1,0:T(8,128)S(1)}, f32[48,384]{1,0:T(8,128)S(1)}, u32[]{:S(2)}, u32[]{:S(2)}) %collective-permute-start.4) | collective-permute-done | bytes 73760 | tf_op jit(solution)/shard_map/ppermute | solution.py:355
  44.6 3.3 %collective-permute-start.5 = (f32[48,384]{1,0:T(8,128)S(1)}, f32[48,384]{1,0:T(8,128)S(1)}, u32[]{:S(2)}, u32[]{:S(2)}) collective-permute-start(f32[48,384]{1,0:T(8,128)S(1)} %add.88.use_a), channel_id=1, source_target_pairs={{0,6},{1,7},{2,4},{3,5},{4,2},{5,3},{6,0},{7,1},{8,14},{9,15},{10,... | collective-permute-start | bytes 221192 | tf_op jit(solution)/shard_map/ppermute | solution.py:356
  48.0 2.2 collective-permute-done.5.use_b
  50.3 9.9 %three_steps.4 = (f32[16,128,896]{2,1,0:T(8,128)S(1)}, f32[48,384]{1,0:T(8,128)S(1)}, f32[16,384]{1,0:T(8,128)S(1)}) custom-call(f32[16,128,896]{2,1,0:T(8,128)S(1)} %get-tuple-element.72.partial_ref, f32[16,128,896]{2,1,0:T(8,128)S(1)} %get-tuple-element.68.linear_ref, bf16[16,128,128]{2,1,0:T(8,128)(2,1)S(1)} %copy-done, ...), custom_call_target="tpu_custom_call", output_to_operand_aliasing={{0}: (0, {})} | custom-call | tf_op jit(solution)/shard_map/three_steps/pallas_call | solution.py:501
  61.7 4.2 %collective-permute-done.7 = f32[48,384]{1,0:T(8,128)S(1)} collective-permute-done((f32[48,384]{1,0:T(8,128)S(1)}, f32[48,384]{1,0:T(8,128)S(1)}, u32[]{:S(2)}, u32[]{:S(2)}) %collective-permute-start.7) | collective-permute-done | bytes 73760 | tf_op jit(solution)/shard_map/ppermute | solution.py:355
  66.0 3.3 %collective-permute-start.8 = (f32[48,384]{1,0:T(8,128)S(1)}, f32[48,384]{1,0:T(8,128)S(1)}, u32[]{:S(2)}, u32[]{:S(2)}) collective-permute-start(f32[48,384]{1,0:T(8,128)S(1)} %add.90.use_a), channel_id=1, source_target_pairs={{0,6},{1,7},{2,4},{3,5},{4,2},{5,3},{6,0},{7,1},{8,14},{9,15},{10,... | collective-permute-start | bytes 221192 | tf_op jit(solution)/shard_map/ppermute | solution.py:356
  69.4 2.2 collective-permute-done.8.use_b
  71.6 9.9 %three_steps.5 = (f32[16,128,896]{2,1,0:T(8,128)S(1)}, f32[48,384]{1,0:T(8,128)S(1)}, f32[16,384]{1,0:T(8,128)S(1)}) custom-call(f32[16,128,896]{2,1,0:T(8,128)S(1)} %get-tuple-element.75.partial_ref, f32[16,128,896]{2,1,0:T(8,128)S(1)} %get-tuple-element.68.linear_ref, bf16[16,128,128]{2,1,0:T(8,128)(2,1)S(1)} %copy-done, ...), custom_call_target="tpu_custom_call", output_to_operand_aliasing={{0}: (0, {})} | custom-call | tf_op jit(solution)/shard_map/three_steps/pallas_call | solution.py:501
  83.2 4.3 %collective-permute-done.10 = f32[48,384]{1,0:T(8,128)S(1)} collective-permute-done((f32[48,384]{1,0:T(8,128)S(1)}, f32[48,384]{1,0:T(8,128)S(1)}, u32[]{:S(2)}, u32[]{:S(2)}) %collective-permute-start.10) | collective-permute-done | bytes 73760 | tf_op jit(solution)/shard_map/ppermute | solution.py:355
  87.5 3.3 %collective-permute-start.11 = (f32[48,384]{1,0:T(8,128)S(1)}, f32[48,384]{1,0:T(8,128)S(1)}, u32[]{:S(2)}, u32[]{:S(2)}) collective-permute-start(f32[48,384]{1,0:T(8,128)S(1)} %add.92.use_a), channel_id=1, source_target_pairs={{0,6},{1,7},{2,4},{3,5},{4,2},{5,3},{6,0},{7,1},{8,14},{9,15},{10,... | collective-permute-start | bytes 221192 | tf_op jit(solution)/shard_map/ppermute | solution.py:356
  90.8 2.3 %collective-permute-done.11.use_b = f32[48,384]{1,0:T(8,128)S(1)} collective-permute-done((f32[48,384]{1,0:T(8,128)S(1)}, f32[48,384]{1,0:T(8,128)S(1)}, u32[]{:S(2)}, u32[]{:S(2)}) %collective-permute-start.11) | collective-permute-done | bytes 73760 | tf_op jit(solution)/shard_map/ppermute | solution.py:356
  93.1 10.4 %last_step.1 = (bf16[16,896,128]{2,1,0:T(8,128)(2,1)}, f32[16,896,128]{2,1,0:T(8,128)S(1)}, f32[16,448,128]{2,1,0:T(8,128)S(1)}, f32[16,448,128]{2,1,0:T(8,128)S...) custom-call(s32[2,16]{1,0:T(2,128)S(1)} %pad_add_fusion.slots, ...), custom_call_target="tpu_custom_call" | custom-call | tf_op jit(solution)/shard_map/last_step/pallas_call | solution.py:562
  103.6 1.6 collective-permute-start.20
  105.2 1.6 collective-permute-start.21
  108.2 1.9 collective-permute-start.13
  110.3 5.1 %collective-permute-done.20.up_in = f32[4,224,128]{2,1,0:T(8,128)S(1)} collective-permute-done((f32[4,224,128]{2,1,0:T(8,128)S(1)}, f32[4,224,128]{2,1,0:T(8,128)S(1)}, u32[]{:S(2)}, u32[]{:S(2)}) %collective-permute-start.20) | collective-permute-done | bytes 458784 | tf_op jit(solution)/shard_map/ppermute | solution.py:372
  116.4 1.5 collective-permute-start.22
  117.9 1.8 collective-permute-start.23
  120.7 1.5 collective-permute-start.14
  122.2 1.8 collective-permute-start.15
  124.0 13.1 %collective-permute-done.22.up_in = f32[2,4,224,128]{3,2,1,0:T(8,128)S(1)} collective-permute-done((f32[2,4,224,128]{3,2,1,0:T(8,128)S(1)}, f32[2,4,224,128]{3,2,1,0:T(8,128)S(1)}, u32[]{:S(2)}, u32[]{:S(2)}) %collective-permute-start.22) | collective-permute-done | bytes 917536 | tf_op jit(solution)/shard_map/ppermute | solution.py:372
  139.6 3.2 %collective-permute-start.25 = (f32[448,128]{1,0:T(8,128)S(1)}, f32[448,128]{1,0:T(8,128)S(1)}, u32[]{:S(2)}, u32[]{:S(2)}) collective-permute-start(f32[448,128]{1,0:T(8,128)S(1)} %get-tuple-element.100), channel_id=1, source_target_pairs={{0,16},{8,24},{16,0},{24,8},{32,48},{40,56},{48,32},{56,40},{64,80... | collective-permute-start | bytes 688136 | tf_op jit(solution)/shard_map/ppermute | solution.py:372
  146.3 3.5 %collective-permute-start.17 = (f32[448,128]{1,0:T(8,128)S(1)}, f32[448,128]{1,0:T(8,128)S(1)}, u32[]{:S(2)}, u32[]{:S(2)}) collective-permute-start(f32[448,128]{1,0:T(8,128)S(1)} %get-tuple-element.90), channel_id=1, source_target_pairs={{0,64},{8,72},{16,80},{24,88},{32,96},{40,104},{48,112},{56,120},{... | collective-permute-start | bytes 688136 | tf_op jit(solution)/shard_map/ppermute | solution.py:372
  152.8 1.9 collective-permute-start.27
  154.7 1.5 collective-permute-done.17.in_2
  157.1 2.5 %collective-permute-start.19 = (f32[448,128]{1,0:T(8,128)S(1)}, f32[448,128]{1,0:T(8,128)S(1)}, u32[]{:S(2)}, u32[]{:S(2)}) collective-permute-start(f32[448,128]{1,0:T(8,128)S(1)} %get-tuple-element.119), channel_id=1, source_target_pairs={{0,96},{8,104},{16,112},{24,120},{32,0},{40,8},{48,16},{56,24},{64... | collective-permute-start | bytes 688136 | tf_op jit(solution)/shard_map/ppermute | solution.py:372
  159.6 4.6 %collective-permute-start.30 = (f32[448,128]{1,0:T(8,128)S(1)}, f32[448,128]{1,0:T(8,128)S(1)}, u32[]{:S(2)}, u32[]{:S(2)}) collective-permute-start(f32[448,128]{1,0:T(8,128)S(1)} %get-tuple-element.113), channel_id=1, source_target_pairs={{0,16},{8,24},{16,0},{24,8},{32,48},{40,56},{48,32},{56,40},{64,80... | collective-permute-start | bytes 688136 | tf_op jit(solution)/shard_map/ppermute | solution.py:372
  164.1 1.7 collective-permute-start.31
  168.2 3.5 %collective-permute-done.33 = f32[8,128]{1,0:T(8,128)S(1)} collective-permute-done((f32[8,128]{1,0:T(8,128)S(1)}, f32[8,128]{1,0:T(8,128)S(1)}, u32[]{:S(2)}, u32[]{:S(2)}) %collective-permute-start.33) | collective-permute-done | bytes 4128 | tf_op jit(solution)/shard_map/ppermute | solution.py:355
  171.7 3.3 %collective-permute-start.34 = (f32[8,128]{1,0:T(8,128)S(1)}, f32[8,128]{1,0:T(8,128)S(1)}, u32[]{:S(2)}, u32[]{:S(2)}) collective-permute-start(f32[8,128]{1,0:T(8,128)S(1)} %add.100), channel_id=1, source_target_pairs={{0,6},{1,7},{2,4},{3,5},{4,2},{5,3},{6,0},{7,1},{8,14},{9,15},{10,... | collective-permute-start | bytes 12296 | tf_op jit(solution)/shard_map/ppermute | solution.py:356
  175.0 1.6 collective-permute-done.34
  176.7 4.2 %collective-permute-start.42 = (f32[2,4,224,128]{3,2,1,0:T(8,128)S(1)}, f32[2,4,224,128]{3,2,1,0:T(8,128)S(1)}, u32[]{:S(2)}, u32[]{:S(2)}) collective-permute-start(f32[2,4,224,128]{3,2,1,0:T(8,128)S(1)} %pad_maximum_fusion.1.refs_0_), channel_id=1, source_target_pairs={{0,8},{8,16},{16,24},{24,0},{32,40},{40,48},{48,56},{56,32},{64,72... | collective-permute-start | bytes 2752520 | tf_op jit(solution)/shard_map/ppermute | solution.py:372
  180.9 3.7 %collective-permute-start.35 = (f32[2,4,224,128]{3,2,1,0:T(8,128)S(1)}, f32[2,4,224,128]{3,2,1,0:T(8,128)S(1)}, u32[]{:S(2)}, u32[]{:S(2)}) collective-permute-start(f32[2,4,224,128]{3,2,1,0:T(8,128)S(1)} %pad_maximum_fusion.refs_5_), channel_id=1, source_target_pairs={{0,96},{8,104},{16,112},{24,120},{32,0},{40,8},{48,16},{56,24},{64... | collective-permute-start | bytes 2752520 | tf_op jit(solution)/shard_map/ppermute | solution.py:372
  184.7 14.5 %collective-permute-done.42.refs_2_ = f32[2,4,224,128]{3,2,1,0:T(8,128)S(1)} collective-permute-done((f32[2,4,224,128]{3,2,1,0:T(8,128)S(1)}, f32[2,4,224,128]{3,2,1,0:T(8,128)S(1)}, u32[]{:S(2)}, u32[]{:S(2)}) %collective-permute-start.42) | collective-permute-done | bytes 917536 | tf_op jit(solution)/shard_map/ppermute | solution.py:372
  199.2 2.4 %collective-permute-start.43 = (f32[4,224,128]{2,1,0:T(8,128)S(1)}, f32[4,224,128]{2,1,0:T(8,128)S(1)}, u32[]{:S(2)}, u32[]{:S(2)}) collective-permute-start(f32[4,224,128]{2,1,0:T(8,128)S(1)} %slice_bitcast_fusion.1), channel_id=1, source_target_pairs={{0,8},{8,16},{16,24},{24,0},{32,40},{40,48},{48,56},{56,32},{64,72... | collective-permute-start | bytes 1376264 | tf_op jit(solution)/shard_map/ppermute | solution.py:372
  202.9 2.8 %collective-permute-done.36.refs_7_ = f32[2,4,224,128]{3,2,1,0:T(8,128)S(1)} collective-permute-done((f32[2,4,224,128]{3,2,1,0:T(8,128)S(1)}, f32[2,4,224,128]{3,2,1,0:T(8,128)S(1)}, u32[]{:S(2)}, u32[]{:S(2)}) %collective-permute-start.36) | collective-permute-done | bytes 917536 | tf_op jit(solution)/shard_map/ppermute | solution.py:372
  205.8 1.8 collective-permute-start.37
  207.7 3.2 %collective-permute-start.46 = (f32[4,224,128]{2,1,0:T(8,128)S(1)}, f32[4,224,128]{2,1,0:T(8,128)S(1)}, u32[]{:S(2)}, u32[]{:S(2)}) collective-permute-start(f32[4,224,128]{2,1,0:T(8,128)S(1)} %slice_bitcast_fusion.2), channel_id=1, source_target_pairs={{0,96},{8,104},{16,112},{24,120},{32,0},{40,8},{48,16},{56,24},{64... | collective-permute-start | bytes 1376264 | tf_op jit(solution)/shard_map/ppermute | solution.py:372
  211.9 4.5 %collective-permute-done.38 = f32[8,128]{1,0:T(8,128)S(1)} collective-permute-done((f32[8,128]{1,0:T(8,128)S(1)}, f32[8,128]{1,0:T(8,128)S(1)}, u32[]{:S(2)}, u32[]{:S(2)}) %collective-permute-start.38) | collective-permute-done | bytes 4128 | tf_op jit(solution)/shard_map/ppermute | solution.py:362
  216.6 3.4 %collective-permute-done.39 = f32[8,128]{1,0:T(8,128)S(1)} collective-permute-done((f32[8,128]{1,0:T(8,128)S(1)}, f32[8,128]{1,0:T(8,128)S(1)}, u32[]{:S(2)}, u32[]{:S(2)}) %collective-permute-start.39) | collective-permute-done | bytes 4128 | tf_op jit(solution)/shard_map/ppermute | solution.py:362
  220.0 3.1 %collective-permute-start.40 = (f32[8,128]{1,0:T(8,128)S(1)}, f32[8,128]{1,0:T(8,128)S(1)}, u32[]{:S(2)}, u32[]{:S(2)}) collective-permute-start(f32[8,128]{1,0:T(8,128)S(1)} %add.104), channel_id=1, source_target_pairs={{0,96},{8,104},{16,112},{24,120},{32,64},{40,72},{48,80},{56,88},{... | collective-permute-start | bytes 12296 | tf_op jit(solution)/shard_map/ppermute | solution.py:362
  224.8 7.7 %new_price.1 = (bf16[16,896,128]{2,1,0:T(8,128)(2,1)}, f32[1,1]{1,0:T(1,128)}) custom-call(s32[2,16]{1,0:T(2,128)S(1)} %pad_add_fusion.slots, f32[16,896,128]{2,1,0:T(8,128)S(1)} %get-tuple-element.82.roster_ref, bf16[16,896,128]{2,1,0:T(8,128)(2,1)} %price_ref.3, f32[8,128]{1,0:T(8,128)S(1)} %add.105.spread_ref, f32[1,256]{1,0:T(1,128)S(1)} %bitcast.36, ...), custom_call_target="tpu_custom_call" | custom-call | tf_op jit(solution)/shard_map/new_price/pallas_call | solution.py:660
  (118 shorter events, 29.0 us)
Async XLA Ops:
  2.8 26.1 %copy-start = (bf16[16,128,128]{2,1,0:T(8,128)(2,1)S(1)}, bf16[16,128,128]{2,1,0:T(8,128)(2,1)}, u32[]{:S(2)}) copy-start(bf16[16,128,128]{2,1,0:T(8,128)(2,1)} %hess_ref.9) | copy-start | bytes 1572868
  16.2 1.4 collective-permute-start
  17.5 4.9 %collective-permute-start.1 = (f32[56,384]{1,0:T(8,128)S(1)}, f32[56,384]{1,0:T(8,128)S(1)}, u32[]{:S(2)}, u32[]{:S(2)}) collective-permute-start(f32[56,384]{1,0:T(8,128)S(1)} %add.84), channel_id=1, source_target_pairs={{0,2},{1,3},{2,0},{3,1},{4,6},{5,7},{6,4},{7,5},{8,10},{9,11},{10,... | collective-permute-start | bytes 258056 | tf_op jit(solution)/shard_map/ppermute | solution.py:355
  22.5 6.4 %collective-permute-start.2 = (f32[56,384]{1,0:T(8,128)S(1)}, f32[56,384]{1,0:T(8,128)S(1)}, u32[]{:S(2)}, u32[]{:S(2)}) collective-permute-start(f32[56,384]{1,0:T(8,128)S(1)} %add.85.use_a), channel_id=1, source_target_pairs={{0,6},{1,7},{2,4},{3,5},{4,2},{5,3},{6,0},{7,1},{8,14},{9,15},{10,... | collective-permute-start | bytes 258056 | tf_op jit(solution)/shard_map/ppermute | solution.py:356
  38.8 1.3 collective-permute-start.3
  40.2 4.4 %collective-permute-start.4 = (f32[48,384]{1,0:T(8,128)S(1)}, f32[48,384]{1,0:T(8,128)S(1)}, u32[]{:S(2)}, u32[]{:S(2)}) collective-permute-start(f32[48,384]{1,0:T(8,128)S(1)} %add.87), channel_id=1, source_target_pairs={{0,2},{1,3},{2,0},{3,1},{4,6},{5,7},{6,4},{7,5},{8,10},{9,11},{10,... | collective-permute-start | bytes 221192 | tf_op jit(solution)/shard_map/ppermute | solution.py:355
  44.6 5.6 %collective-permute-start.5 = (f32[48,384]{1,0:T(8,128)S(1)}, f32[48,384]{1,0:T(8,128)S(1)}, u32[]{:S(2)}, u32[]{:S(2)}) collective-permute-start(f32[48,384]{1,0:T(8,128)S(1)} %add.88.use_a), channel_id=1, source_target_pairs={{0,6},{1,7},{2,4},{3,5},{4,2},{5,3},{6,0},{7,1},{8,14},{9,15},{10,... | collective-permute-start | bytes 221192 | tf_op jit(solution)/shard_map/ppermute | solution.py:356
  60.2 1.3 collective-permute-start.6
  61.5 4.4 %collective-permute-start.7 = (f32[48,384]{1,0:T(8,128)S(1)}, f32[48,384]{1,0:T(8,128)S(1)}, u32[]{:S(2)}, u32[]{:S(2)}) collective-permute-start(f32[48,384]{1,0:T(8,128)S(1)} %add.89), channel_id=1, source_target_pairs={{0,2},{1,3},{2,0},{3,1},{4,6},{5,7},{6,4},{7,5},{8,10},{9,11},{10,... | collective-permute-start | bytes 221192 | tf_op jit(solution)/shard_map/ppermute | solution.py:355
  66.0 5.6 %collective-permute-start.8 = (f32[48,384]{1,0:T(8,128)S(1)}, f32[48,384]{1,0:T(8,128)S(1)}, u32[]{:S(2)}, u32[]{:S(2)}) collective-permute-start(f32[48,384]{1,0:T(8,128)S(1)} %add.90.use_a), channel_id=1, source_target_pairs={{0,6},{1,7},{2,4},{3,5},{4,2},{5,3},{6,0},{7,1},{8,14},{9,15},{10,... | collective-permute-start | bytes 221192 | tf_op jit(solution)/shard_map/ppermute | solution.py:356
  81.5 1.5 collective-permute-start.9
  83.0 4.4 %collective-permute-start.10 = (f32[48,384]{1,0:T(8,128)S(1)}, f32[48,384]{1,0:T(8,128)S(1)}, u32[]{:S(2)}, u32[]{:S(2)}) collective-permute-start(f32[48,384]{1,0:T(8,128)S(1)} %add.91), channel_id=1, source_target_pairs={{0,2},{1,3},{2,0},{3,1},{4,6},{5,7},{6,4},{7,5},{8,10},{9,11},{10,... | collective-permute-start | bytes 221192 | tf_op jit(solution)/shard_map/ppermute | solution.py:355
  87.5 5.6 %collective-permute-start.11 = (f32[48,384]{1,0:T(8,128)S(1)}, f32[48,384]{1,0:T(8,128)S(1)}, u32[]{:S(2)}, u32[]{:S(2)}) collective-permute-start(f32[48,384]{1,0:T(8,128)S(1)} %add.92.use_a), channel_id=1, source_target_pairs={{0,6},{1,7},{2,4},{3,5},{4,2},{5,3},{6,0},{7,1},{8,14},{9,15},{10,... | collective-permute-start | bytes 221192 | tf_op jit(solution)/shard_map/ppermute | solution.py:356
  103.6 11.8 %collective-permute-start.20 = (f32[4,224,128]{2,1,0:T(8,128)S(1)}, f32[4,224,128]{2,1,0:T(8,128)S(1)}, u32[]{:S(2)}, u32[]{:S(2)}) collective-permute-start(f32[4,224,128]{2,1,0:T(8,128)S(1)} %get-tuple-element.94), channel_id=1, source_target_pairs={{0,32},{8,40},{16,48},{24,56},{32,64},{40,72},{48,80},{56,88},{64,... | collective-permute-start | bytes 1376264 | tf_op jit(solution)/shard_map/ppermute | solution.py:372
  105.2 10.3 %collective-permute-start.21 = (f32[4,224,128]{2,1,0:T(8,128)S(1)}, f32[4,224,128]{2,1,0:T(8,128)S(1)}, u32[]{:S(2)}, u32[]{:S(2)}) collective-permute-start(f32[4,224,128]{2,1,0:T(8,128)S(1)} %get-tuple-element.95), channel_id=1, source_target_pairs={{0,96},{8,104},{16,112},{24,120},{32,0},{40,8},{48,16},{56,24},{64... | collective-permute-start | bytes 1376264 | tf_op jit(solution)/shard_map/ppermute | solution.py:372
  106.8 12.9 %collective-permute-start.12 = (f32[4,224,128]{2,1,0:T(8,128)S(1)}, f32[4,224,128]{2,1,0:T(8,128)S(1)}, u32[]{:S(2)}, u32[]{:S(2)}) collective-permute-start(f32[4,224,128]{2,1,0:T(8,128)S(1)} %get-tuple-element.84), channel_id=1, source_target_pairs={{0,8},{8,16},{16,24},{24,0},{32,40},{40,48},{48,56},{56,32},{64,72... | collective-permute-start | bytes 1376264 | tf_op jit(solution)/shard_map/ppermute | solution.py:372
  108.2 11.5 %collective-permute-start.13 = (f32[4,224,128]{2,1,0:T(8,128)S(1)}, f32[4,224,128]{2,1,0:T(8,128)S(1)}, u32[]{:S(2)}, u32[]{:S(2)}) collective-permute-start(f32[4,224,128]{2,1,0:T(8,128)S(1)} %get-tuple-element.85), channel_id=1, source_target_pairs={{0,24},{8,0},{16,8},{24,16},{32,56},{40,32},{48,40},{56,48},{64,88... | collective-permute-start | bytes 1376264 | tf_op jit(solution)/shard_map/ppermute | solution.py:372
  116.4 20.7 %collective-permute-start.22 = (f32[2,4,224,128]{3,2,1,0:T(8,128)S(1)}, f32[2,4,224,128]{3,2,1,0:T(8,128)S(1)}, u32[]{:S(2)}, u32[]{:S(2)}) collective-permute-start(f32[2,4,224,128]{3,2,1,0:T(8,128)S(1)} %get-tuple-element.96), channel_id=1, source_target_pairs={{0,32},{8,40},{16,48},{24,56},{32,64},{40,72},{48,80},{56,88},{64,... | collective-permute-start | bytes 2752520 | tf_op jit(solution)/shard_map/ppermute | solution.py:372
  117.9 19.2 %collective-permute-start.23 = (f32[2,4,224,128]{3,2,1,0:T(8,128)S(1)}, f32[2,4,224,128]{3,2,1,0:T(8,128)S(1)}, u32[]{:S(2)}, u32[]{:S(2)}) collective-permute-start(f32[2,4,224,128]{3,2,1,0:T(8,128)S(1)} %get-tuple-element.97), channel_id=1, source_target_pairs={{0,96},{8,104},{16,112},{24,120},{32,0},{40,8},{48,16},{56,24},{64... | collective-permute-start | bytes 2752520 | tf_op jit(solution)/shard_map/ppermute | solution.py:372
  120.7 23.5 %collective-permute-start.14 = (f32[2,4,224,128]{3,2,1,0:T(8,128)S(1)}, f32[2,4,224,128]{3,2,1,0:T(8,128)S(1)}, u32[]{:S(2)}, u32[]{:S(2)}) collective-permute-start(f32[2,4,224,128]{3,2,1,0:T(8,128)S(1)} %get-tuple-element.86), channel_id=1, source_target_pairs={{0,8},{8,16},{16,24},{24,0},{32,40},{40,48},{48,56},{56,32},{64,72... | collective-permute-start | bytes 2752520 | tf_op jit(solution)/shard_map/ppermute | solution.py:372
  122.2 22.0 %collective-permute-start.15 = (f32[2,4,224,128]{3,2,1,0:T(8,128)S(1)}, f32[2,4,224,128]{3,2,1,0:T(8,128)S(1)}, u32[]{:S(2)}, u32[]{:S(2)}) collective-permute-start(f32[2,4,224,128]{3,2,1,0:T(8,128)S(1)} %get-tuple-element.87), channel_id=1, source_target_pairs={{0,24},{8,0},{16,8},{24,16},{32,56},{40,32},{48,40},{56,48},{64,88... | collective-permute-start | bytes 2752520 | tf_op jit(solution)/shard_map/ppermute | solution.py:372
  138.2 11.6 %collective-permute-start.24 = (f32[448,128]{1,0:T(8,128)S(1)}, f32[448,128]{1,0:T(8,128)S(1)}, u32[]{:S(2)}, u32[]{:S(2)}) collective-permute-start(f32[448,128]{1,0:T(8,128)S(1)} %get-tuple-element.99), channel_id=1, source_target_pairs={{0,8},{8,16},{16,24},{24,0},{32,40},{40,48},{48,56},{56,32},{64,72... | collective-permute-start | bytes 688136 | tf_op jit(solution)/shard_map/ppermute | solution.py:372
  139.6 12.3 %collective-permute-start.25 = (f32[448,128]{1,0:T(8,128)S(1)}, f32[448,128]{1,0:T(8,128)S(1)}, u32[]{:S(2)}, u32[]{:S(2)}) collective-permute-start(f32[448,128]{1,0:T(8,128)S(1)} %get-tuple-element.100), channel_id=1, source_target_pairs={{0,16},{8,24},{16,0},{24,8},{32,48},{40,56},{48,32},{56,40},{64,80... | collective-permute-start | bytes 688136 | tf_op jit(solution)/shard_map/ppermute | solution.py:372
  142.8 9.2 %collective-permute-start.26 = (f32[448,128]{1,0:T(8,128)S(1)}, f32[448,128]{1,0:T(8,128)S(1)}, u32[]{:S(2)}, u32[]{:S(2)}) collective-permute-start(f32[448,128]{1,0:T(8,128)S(1)} %get-tuple-element.101), channel_id=1, source_target_pairs={{0,24},{8,0},{16,8},{24,16},{32,56},{40,32},{48,40},{56,48},{64,88... | collective-permute-start | bytes 688136 | tf_op jit(solution)/shard_map/ppermute | solution.py:372
  145.3 9.4 %collective-permute-start.16 = (f32[448,128]{1,0:T(8,128)S(1)}, f32[448,128]{1,0:T(8,128)S(1)}, u32[]{:S(2)}, u32[]{:S(2)}) collective-permute-start(f32[448,128]{1,0:T(8,128)S(1)} %get-tuple-element.89), channel_id=1, source_target_pairs={{0,32},{8,40},{16,48},{24,56},{32,64},{40,72},{48,80},{56,88},{64,... | collective-permute-start | bytes 688136 | tf_op jit(solution)/shard_map/ppermute | solution.py:372
  146.3 10.0 %collective-permute-start.17 = (f32[448,128]{1,0:T(8,128)S(1)}, f32[448,128]{1,0:T(8,128)S(1)}, u32[]{:S(2)}, u32[]{:S(2)}) collective-permute-start(f32[448,128]{1,0:T(8,128)S(1)} %get-tuple-element.90), channel_id=1, source_target_pairs={{0,64},{8,72},{16,80},{24,88},{32,96},{40,104},{48,112},{56,120},{... | collective-permute-start | bytes 688136 | tf_op jit(solution)/shard_map/ppermute | solution.py:372
  149.8 6.5 %collective-permute-start.18 = (f32[448,128]{1,0:T(8,128)S(1)}, f32[448,128]{1,0:T(8,128)S(1)}, u32[]{:S(2)}, u32[]{:S(2)}) collective-permute-start(f32[448,128]{1,0:T(8,128)S(1)} %get-tuple-element.91), channel_id=1, source_target_pairs={{0,96},{8,104},{16,112},{24,120},{32,0},{40,8},{48,16},{56,24},{64... | collective-permute-start | bytes 688136 | tf_op jit(solution)/shard_map/ppermute | solution.py:372
  152.8 13.2 %collective-permute-start.27 = (f32[448,128]{1,0:T(8,128)S(1)}, f32[448,128]{1,0:T(8,128)S(1)}, u32[]{:S(2)}, u32[]{:S(2)}) collective-permute-start(f32[448,128]{1,0:T(8,128)S(1)} %get-tuple-element.113), channel_id=1, source_target_pairs={{0,24},{8,0},{16,8},{24,16},{32,56},{40,32},{48,40},{56,48},{64,88... | collective-permute-start | bytes 688136 | tf_op jit(solution)/shard_map/ppermute | solution.py:372
  157.1 9.8 %collective-permute-start.19 = (f32[448,128]{1,0:T(8,128)S(1)}, f32[448,128]{1,0:T(8,128)S(1)}, u32[]{:S(2)}, u32[]{:S(2)}) collective-permute-start(f32[448,128]{1,0:T(8,128)S(1)} %get-tuple-element.119), channel_id=1, source_target_pairs={{0,96},{8,104},{16,112},{24,120},{32,0},{40,8},{48,16},{56,24},{64... | collective-permute-start | bytes 688136 | tf_op jit(solution)/shard_map/ppermute | solution.py:372
  159.6 17.0 %collective-permute-start.30 = (f32[448,128]{1,0:T(8,128)S(1)}, f32[448,128]{1,0:T(8,128)S(1)}, u32[]{:S(2)}, u32[]{:S(2)}) collective-permute-start(f32[448,128]{1,0:T(8,128)S(1)} %get-tuple-element.113), channel_id=1, source_target_pairs={{0,16},{8,24},{16,0},{24,8},{32,48},{40,56},{48,32},{56,40},{64,80... | collective-permute-start | bytes 688136 | tf_op jit(solution)/shard_map/ppermute | solution.py:372
  164.1 12.5 %collective-permute-start.31 = (f32[448,128]{1,0:T(8,128)S(1)}, f32[448,128]{1,0:T(8,128)S(1)}, u32[]{:S(2)}, u32[]{:S(2)}) collective-permute-start(f32[448,128]{1,0:T(8,128)S(1)} %get-tuple-element.113), channel_id=1, source_target_pairs={{0,8},{8,16},{16,24},{24,0},{32,40},{40,48},{48,56},{56,32},{64,72... | collective-permute-start | bytes 688136 | tf_op jit(solution)/shard_map/ppermute | solution.py:372
  165.9 10.7 %collective-permute-start.28 = (f32[448,128]{1,0:T(8,128)S(1)}, f32[448,128]{1,0:T(8,128)S(1)}, u32[]{:S(2)}, u32[]{:S(2)}) collective-permute-start(f32[448,128]{1,0:T(8,128)S(1)} %get-tuple-element.119), channel_id=1, source_target_pairs={{0,64},{8,72},{16,80},{24,88},{32,96},{40,104},{48,112},{56,120},{... | collective-permute-start | bytes 688136 | tf_op jit(solution)/shard_map/ppermute | solution.py:372
  166.0 10.6 %collective-permute-start.29 = (f32[448,128]{1,0:T(8,128)S(1)}, f32[448,128]{1,0:T(8,128)S(1)}, u32[]{:S(2)}, u32[]{:S(2)}) collective-permute-start(f32[448,128]{1,0:T(8,128)S(1)} %get-tuple-element.119), channel_id=1, source_target_pairs={{0,32},{8,40},{16,48},{24,56},{32,64},{40,72},{48,80},{56,88},{64,... | collective-permute-start | bytes 688136 | tf_op jit(solution)/shard_map/ppermute | solution.py:372
  166.8 1.2 collective-permute-start.32
  168.1 3.6 %collective-permute-start.33 = (f32[8,128]{1,0:T(8,128)S(1)}, f32[8,128]{1,0:T(8,128)S(1)}, u32[]{:S(2)}, u32[]{:S(2)}) collective-permute-start(f32[8,128]{1,0:T(8,128)S(1)} %add.99), channel_id=1, source_target_pairs={{0,2},{1,3},{2,0},{3,1},{4,6},{5,7},{6,4},{7,5},{8,10},{9,11},{10,... | collective-permute-start | bytes 12296 | tf_op jit(solution)/shard_map/ppermute | solution.py:355
  171.7 4.9 %collective-permute-start.34 = (f32[8,128]{1,0:T(8,128)S(1)}, f32[8,128]{1,0:T(8,128)S(1)}, u32[]{:S(2)}, u32[]{:S(2)}) collective-permute-start(f32[8,128]{1,0:T(8,128)S(1)} %add.100), channel_id=1, source_target_pairs={{0,6},{1,7},{2,4},{3,5},{4,2},{5,3},{6,0},{7,1},{8,14},{9,15},{10,... | collective-permute-start | bytes 12296 | tf_op jit(solution)/shard_map/ppermute | solution.py:356
  176.7 22.5 %collective-permute-start.42 = (f32[2,4,224,128]{3,2,1,0:T(8,128)S(1)}, f32[2,4,224,128]{3,2,1,0:T(8,128)S(1)}, u32[]{:S(2)}, u32[]{:S(2)}) collective-permute-start(f32[2,4,224,128]{3,2,1,0:T(8,128)S(1)} %pad_maximum_fusion.1.refs_0_), channel_id=1, source_target_pairs={{0,8},{8,16},{16,24},{24,0},{32,40},{40,48},{48,56},{56,32},{64,72... | collective-permute-start | bytes 2752520 | tf_op jit(solution)/shard_map/ppermute | solution.py:372
  180.9 20.8 %collective-permute-start.41 = (f32[2,4,224,128]{3,2,1,0:T(8,128)S(1)}, f32[2,4,224,128]{3,2,1,0:T(8,128)S(1)}, u32[]{:S(2)}, u32[]{:S(2)}) collective-permute-start(f32[2,4,224,128]{3,2,1,0:T(8,128)S(1)} %pad_maximum_fusion.1.refs_0_), channel_id=1, source_target_pairs={{0,24},{8,0},{16,8},{24,16},{32,56},{40,32},{48,40},{56,48},{64,88... | collective-permute-start | bytes 2752520 | tf_op jit(solution)/shard_map/ppermute | solution.py:372
  180.9 22.0 %collective-permute-start.35 = (f32[2,4,224,128]{3,2,1,0:T(8,128)S(1)}, f32[2,4,224,128]{3,2,1,0:T(8,128)S(1)}, u32[]{:S(2)}, u32[]{:S(2)}) collective-permute-start(f32[2,4,224,128]{3,2,1,0:T(8,128)S(1)} %pad_maximum_fusion.refs_5_), channel_id=1, source_target_pairs={{0,96},{8,104},{16,112},{24,120},{32,0},{40,8},{48,16},{56,24},{64... | collective-permute-start | bytes 2752520 | tf_op jit(solution)/shard_map/ppermute | solution.py:372
  184.7 21.1 %collective-permute-start.36 = (f32[2,4,224,128]{3,2,1,0:T(8,128)S(1)}, f32[2,4,224,128]{3,2,1,0:T(8,128)S(1)}, u32[]{:S(2)}, u32[]{:S(2)}) collective-permute-start(f32[2,4,224,128]{3,2,1,0:T(8,128)S(1)} %pad_maximum_fusion.refs_5_), channel_id=1, source_target_pairs={{0,32},{8,40},{16,48},{24,56},{32,64},{40,72},{48,80},{56,88},{64,... | collective-permute-start | bytes 2752520 | tf_op jit(solution)/shard_map/ppermute | solution.py:372
  199.2 25.6 %collective-permute-start.43 = (f32[4,224,128]{2,1,0:T(8,128)S(1)}, f32[4,224,128]{2,1,0:T(8,128)S(1)}, u32[]{:S(2)}, u32[]{:S(2)}) collective-permute-start(f32[4,224,128]{2,1,0:T(8,128)S(1)} %slice_bitcast_fusion.1), channel_id=1, source_target_pairs={{0,8},{8,16},{16,24},{24,0},{32,40},{40,48},{48,56},{56,32},{64,72... | collective-permute-start | bytes 1376264 | tf_op jit(solution)/shard_map/ppermute | solution.py:372
  201.7 23.1 %collective-permute-start.44 = (f32[4,224,128]{2,1,0:T(8,128)S(1)}, f32[4,224,128]{2,1,0:T(8,128)S(1)}, u32[]{:S(2)}, u32[]{:S(2)}) collective-permute-start(f32[4,224,128]{2,1,0:T(8,128)S(1)} %slice_bitcast_fusion), channel_id=1, source_target_pairs={{0,24},{8,0},{16,8},{24,16},{32,56},{40,32},{48,40},{56,48},{64,88... | collective-permute-start | bytes 1376264 | tf_op jit(solution)/shard_map/ppermute | solution.py:372
  205.8 19.0 %collective-permute-start.45 = (f32[4,224,128]{2,1,0:T(8,128)S(1)}, f32[4,224,128]{2,1,0:T(8,128)S(1)}, u32[]{:S(2)}, u32[]{:S(2)}) collective-permute-start(f32[4,224,128]{2,1,0:T(8,128)S(1)} %slice_bitcast_fusion.3), channel_id=1, source_target_pairs={{0,32},{8,40},{16,48},{24,56},{32,64},{40,72},{48,80},{56,88},{64,... | collective-permute-start | bytes 1376264 | tf_op jit(solution)/shard_map/ppermute | solution.py:372
  205.8 5.7 %collective-permute-start.37 = (f32[8,128]{1,0:T(8,128)S(1)}, f32[8,128]{1,0:T(8,128)S(1)}, u32[]{:S(2)}, u32[]{:S(2)}) collective-permute-start(f32[8,128]{1,0:T(8,128)S(1)} %add.101), channel_id=1, source_target_pairs={{0,8},{8,0},{16,24},{24,16},{32,40},{40,32},{48,56},{56,48},{64,72... | collective-permute-start | bytes 12296 | tf_op jit(solution)/shard_map/ppermute | solution.py:362
  207.7 17.1 %collective-permute-start.46 = (f32[4,224,128]{2,1,0:T(8,128)S(1)}, f32[4,224,128]{2,1,0:T(8,128)S(1)}, u32[]{:S(2)}, u32[]{:S(2)}) collective-permute-start(f32[4,224,128]{2,1,0:T(8,128)S(1)} %slice_bitcast_fusion.2), channel_id=1, source_target_pairs={{0,96},{8,104},{16,112},{24,120},{32,0},{40,8},{48,16},{56,24},{64... | collective-permute-start | bytes 1376264 | tf_op jit(solution)/shard_map/ppermute | solution.py:372
  211.5 4.8 %collective-permute-start.38 = (f32[8,128]{1,0:T(8,128)S(1)}, f32[8,128]{1,0:T(8,128)S(1)}, u32[]{:S(2)}, u32[]{:S(2)}) collective-permute-start(f32[8,128]{1,0:T(8,128)S(1)} %add.102), channel_id=1, source_target_pairs={{0,24},{8,16},{16,8},{24,0},{32,56},{40,48},{48,40},{56,32},{64,88... | collective-permute-start | bytes 12296 | tf_op jit(solution)/shard_map/ppermute | solution.py:362
  216.4 3.6 %collective-permute-start.39 = (f32[8,128]{1,0:T(8,128)S(1)}, f32[8,128]{1,0:T(8,128)S(1)}, u32[]{:S(2)}, u32[]{:S(2)}) collective-permute-start(f32[8,128]{1,0:T(8,128)S(1)} %add.103), channel_id=1, source_target_pairs={{0,32},{8,40},{16,48},{24,56},{32,0},{40,8},{48,16},{56,24},{64,96... | collective-permute-start | bytes 12296 | tf_op jit(solution)/shard_map/ppermute | solution.py:362
  220.0 4.8 %collective-permute-start.40 = (f32[8,128]{1,0:T(8,128)S(1)}, f32[8,128]{1,0:T(8,128)S(1)}, u32[]{:S(2)}, u32[]{:S(2)}) collective-permute-start(f32[8,128]{1,0:T(8,128)S(1)} %add.104), channel_id=1, source_target_pairs={{0,96},{8,104},{16,112},{24,120},{32,64},{40,72},{48,80},{56,88},{... | collective-permute-start | bytes 12296 | tf_op jit(solution)/shard_map/ppermute | solution.py:362
  (6 other events, 100.2 us)

commit v4 on v3

--- a/solution.py
+++ b/solution.py
@@ -95,7 +95,7 @@
             cost_ref[i].astype(f32) + price_ref[i].astype(f32) - penalty * anchor_ref[0].astype(f32)
         )
         linear_ref[s + i] = linear.T
-        x = start_ref[i].astype(f32).T
+        x = start_ref[i].T.astype(f32)
         used_scr[s + i] = folded(c * x)
         xs.append(x)
     for k in (1, 2):
@@ -115,6 +115,10 @@
         usage_ref[...] = used_dot(used_scr[...], row_to_veh[...])
 
 
+def summed(a, b, c, d):
+    return (a[...] + c[...]) + (b[...] + d[...])
+
+
 def crew_update(usage, norms, limit, dual):
     one = jnp.maximum(dual + dual_step * (usage[0:16] - limit), 0.0)
     third = usage[32:48] - step_size * one * norms
@@ -128,8 +132,10 @@
     linear_ref,
     hess_ref,
     coef_t_ref,
-    use_a,
-    use_b,
+    use_0,
+    use_1,
+    use_2,
+    use_3,
     norms_ref,
     limit_ref,
     dual_ref,
@@ -144,7 +150,7 @@
     count = partial_ref.shape[0]
     n = hess_ref.shape[-1]
     one, two, three = crew_update(
-        use_a[0:48] + use_b[0:48], norms_ref[0:1], limit_ref[...], dual_ref[...]
+        summed(use_0, use_1, use_2, use_3)[0:48], norms_ref[0:1], limit_ref[...], dual_ref[...]
     )
     new_dual_ref[...] = three
     crew_scr[:, 0, :] = step_size * exact_dot(
@@ -183,8 +189,10 @@
     linear_ref,
     hess_ref,
     coef_t_ref,
-    use_a,
-    use_b,
+    use_0,
+    use_1,
+    use_2,
+    use_3,
     norms_ref,
     limit_ref,
     dual_ref,
@@ -208,7 +216,7 @@
     @pl.when(s == 0)
     def _():
         one, two, three = crew_update(
-            use_a[0:48] + use_b[0:48], norms_ref[0:1], limit_ref[...], dual_ref[...]
+            summed(use_0, use_1, use_2, use_3)[0:48], norms_ref[0:1], limit_ref[...], dual_ref[...]
         )
         new_dual_ref[...] = three
         crew_scr[:, 0, :] = step_size * exact_dot(
@@ -352,8 +360,17 @@
 
 def usage_exchange(value):
     value = value + lax.ppermute(value, "veh", veh_pairs("core"))
-    value = value + lax.ppermute(value, "veh", veh_pairs(PAIR_A))
-    return value, lax.ppermute(value, "veh", veh_pairs(PAIR_B))
+    turns = [
+        lax.ppermute(value, "veh", veh_pairs({z: (z + by) % 4 for z in range(4)}))
+        for by in (1, 3, 2)
+    ]
+    return [value, turns[0], turns[2], turns[1]]
+
+
+def spread_over_veh(value):
+    for kind in ("core", PAIR_A, PAIR_B):
+        value = value + lax.ppermute(value, "veh", veh_pairs(kind))
+    return value
 
 
 def sum_over_scen(value):
@@ -399,9 +416,12 @@
     return {0: own, **{by: shift(own, second, -by) for by in (1, 3, 2)}}
 
 
-def gather_near(row, first):
+def gather_pack(row):
     rows = row[0].shape[0] // 2
-    pack = jnp.stack([row[k].reshape(2, rows, -1) for k in range(4)], axis=1)
+    return jnp.stack([row[k].reshape(2, rows, -1) for k in range(4)], axis=1)
+
+
+def gather_near(pack, first):
     return pack, shift(pack, first, -1), shift(pack, first, 1)
 
 
@@ -495,12 +515,12 @@
         crew_row[None, :],
     )
 
-    use_a, use_b = usage_exchange(usage)
-    norms = use_a[48:56] + use_b[48:56]
+    use = usage_exchange(usage)
+    norms = summed(*[u[48:56] for u in use])
     for _ in range(3):
         partial, usage, dual = pl.pallas_call(
             middle_kernel,
-            in_specs=[vm] * 10,
+            in_specs=[vm] * 12,
             out_specs=[vm] * 3,
             out_shape=[
                 tall,
@@ -523,8 +543,7 @@
                     linear,
                     hessian,
                     coef_t,
-                    use_a,
-                    use_b,
+                    *use,
                     norms,
                     limit,
                     dual,
@@ -532,7 +551,7 @@
                 )
             ]
         )
-        use_a, use_b = usage_exchange(usage)
+        use = usage_exchange(usage)
 
     me_y, me_x = np.arange(16)[:, None] // 4, np.arange(16)[:, None] % 4
     it_y, it_x = np.arange(16)[None, :] // 4, np.arange(16)[None, :] % 4
@@ -564,7 +583,7 @@
         grid_spec=pltpu.PrefetchScalarGridSpec(
             num_scalar_prefetch=2,
             grid=(count,),
-            in_specs=[vm] * 10,
+            in_specs=[vm] * 12,
             out_specs=[flat_block] + [vm] * 9,
             scratch_shapes=[pltpu.VMEM((32, 1, vehicles), f32)],
         ),
@@ -592,8 +611,7 @@
                 linear,
                 hessian,
                 coef_t,
-                use_a,
-                use_b,
+                *use,
                 norms,
                 limit,
                 dual,
@@ -647,10 +665,10 @@
     spreads += [m[1] for m in moved]
     own_a, own_b = moved[0][0], moved[1][0]
     row_a, row_b = gather_row(own_a, "y"), gather_row(own_b, "x")
-    row_a[1], row_b[1], spread = lax.optimization_barrier((row_a[1], row_b[1], sum(spreads)))
-    spread = sum(usage_exchange(spread))
-    row_a, row_b, spread = lax.optimization_barrier((row_a, row_b, spread))
-    near_a, near_b = gather_near(row_a, "x"), gather_near(row_b, "y")
+    pack_a, pack_b = gather_pack(row_a), gather_pack(row_b)
+    pack_a, pack_b, spread = lax.optimization_barrier((pack_a, pack_b, sum(spreads)))
+    near_a, near_b = gather_near(pack_a, "x"), gather_near(pack_b, "y")
+    spread = spread_over_veh(spread)
     near_b, spread = lax.optimization_barrier((near_b, spread))
     spread_total = sum_over_scen(spread)
     means = gather_far(*near_a, "x") + gather_far(*near_b, "y")

time: 232 us -> 226 us (0.974); the launches traced: 233 us -> 223 us
  waiting for transfers between devices: 83.5 us -> 75.3 us
    ppermute x10 -> x15, waiting for transfers between devices: 29.7 us -> 19.6 us  [the longest x12 16.5 us: usage_exchange(): lax.ppermute(value, 'veh', veh_pairs({z: (z + by) % 4 for z in range(4)}))]
    ppermute x28, starting transfers between devices: 51.2 us -> 45 us  [shift(): return lax.ppermute(value, 'scen', pairs)]
    ppermute x10 -> x15, starting transfers between devices: 19.6 us -> 25.6 us  [the longest x12 18.7 us: usage_exchange(): lax.ppermute(value, 'veh', veh_pairs({z: (z + by) % 4 for z in range(4)}))]
    ppermute x4, waiting for transfers between devices: 9.54 us -> 14.3 us  [sum_over_scen(): value = value + lax.ppermute(value, 'scen', scen_pairs(pair, axis))]
    ppermute x5 -> x4, waiting for transfers between devices: 6.01 us -> 4.42 us  [usage_exchange(): value = value + lax.ppermute(value, 'veh', veh_pairs('core'))]
  transfers between devices with their start and end apart: 47 -> 51, of which waited for: 26 -> 34; matrix products, arithmetic and copies ran while one was open for 1% -> 1% of each run, Pallas kernels for 2% -> 3%
where the time goes in v4:
time: 226 us; the launch traced here: 223 us
  waiting for transfers between devices  75.3 us (33%)
  starting transfers between devices  75 us (33%)
  Pallas kernels  66.6 us (29%)
  local copies, waits for them, and re-layouts  3.08 us (1%)
    ppermute x28, starting transfers between devices, shift(): return lax.ppermute(value, 'scen', pairs)  45 us
    ppermute x28, waiting for transfers between devices, shift(): return lax.ppermute(value, 'scen', pairs)  37 us
    pallas_call x3, Pallas kernels, shards(): pl.pallas_call(middle_kernel, in_specs=[vm] * 12, out_specs=[vm] * 3, out...  29.7 us
    ppermute x12, starting transfers between devices, usage_exchange(): lax.ppermute(value, 'veh', veh_pairs({z: (z + by) % 4 for z in range(4)}))  18.7 us
    ppermute x12, waiting for transfers between devices, usage_exchange(): lax.ppermute(value, 'veh', veh_pairs({z: (z + by) % 4 for z in range(4)}))  16.5 us
    ppermute x4, waiting for transfers between devices, sum_over_scen(): value = value + lax.ppermute(value, 'scen', scen_pairs(pair, axis))  14.3 us
    pallas_call x1, Pallas kernels, shards(): pl.pallas_call(first_kernel, grid_spec=pltpu.PrefetchScalarGridSpec(num_s...  13 us
    pallas_call x1, Pallas kernels, shards(): pl.pallas_call(last_kernel, grid_spec=pltpu.PrefetchScalarGridSpec(num_sc...  10.4 us
  transfers between devices with their start and end apart: 51, of which 34 were waited for; matrix products, arithmetic and copies ran while one was open for 1% of the time, Pallas kernels for 3%

profile of v4, /device:TPU:0, one launch (start us, length us, event | category | flops | bytes accessed | tf_op | source)
XLA Modules:
  0.0 222.6 jit_solution(5753991951155066415)
XLA Ops:
  2.8 13.0 %first_steps.1 = (f32[16,128,896]{2,1,0:T(8,128)S(1)}, f32[16,128,896]{2,1,0:T(8,128)S(1)}, f32[128,896]{1,0:T(8,128)S(1)}, bf16[384,896]{1,0:T(8,128)(2,1)S(1)}, f32[56,384]{1,0:T(8,128)S(1)}) custom-call(s32[16]{0:T(128)S(1)} %dynamic-slice_bitcast_fusion.bundles, bf16[16,896,128]{2,1,0:T(8,128)(2,1)} %start_ref.1, bf16[16,896,128]{2,1,0:T(8,128)(2,1)} %cost_ref.1, ...), custom_call_target="tpu_custom_call" | custom-call | tf_op jit(solution)/shard_map/first_steps/pallas_call | solution.py:473
  17.2 2.1 collective-permute-start.1
  19.3 3.6 %collective-permute-start.2 = (f32[56,384]{1,0:T(8,128)S(1)}, f32[56,384]{1,0:T(8,128)S(1)}, u32[]{:S(2)}, u32[]{:S(2)}) collective-permute-start(f32[56,384]{1,0:T(8,128)S(1)} %add.78.use_0), channel_id=1, source_target_pairs={{0,4},{1,5},{2,6},{3,7},{4,0},{5,1},{6,2},{7,3},{8,12},{9,13},{10,... | collective-permute-start | bytes 258056 | tf_op jit(solution)/shard_map/ppermute | solution.py:364
  24.2 3.0 %collective-permute-done.2.use_2 = f32[56,384]{1,0:T(8,128)S(1)} collective-permute-done((f32[56,384]{1,0:T(8,128)S(1)}, f32[56,384]{1,0:T(8,128)S(1)}, u32[]{:S(2)}, u32[]{:S(2)}) %collective-permute-start.2) | collective-permute-done | bytes 86048 | tf_op jit(solution)/shard_map/ppermute | solution.py:364
  27.3 9.9 %three_steps.3 = (f32[16,128,896]{2,1,0:T(8,128)S(1)}, f32[48,384]{1,0:T(8,128)S(1)}, f32[16,384]{1,0:T(8,128)S(1)}) custom-call(f32[16,128,896]{2,1,0:T(8,128)S(1)} %get-tuple-element.58.partial_ref, f32[16,128,896]{2,1,0:T(8,128)S(1)} %get-tuple-element.59.linear_ref, bf16[16,128,128]{2,1,0:T(8,128)(2,1)S(1)} %copy-done, ...), custom_call_target="tpu_custom_call", output_to_operand_aliasing={{0}: (0, {})} | custom-call | tf_op jit(solution)/shard_map/three_steps/pallas_call | solution.py:521
  39.8 2.5 %collective-permute-start.6 = (f32[48,384]{1,0:T(8,128)S(1)}, f32[48,384]{1,0:T(8,128)S(1)}, u32[]{:S(2)}, u32[]{:S(2)}) collective-permute-start(f32[48,384]{1,0:T(8,128)S(1)} %add.82.use_0), channel_id=1, source_target_pairs={{0,4},{1,5},{2,6},{3,7},{4,0},{5,1},{6,2},{7,3},{8,12},{9,13},{10,... | collective-permute-start | bytes 221192 | tf_op jit(solution)/shard_map/ppermute | solution.py:364
  44.6 1.6 collective-permute-done.6.use_2
  46.7 9.9 %three_steps.4 = (f32[16,128,896]{2,1,0:T(8,128)S(1)}, f32[48,384]{1,0:T(8,128)S(1)}, f32[16,384]{1,0:T(8,128)S(1)}) custom-call(f32[16,128,896]{2,1,0:T(8,128)S(1)} %get-tuple-element.63.partial_ref, f32[16,128,896]{2,1,0:T(8,128)S(1)} %get-tuple-element.59.linear_ref, bf16[16,128,128]{2,1,0:T(8,128)(2,1)S(1)} %copy-done, ...), custom_call_target="tpu_custom_call", output_to_operand_aliasing={{0}: (0, {})} | custom-call | tf_op jit(solution)/shard_map/three_steps/pallas_call | solution.py:521
  58.0 1.9 collective-permute-start.10
  59.8 2.1 collective-permute-start.11
  62.0 1.9 collective-permute-done.10.use_2
  65.3 2.2 collective-permute-done.9.use_1
  67.5 9.9 %three_steps.5 = (f32[16,128,896]{2,1,0:T(8,128)S(1)}, f32[48,384]{1,0:T(8,128)S(1)}, f32[16,384]{1,0:T(8,128)S(1)}) custom-call(f32[16,128,896]{2,1,0:T(8,128)S(1)} %get-tuple-element.66.partial_ref, f32[16,128,896]{2,1,0:T(8,128)S(1)} %get-tuple-element.59.linear_ref, bf16[16,128,128]{2,1,0:T(8,128)(2,1)S(1)} %copy-done, ...), custom_call_target="tpu_custom_call", output_to_operand_aliasing={{0}: (0, {})} | custom-call | tf_op jit(solution)/shard_map/three_steps/pallas_call | solution.py:521
  78.8 1.9 collective-permute-start.14
  82.0 3.9 %collective-permute-done.13.use_1 = f32[48,384]{1,0:T(8,128)S(1)} collective-permute-done((f32[48,384]{1,0:T(8,128)S(1)}, f32[48,384]{1,0:T(8,128)S(1)}, u32[]{:S(2)}, u32[]{:S(2)}) %collective-permute-start.13) | collective-permute-done | bytes 73760 | tf_op jit(solution)/shard_map/ppermute | solution.py:364
  86.5 10.4 %last_step.1 = (bf16[16,896,128]{2,1,0:T(8,128)(2,1)}, f32[16,896,128]{2,1,0:T(8,128)S(1)}, f32[16,448,128]{2,1,0:T(8,128)S(1)}, f32[16,448,128]{2,1,0:T(8,128)S...) custom-call(s32[2,16]{1,0:T(2,128)S(1)} %pad_add_fusion.slots, ...), custom_call_target="tpu_custom_call" | custom-call | tf_op jit(solution)/shard_map/last_step/pallas_call | solution.py:581
  97.5 1.6 collective-permute-start.26
  99.1 1.6 collective-permute-start.27
  100.7 1.6 collective-permute-start.16
  102.4 1.7 collective-permute-start.17
  104.2 6.0 %collective-permute-done.26.up_in = f32[4,224,128]{2,1,0:T(8,128)S(1)} collective-permute-done((f32[4,224,128]{2,1,0:T(8,128)S(1)}, f32[4,224,128]{2,1,0:T(8,128)S(1)}, u32[]{:S(2)}, u32[]{:S(2)}) %collective-permute-start.26) | collective-permute-done | bytes 458784 | tf_op jit(solution)/shard_map/ppermute | solution.py:389
  111.3 1.7 collective-permute-start.28
  113.0 1.6 collective-permute-start.29
  115.6 1.7 collective-permute-start.18
  117.2 1.6 collective-permute-start.19
  118.9 14.0 %collective-permute-done.28.up_in = f32[2,4,224,128]{3,2,1,0:T(8,128)S(1)} collective-permute-done((f32[2,4,224,128]{3,2,1,0:T(8,128)S(1)}, f32[2,4,224,128]{3,2,1,0:T(8,128)S(1)}, u32[]{:S(2)}, u32[]{:S(2)}) %collective-permute-start.28) | collective-permute-done | bytes 917536 | tf_op jit(solution)/shard_map/ppermute | solution.py:389
  134.0 1.6 collective-permute-start.30
  135.6 2.9 %collective-permute-start.31 = (f32[448,128]{1,0:T(8,128)S(1)}, f32[448,128]{1,0:T(8,128)S(1)}, u32[]{:S(2)}, u32[]{:S(2)}) collective-permute-start(f32[448,128]{1,0:T(8,128)S(1)} %get-tuple-element.91), channel_id=1, source_target_pairs={{0,16},{8,24},{16,0},{24,8},{32,48},{40,56},{48,32},{56,40},{64,80... | collective-permute-start | bytes 688136 | tf_op jit(solution)/shard_map/ppermute | solution.py:389
  142.1 3.4 %collective-permute-start.21 = (f32[448,128]{1,0:T(8,128)S(1)}, f32[448,128]{1,0:T(8,128)S(1)}, u32[]{:S(2)}, u32[]{:S(2)}) collective-permute-start(f32[448,128]{1,0:T(8,128)S(1)} %get-tuple-element.81), channel_id=1, source_target_pairs={{0,64},{8,72},{16,80},{24,88},{32,96},{40,104},{48,112},{56,120},{... | collective-permute-start | bytes 688136 | tf_op jit(solution)/shard_map/ppermute | solution.py:389
  148.5 1.9 collective-permute-start.33
  152.8 2.0 collective-permute-start.25
  156.1 2.9 %collective-permute-done.33 = f32[448,128]{1,0:T(8,128)S(1)} collective-permute-done((f32[448,128]{1,0:T(8,128)S(1)}, f32[448,128]{1,0:T(8,128)S(1)}, u32[]{:S(2)}, u32[]{:S(2)}) %collective-permute-start.33) | collective-permute-done | bytes 229408 | tf_op jit(solution)/shard_map/ppermute | solution.py:389
  160.3 2.4 %collective-permute-done.35 = f32[448,128]{1,0:T(8,128)S(1)} collective-permute-done((f32[448,128]{1,0:T(8,128)S(1)}, f32[448,128]{1,0:T(8,128)S(1)}, u32[]{:S(2)}, u32[]{:S(2)}) %collective-permute-start.35) | collective-permute-done | bytes 229408 | tf_op jit(solution)/shard_map/ppermute | solution.py:389
  163.5 3.0 %collective-permute-done.24 = f32[448,128]{1,0:T(8,128)S(1)} collective-permute-done((f32[448,128]{1,0:T(8,128)S(1)}, f32[448,128]{1,0:T(8,128)S(1)}, u32[]{:S(2)}, u32[]{:S(2)}) %collective-permute-start.24) | collective-permute-done | bytes 229408 | tf_op jit(solution)/shard_map/ppermute | solution.py:389
  167.3 1.4 collective-permute-start.37
  171.0 2.9 %collective-permute-start.45 = (f32[2,4,224,128]{3,2,1,0:T(8,128)S(1)}, f32[2,4,224,128]{3,2,1,0:T(8,128)S(1)}, u32[]{:S(2)}, u32[]{:S(2)}) collective-permute-start(f32[2,4,224,128]{3,2,1,0:T(8,128)S(1)} %pad_maximum_fusion.refs_0_), channel_id=1, source_target_pairs={{0,24},{8,0},{16,8},{24,16},{32,56},{40,32},{48,40},{56,48},{64,88... | collective-permute-start | bytes 2752520 | tf_op jit(solution)/shard_map/ppermute | solution.py:389
  174.3 6.5 %collective-permute-start.40 = (f32[8,128]{1,0:T(8,128)S(1)}, f32[8,128]{1,0:T(8,128)S(1)}, u32[]{:S(2)}, u32[]{:S(2)}) collective-permute-start(f32[8,128]{1,0:T(8,128)S(1)} %add.92), channel_id=1, source_target_pairs={{0,6},{1,7},{2,4},{3,5},{4,2},{5,3},{6,0},{7,1},{8,14},{9,15},{10,... | collective-permute-start | bytes 12296 | tf_op jit(solution)/shard_map/ppermute | solution.py:372
  180.7 1.6 collective-permute-done.40
  182.3 3.2 %collective-permute-done.36.refs_6_ = f32[2,4,224,128]{3,2,1,0:T(8,128)S(1)} collective-permute-done((f32[2,4,224,128]{3,2,1,0:T(8,128)S(1)}, f32[2,4,224,128]{3,2,1,0:T(8,128)S(1)}, u32[]{:S(2)}, u32[]{:S(2)}) %collective-permute-start.36) | collective-permute-done | bytes 917536 | tf_op jit(solution)/shard_map/ppermute | solution.py:389
  185.5 2.2 collective-permute-done.37.refs_7_
  188.9 2.2 collective-permute-start.50
  191.1 1.6 collective-permute-start.41
  193.6 3.8 %collective-permute-start.48 = (f32[4,224,128]{2,1,0:T(8,128)S(1)}, f32[4,224,128]{2,1,0:T(8,128)S(1)}, u32[]{:S(2)}, u32[]{:S(2)}) collective-permute-start(f32[4,224,128]{2,1,0:T(8,128)S(1)} %slice_bitcast_fusion), channel_id=1, source_target_pairs={{0,24},{8,0},{16,8},{24,16},{32,56},{40,32},{48,40},{56,48},{64,88... | collective-permute-start | bytes 1376264 | tf_op jit(solution)/shard_map/ppermute | solution.py:389
  198.2 8.2 %collective-permute-done.42 = f32[8,128]{1,0:T(8,128)S(1)} collective-permute-done((f32[8,128]{1,0:T(8,128)S(1)}, f32[8,128]{1,0:T(8,128)S(1)}, u32[]{:S(2)}, u32[]{:S(2)}) %collective-permute-start.42) | collective-permute-done | bytes 4128 | tf_op jit(solution)/shard_map/ppermute | solution.py:379
  206.4 3.6 %collective-permute-done.43 = f32[8,128]{1,0:T(8,128)S(1)} collective-permute-done((f32[8,128]{1,0:T(8,128)S(1)}, f32[8,128]{1,0:T(8,128)S(1)}, u32[]{:S(2)}, u32[]{:S(2)}) %collective-permute-start.43) | collective-permute-done | bytes 4128 | tf_op jit(solution)/shard_map/ppermute | solution.py:379
  210.0 1.6 collective-permute-start.44
  212.3 2.5 %collective-permute-done.44 = f32[8,128]{1,0:T(8,128)S(1)} collective-permute-done((f32[8,128]{1,0:T(8,128)S(1)}, f32[8,128]{1,0:T(8,128)S(1)}, u32[]{:S(2)}, u32[]{:S(2)}) %collective-permute-start.44) | collective-permute-done | bytes 4128 | tf_op jit(solution)/shard_map/ppermute | solution.py:379
  214.9 7.7 %new_price.1 = (bf16[16,896,128]{2,1,0:T(8,128)(2,1)}, f32[1,1]{1,0:T(1,128)}) custom-call(s32[2,16]{1,0:T(2,128)S(1)} %pad_add_fusion.slots, f32[16,896,128]{2,1,0:T(8,128)S(1)} %get-tuple-element.73.roster_ref, bf16[16,896,128]{2,1,0:T(8,128)(2,1)} %price_ref.3, f32[8,128]{1,0:T(8,128)S(1)} %add.97.spread_ref, f32[1,256]{1,0:T(1,128)S(1)} %bitcast.36, ...), custom_call_target="tpu_custom_call" | custom-call | tf_op jit(solution)/shard_map/new_price/pallas_call | solution.py:678
  (122 shorter events, 39.8 us)
Async XLA Ops:
  15.8 1.4 collective-permute-start
  17.2 7.0 %collective-permute-start.1 = (f32[56,384]{1,0:T(8,128)S(1)}, f32[56,384]{1,0:T(8,128)S(1)}, u32[]{:S(2)}, u32[]{:S(2)}) collective-permute-start(f32[56,384]{1,0:T(8,128)S(1)} %add.78.use_0), channel_id=1, source_target_pairs={{0,2},{1,3},{2,4},{3,5},{4,6},{5,7},{6,0},{7,1},{8,10},{9,11},{10,... | collective-permute-start | bytes 258056 | tf_op jit(solution)/shard_map/ppermute | solution.py:364
  19.3 8.0 %collective-permute-start.2 = (f32[56,384]{1,0:T(8,128)S(1)}, f32[56,384]{1,0:T(8,128)S(1)}, u32[]{:S(2)}, u32[]{:S(2)}) collective-permute-start(f32[56,384]{1,0:T(8,128)S(1)} %add.78.use_0), channel_id=1, source_target_pairs={{0,4},{1,5},{2,6},{3,7},{4,0},{5,1},{6,2},{7,3},{8,12},{9,13},{10,... | collective-permute-start | bytes 258056 | tf_op jit(solution)/shard_map/ppermute | solution.py:364
  22.8 4.5 %collective-permute-start.3 = (f32[56,384]{1,0:T(8,128)S(1)}, f32[56,384]{1,0:T(8,128)S(1)}, u32[]{:S(2)}, u32[]{:S(2)}) collective-permute-start(f32[56,384]{1,0:T(8,128)S(1)} %add.78.use_0), channel_id=1, source_target_pairs={{0,6},{1,7},{2,0},{3,1},{4,2},{5,3},{6,4},{7,5},{8,14},{9,15},{10,... | collective-permute-start | bytes 258056 | tf_op jit(solution)/shard_map/ppermute | solution.py:364
  37.3 1.3 collective-permute-start.4
  38.6 6.0 %collective-permute-start.5 = (f32[48,384]{1,0:T(8,128)S(1)}, f32[48,384]{1,0:T(8,128)S(1)}, u32[]{:S(2)}, u32[]{:S(2)}) collective-permute-start(f32[48,384]{1,0:T(8,128)S(1)} %add.82.use_0), channel_id=1, source_target_pairs={{0,2},{1,3},{2,4},{3,5},{4,6},{5,7},{6,0},{7,1},{8,10},{9,11},{10,... | collective-permute-start | bytes 221192 | tf_op jit(solution)/shard_map/ppermute | solution.py:364
  39.8 6.4 %collective-permute-start.6 = (f32[48,384]{1,0:T(8,128)S(1)}, f32[48,384]{1,0:T(8,128)S(1)}, u32[]{:S(2)}, u32[]{:S(2)}) collective-permute-start(f32[48,384]{1,0:T(8,128)S(1)} %add.82.use_0), channel_id=1, source_target_pairs={{0,4},{1,5},{2,6},{3,7},{4,0},{5,1},{6,2},{7,3},{8,12},{9,13},{10,... | collective-permute-start | bytes 221192 | tf_op jit(solution)/shard_map/ppermute | solution.py:364
  42.4 4.4 %collective-permute-start.7 = (f32[48,384]{1,0:T(8,128)S(1)}, f32[48,384]{1,0:T(8,128)S(1)}, u32[]{:S(2)}, u32[]{:S(2)}) collective-permute-start(f32[48,384]{1,0:T(8,128)S(1)} %add.82.use_0), channel_id=1, source_target_pairs={{0,6},{1,7},{2,0},{3,1},{4,2},{5,3},{6,4},{7,5},{8,14},{9,15},{10,... | collective-permute-start | bytes 221192 | tf_op jit(solution)/shard_map/ppermute | solution.py:364
  58.0 5.9 %collective-permute-start.10 = (f32[48,384]{1,0:T(8,128)S(1)}, f32[48,384]{1,0:T(8,128)S(1)}, u32[]{:S(2)}, u32[]{:S(2)}) collective-permute-start(f32[48,384]{1,0:T(8,128)S(1)} %add.83.use_0), channel_id=1, source_target_pairs={{0,4},{1,5},{2,6},{3,7},{4,0},{5,1},{6,2},{7,3},{8,12},{9,13},{10,... | collective-permute-start | bytes 221192 | tf_op jit(solution)/shard_map/ppermute | solution.py:364
  59.8 5.4 %collective-permute-start.11 = (f32[48,384]{1,0:T(8,128)S(1)}, f32[48,384]{1,0:T(8,128)S(1)}, u32[]{:S(2)}, u32[]{:S(2)}) collective-permute-start(f32[48,384]{1,0:T(8,128)S(1)} %add.83.use_0), channel_id=1, source_target_pairs={{0,6},{1,7},{2,0},{3,1},{4,2},{5,3},{6,4},{7,5},{8,14},{9,15},{10,... | collective-permute-start | bytes 221192 | tf_op jit(solution)/shard_map/ppermute | solution.py:364
  61.9 5.6 %collective-permute-start.9 = (f32[48,384]{1,0:T(8,128)S(1)}, f32[48,384]{1,0:T(8,128)S(1)}, u32[]{:S(2)}, u32[]{:S(2)}) collective-permute-start(f32[48,384]{1,0:T(8,128)S(1)} %add.83.use_0), channel_id=1, source_target_pairs={{0,2},{1,3},{2,4},{3,5},{4,6},{5,7},{6,0},{7,1},{8,10},{9,11},{10,... | collective-permute-start | bytes 221192 | tf_op jit(solution)/shard_map/ppermute | solution.py:364
  78.7 7.2 %collective-permute-start.13 = (f32[48,384]{1,0:T(8,128)S(1)}, f32[48,384]{1,0:T(8,128)S(1)}, u32[]{:S(2)}, u32[]{:S(2)}) collective-permute-start(f32[48,384]{1,0:T(8,128)S(1)} %add.84.use_0), channel_id=1, source_target_pairs={{0,2},{1,3},{2,4},{3,5},{4,6},{5,7},{6,0},{7,1},{8,10},{9,11},{10,... | collective-permute-start | bytes 221192 | tf_op jit(solution)/shard_map/ppermute | solution.py:364
  78.8 7.1 %collective-permute-start.14 = (f32[48,384]{1,0:T(8,128)S(1)}, f32[48,384]{1,0:T(8,128)S(1)}, u32[]{:S(2)}, u32[]{:S(2)}) collective-permute-start(f32[48,384]{1,0:T(8,128)S(1)} %add.84.use_0), channel_id=1, source_target_pairs={{0,4},{1,5},{2,6},{3,7},{4,0},{5,1},{6,2},{7,3},{8,12},{9,13},{10,... | collective-permute-start | bytes 221192 | tf_op jit(solution)/shard_map/ppermute | solution.py:364
  80.7 5.7 %collective-permute-start.15 = (f32[48,384]{1,0:T(8,128)S(1)}, f32[48,384]{1,0:T(8,128)S(1)}, u32[]{:S(2)}, u32[]{:S(2)}) collective-permute-start(f32[48,384]{1,0:T(8,128)S(1)} %add.84.use_0), channel_id=1, source_target_pairs={{0,6},{1,7},{2,0},{3,1},{4,2},{5,3},{6,4},{7,5},{8,14},{9,15},{10,... | collective-permute-start | bytes 221192 | tf_op jit(solution)/shard_map/ppermute | solution.py:364
  97.5 12.7 %collective-permute-start.26 = (f32[4,224,128]{2,1,0:T(8,128)S(1)}, f32[4,224,128]{2,1,0:T(8,128)S(1)}, u32[]{:S(2)}, u32[]{:S(2)}) collective-permute-start(f32[4,224,128]{2,1,0:T(8,128)S(1)} %get-tuple-element.85), channel_id=1, source_target_pairs={{0,32},{8,40},{16,48},{24,56},{32,64},{40,72},{48,80},{56,88},{64,... | collective-permute-start | bytes 1376264 | tf_op jit(solution)/shard_map/ppermute | solution.py:389
  99.1 11.2 %collective-permute-start.27 = (f32[4,224,128]{2,1,0:T(8,128)S(1)}, f32[4,224,128]{2,1,0:T(8,128)S(1)}, u32[]{:S(2)}, u32[]{:S(2)}) collective-permute-start(f32[4,224,128]{2,1,0:T(8,128)S(1)} %get-tuple-element.86), channel_id=1, source_target_pairs={{0,96},{8,104},{16,112},{24,120},{32,0},{40,8},{48,16},{56,24},{64... | collective-permute-start | bytes 1376264 | tf_op jit(solution)/shard_map/ppermute | solution.py:389
  100.7 13.9 %collective-permute-start.16 = (f32[4,224,128]{2,1,0:T(8,128)S(1)}, f32[4,224,128]{2,1,0:T(8,128)S(1)}, u32[]{:S(2)}, u32[]{:S(2)}) collective-permute-start(f32[4,224,128]{2,1,0:T(8,128)S(1)} %get-tuple-element.75), channel_id=1, source_target_pairs={{0,8},{8,16},{16,24},{24,0},{32,40},{40,48},{48,56},{56,32},{64,72... | collective-permute-start | bytes 1376264 | tf_op jit(solution)/shard_map/ppermute | solution.py:389
  102.4 12.2 %collective-permute-start.17 = (f32[4,224,128]{2,1,0:T(8,128)S(1)}, f32[4,224,128]{2,1,0:T(8,128)S(1)}, u32[]{:S(2)}, u32[]{:S(2)}) collective-permute-start(f32[4,224,128]{2,1,0:T(8,128)S(1)} %get-tuple-element.76), channel_id=1, source_target_pairs={{0,24},{8,0},{16,8},{24,16},{32,56},{40,32},{48,40},{56,48},{64,88... | collective-permute-start | bytes 1376264 | tf_op jit(solution)/shard_map/ppermute | solution.py:389
  111.3 21.6 %collective-permute-start.28 = (f32[2,4,224,128]{3,2,1,0:T(8,128)S(1)}, f32[2,4,224,128]{3,2,1,0:T(8,128)S(1)}, u32[]{:S(2)}, u32[]{:S(2)}) collective-permute-start(f32[2,4,224,128]{3,2,1,0:T(8,128)S(1)} %get-tuple-element.87), channel_id=1, source_target_pairs={{0,32},{8,40},{16,48},{24,56},{32,64},{40,72},{48,80},{56,88},{64,... | collective-permute-start | bytes 2752520 | tf_op jit(solution)/shard_map/ppermute | solution.py:389
  113.0 19.9 %collective-permute-start.29 = (f32[2,4,224,128]{3,2,1,0:T(8,128)S(1)}, f32[2,4,224,128]{3,2,1,0:T(8,128)S(1)}, u32[]{:S(2)}, u32[]{:S(2)}) collective-permute-start(f32[2,4,224,128]{3,2,1,0:T(8,128)S(1)} %get-tuple-element.88), channel_id=1, source_target_pairs={{0,96},{8,104},{16,112},{24,120},{32,0},{40,8},{48,16},{56,24},{64... | collective-permute-start | bytes 2752520 | tf_op jit(solution)/shard_map/ppermute | solution.py:389
  115.6 24.3 %collective-permute-start.18 = (f32[2,4,224,128]{3,2,1,0:T(8,128)S(1)}, f32[2,4,224,128]{3,2,1,0:T(8,128)S(1)}, u32[]{:S(2)}, u32[]{:S(2)}) collective-permute-start(f32[2,4,224,128]{3,2,1,0:T(8,128)S(1)} %get-tuple-element.77), channel_id=1, source_target_pairs={{0,8},{8,16},{16,24},{24,0},{32,40},{40,48},{48,56},{56,32},{64,72... | collective-permute-start | bytes 2752520 | tf_op jit(solution)/shard_map/ppermute | solution.py:389
  117.2 22.6 %collective-permute-start.19 = (f32[2,4,224,128]{3,2,1,0:T(8,128)S(1)}, f32[2,4,224,128]{3,2,1,0:T(8,128)S(1)}, u32[]{:S(2)}, u32[]{:S(2)}) collective-permute-start(f32[2,4,224,128]{3,2,1,0:T(8,128)S(1)} %get-tuple-element.78), channel_id=1, source_target_pairs={{0,24},{8,0},{16,8},{24,16},{32,56},{40,32},{48,40},{56,48},{64,88... | collective-permute-start | bytes 2752520 | tf_op jit(solution)/shard_map/ppermute | solution.py:389
  134.0 11.5 %collective-permute-start.30 = (f32[448,128]{1,0:T(8,128)S(1)}, f32[448,128]{1,0:T(8,128)S(1)}, u32[]{:S(2)}, u32[]{:S(2)}) collective-permute-start(f32[448,128]{1,0:T(8,128)S(1)} %get-tuple-element.90), channel_id=1, source_target_pairs={{0,8},{8,16},{16,24},{24,0},{32,40},{40,48},{48,56},{56,32},{64,72... | collective-permute-start | bytes 688136 | tf_op jit(solution)/shard_map/ppermute | solution.py:389
  135.6 12.0 %collective-permute-start.31 = (f32[448,128]{1,0:T(8,128)S(1)}, f32[448,128]{1,0:T(8,128)S(1)}, u32[]{:S(2)}, u32[]{:S(2)}) collective-permute-start(f32[448,128]{1,0:T(8,128)S(1)} %get-tuple-element.91), channel_id=1, source_target_pairs={{0,16},{8,24},{16,0},{24,8},{32,48},{40,56},{48,32},{56,40},{64,80... | collective-permute-start | bytes 688136 | tf_op jit(solution)/shard_map/ppermute | solution.py:389
  138.5 9.1 %collective-permute-start.32 = (f32[448,128]{1,0:T(8,128)S(1)}, f32[448,128]{1,0:T(8,128)S(1)}, u32[]{:S(2)}, u32[]{:S(2)}) collective-permute-start(f32[448,128]{1,0:T(8,128)S(1)} %get-tuple-element.92), channel_id=1, source_target_pairs={{0,24},{8,0},{16,8},{24,16},{32,56},{40,32},{48,40},{56,48},{64,88... | collective-permute-start | bytes 688136 | tf_op jit(solution)/shard_map/ppermute | solution.py:389
  140.9 10.1 %collective-permute-start.20 = (f32[448,128]{1,0:T(8,128)S(1)}, f32[448,128]{1,0:T(8,128)S(1)}, u32[]{:S(2)}, u32[]{:S(2)}) collective-permute-start(f32[448,128]{1,0:T(8,128)S(1)} %get-tuple-element.80), channel_id=1, source_target_pairs={{0,32},{8,40},{16,48},{24,56},{32,64},{40,72},{48,80},{56,88},{64,... | collective-permute-start | bytes 688136 | tf_op jit(solution)/shard_map/ppermute | solution.py:389
  142.1 9.9 %collective-permute-start.21 = (f32[448,128]{1,0:T(8,128)S(1)}, f32[448,128]{1,0:T(8,128)S(1)}, u32[]{:S(2)}, u32[]{:S(2)}) collective-permute-start(f32[448,128]{1,0:T(8,128)S(1)} %get-tuple-element.81), channel_id=1, source_target_pairs={{0,64},{8,72},{16,80},{24,88},{32,96},{40,104},{48,112},{56,120},{... | collective-permute-start | bytes 688136 | tf_op jit(solution)/shard_map/ppermute | solution.py:389
  145.4 6.5 %collective-permute-start.22 = (f32[448,128]{1,0:T(8,128)S(1)}, f32[448,128]{1,0:T(8,128)S(1)}, u32[]{:S(2)}, u32[]{:S(2)}) collective-permute-start(f32[448,128]{1,0:T(8,128)S(1)} %get-tuple-element.82), channel_id=1, source_target_pairs={{0,96},{8,104},{16,112},{24,120},{32,0},{40,8},{48,16},{56,24},{64... | collective-permute-start | bytes 688136 | tf_op jit(solution)/shard_map/ppermute | solution.py:389
  148.5 10.5 %collective-permute-start.33 = (f32[448,128]{1,0:T(8,128)S(1)}, f32[448,128]{1,0:T(8,128)S(1)}, u32[]{:S(2)}, u32[]{:S(2)}) collective-permute-start(f32[448,128]{1,0:T(8,128)S(1)} %get-tuple-element.93), channel_id=1, source_target_pairs={{0,24},{8,0},{16,8},{24,16},{32,56},{40,32},{48,40},{56,48},{64,88... | collective-permute-start | bytes 688136 | tf_op jit(solution)/shard_map/ppermute | solution.py:389
  150.4 9.9 %collective-permute-start.34 = (f32[448,128]{1,0:T(8,128)S(1)}, f32[448,128]{1,0:T(8,128)S(1)}, u32[]{:S(2)}, u32[]{:S(2)}) collective-permute-start(f32[448,128]{1,0:T(8,128)S(1)} %get-tuple-element.93), channel_id=1, source_target_pairs={{0,16},{8,24},{16,0},{24,8},{32,48},{40,56},{48,32},{56,40},{64,80... | collective-permute-start | bytes 688136 | tf_op jit(solution)/shard_map/ppermute | solution.py:389
  151.0 11.6 %collective-permute-start.35 = (f32[448,128]{1,0:T(8,128)S(1)}, f32[448,128]{1,0:T(8,128)S(1)}, u32[]{:S(2)}, u32[]{:S(2)}) collective-permute-start(f32[448,128]{1,0:T(8,128)S(1)} %get-tuple-element.93), channel_id=1, source_target_pairs={{0,8},{8,16},{16,24},{24,0},{32,40},{40,48},{48,56},{56,32},{64,72... | collective-permute-start | bytes 688136 | tf_op jit(solution)/shard_map/ppermute | solution.py:389
  152.8 10.0 %collective-permute-start.25 = (f32[448,128]{1,0:T(8,128)S(1)}, f32[448,128]{1,0:T(8,128)S(1)}, u32[]{:S(2)}, u32[]{:S(2)}) collective-permute-start(f32[448,128]{1,0:T(8,128)S(1)} %get-tuple-element.83), channel_id=1, source_target_pairs={{0,32},{8,40},{16,48},{24,56},{32,64},{40,72},{48,80},{56,88},{64,... | collective-permute-start | bytes 688136 | tf_op jit(solution)/shard_map/ppermute | solution.py:389
  154.8 8.7 %collective-permute-start.23 = (f32[448,128]{1,0:T(8,128)S(1)}, f32[448,128]{1,0:T(8,128)S(1)}, u32[]{:S(2)}, u32[]{:S(2)}) collective-permute-start(f32[448,128]{1,0:T(8,128)S(1)} %get-tuple-element.83), channel_id=1, source_target_pairs={{0,96},{8,104},{16,112},{24,120},{32,0},{40,8},{48,16},{56,24},{64... | collective-permute-start | bytes 688136 | tf_op jit(solution)/shard_map/ppermute | solution.py:389
  159.0 7.5 %collective-permute-start.24 = (f32[448,128]{1,0:T(8,128)S(1)}, f32[448,128]{1,0:T(8,128)S(1)}, u32[]{:S(2)}, u32[]{:S(2)}) collective-permute-start(f32[448,128]{1,0:T(8,128)S(1)} %get-tuple-element.83), channel_id=1, source_target_pairs={{0,64},{8,72},{16,80},{24,88},{32,96},{40,104},{48,112},{56,120},{... | collective-permute-start | bytes 688136 | tf_op jit(solution)/shard_map/ppermute | solution.py:389
  166.6 18.9 %collective-permute-start.36 = (f32[2,4,224,128]{3,2,1,0:T(8,128)S(1)}, f32[2,4,224,128]{3,2,1,0:T(8,128)S(1)}, u32[]{:S(2)}, u32[]{:S(2)}) collective-permute-start(f32[2,4,224,128]{3,2,1,0:T(8,128)S(1)} %pad_maximum_fusion.1.refs_5_), channel_id=1, source_target_pairs={{0,96},{8,104},{16,112},{24,120},{32,0},{40,8},{48,16},{56,24},{64... | collective-permute-start | bytes 2752520 | tf_op jit(solution)/shard_map/ppermute | solution.py:389
  167.3 20.4 %collective-permute-start.37 = (f32[2,4,224,128]{3,2,1,0:T(8,128)S(1)}, f32[2,4,224,128]{3,2,1,0:T(8,128)S(1)}, u32[]{:S(2)}, u32[]{:S(2)}) collective-permute-start(f32[2,4,224,128]{3,2,1,0:T(8,128)S(1)} %pad_maximum_fusion.1.refs_5_), channel_id=1, source_target_pairs={{0,32},{8,40},{16,48},{24,56},{32,64},{40,72},{48,80},{56,88},{64,... | collective-permute-start | bytes 2752520 | tf_op jit(solution)/shard_map/ppermute | solution.py:389
  168.7 24.0 %collective-permute-start.46 = (f32[2,4,224,128]{3,2,1,0:T(8,128)S(1)}, f32[2,4,224,128]{3,2,1,0:T(8,128)S(1)}, u32[]{:S(2)}, u32[]{:S(2)}) collective-permute-start(f32[2,4,224,128]{3,2,1,0:T(8,128)S(1)} %pad_maximum_fusion.refs_0_), channel_id=1, source_target_pairs={{0,8},{8,16},{16,24},{24,0},{32,40},{40,48},{48,56},{56,32},{64,72... | collective-permute-start | bytes 2752520 | tf_op jit(solution)/shard_map/ppermute | solution.py:389
  170.6 3.6 %collective-permute-start.39 = (f32[8,128]{1,0:T(8,128)S(1)}, f32[8,128]{1,0:T(8,128)S(1)}, u32[]{:S(2)}, u32[]{:S(2)}) collective-permute-start(f32[8,128]{1,0:T(8,128)S(1)} %add.91), channel_id=1, source_target_pairs={{0,2},{1,3},{2,0},{3,1},{4,6},{5,7},{6,4},{7,5},{8,10},{9,11},{10,... | collective-permute-start | bytes 12296 | tf_op jit(solution)/shard_map/ppermute | solution.py:372
  171.0 22.5 %collective-permute-start.45 = (f32[2,4,224,128]{3,2,1,0:T(8,128)S(1)}, f32[2,4,224,128]{3,2,1,0:T(8,128)S(1)}, u32[]{:S(2)}, u32[]{:S(2)}) collective-permute-start(f32[2,4,224,128]{3,2,1,0:T(8,128)S(1)} %pad_maximum_fusion.refs_0_), channel_id=1, source_target_pairs={{0,24},{8,0},{16,8},{24,16},{32,56},{40,32},{48,40},{56,48},{64,88... | collective-permute-start | bytes 2752520 | tf_op jit(solution)/shard_map/ppermute | solution.py:389
  174.3 8.1 %collective-permute-start.40 = (f32[8,128]{1,0:T(8,128)S(1)}, f32[8,128]{1,0:T(8,128)S(1)}, u32[]{:S(2)}, u32[]{:S(2)}) collective-permute-start(f32[8,128]{1,0:T(8,128)S(1)} %add.92), channel_id=1, source_target_pairs={{0,6},{1,7},{2,4},{3,5},{4,2},{5,3},{6,0},{7,1},{8,14},{9,15},{10,... | collective-permute-start | bytes 12296 | tf_op jit(solution)/shard_map/ppermute | solution.py:372
  187.7 27.1 %collective-permute-start.49 = (f32[4,224,128]{2,1,0:T(8,128)S(1)}, f32[4,224,128]{2,1,0:T(8,128)S(1)}, u32[]{:S(2)}, u32[]{:S(2)}) collective-permute-start(f32[4,224,128]{2,1,0:T(8,128)S(1)} %slice_bitcast_fusion.3), channel_id=1, source_target_pairs={{0,32},{8,40},{16,48},{24,56},{32,64},{40,72},{48,80},{56,88},{64,... | collective-permute-start | bytes 1376264 | tf_op jit(solution)/shard_map/ppermute | solution.py:389
  188.9 25.9 %collective-permute-start.50 = (f32[4,224,128]{2,1,0:T(8,128)S(1)}, f32[4,224,128]{2,1,0:T(8,128)S(1)}, u32[]{:S(2)}, u32[]{:S(2)}) collective-permute-start(f32[4,224,128]{2,1,0:T(8,128)S(1)} %slice_bitcast_fusion.2), channel_id=1, source_target_pairs={{0,96},{8,104},{16,112},{24,120},{32,0},{40,8},{48,16},{56,24},{64... | collective-permute-start | bytes 1376264 | tf_op jit(solution)/shard_map/ppermute | solution.py:389
  191.1 6.2 %collective-permute-start.41 = (f32[8,128]{1,0:T(8,128)S(1)}, f32[8,128]{1,0:T(8,128)S(1)}, u32[]{:S(2)}, u32[]{:S(2)}) collective-permute-start(f32[8,128]{1,0:T(8,128)S(1)} %add.93), channel_id=1, source_target_pairs={{0,8},{8,0},{16,24},{24,16},{32,40},{40,32},{48,56},{56,48},{64,72... | collective-permute-start | bytes 12296 | tf_op jit(solution)/shard_map/ppermute | solution.py:379
  192.8 22.1 %collective-permute-start.47 = (f32[4,224,128]{2,1,0:T(8,128)S(1)}, f32[4,224,128]{2,1,0:T(8,128)S(1)}, u32[]{:S(2)}, u32[]{:S(2)}) collective-permute-start(f32[4,224,128]{2,1,0:T(8,128)S(1)} %slice_bitcast_fusion.1), channel_id=1, source_target_pairs={{0,8},{8,16},{16,24},{24,0},{32,40},{40,48},{48,56},{56,32},{64,72... | collective-permute-start | bytes 1376264 | tf_op jit(solution)/shard_map/ppermute | solution.py:389
  193.6 21.3 %collective-permute-start.48 = (f32[4,224,128]{2,1,0:T(8,128)S(1)}, f32[4,224,128]{2,1,0:T(8,128)S(1)}, u32[]{:S(2)}, u32[]{:S(2)}) collective-permute-start(f32[4,224,128]{2,1,0:T(8,128)S(1)} %slice_bitcast_fusion), channel_id=1, source_target_pairs={{0,24},{8,0},{16,8},{24,16},{32,56},{40,32},{48,40},{56,48},{64,88... | collective-permute-start | bytes 1376264 | tf_op jit(solution)/shard_map/ppermute | solution.py:389
  197.4 9.0 %collective-permute-start.42 = (f32[8,128]{1,0:T(8,128)S(1)}, f32[8,128]{1,0:T(8,128)S(1)}, u32[]{:S(2)}, u32[]{:S(2)}) collective-permute-start(f32[8,128]{1,0:T(8,128)S(1)} %add.94), channel_id=1, source_target_pairs={{0,24},{8,16},{16,8},{24,0},{32,56},{40,48},{48,40},{56,32},{64,88... | collective-permute-start | bytes 12296 | tf_op jit(solution)/shard_map/ppermute | solution.py:379
  206.4 3.6 %collective-permute-start.43 = (f32[8,128]{1,0:T(8,128)S(1)}, f32[8,128]{1,0:T(8,128)S(1)}, u32[]{:S(2)}, u32[]{:S(2)}) collective-permute-start(f32[8,128]{1,0:T(8,128)S(1)} %add.95), channel_id=1, source_target_pairs={{0,32},{8,40},{16,48},{24,56},{32,0},{40,8},{48,16},{56,24},{64,96... | collective-permute-start | bytes 12296 | tf_op jit(solution)/shard_map/ppermute | solution.py:379
  210.0 4.8 %collective-permute-start.44 = (f32[8,128]{1,0:T(8,128)S(1)}, f32[8,128]{1,0:T(8,128)S(1)}, u32[]{:S(2)}, u32[]{:S(2)}) collective-permute-start(f32[8,128]{1,0:T(8,128)S(1)} %add.96), channel_id=1, source_target_pairs={{0,96},{8,104},{16,112},{24,120},{32,64},{40,72},{48,80},{56,88},{... | collective-permute-start | bytes 12296 | tf_op jit(solution)/shard_map/ppermute | solution.py:379
  (10 other events, 113.4 us)

commit v5 on v4

--- a/solution.py
+++ b/solution.py
@@ -68,6 +68,7 @@
     crew_scr,
     used_scr,
     block_scr,
+    dual_scr,
 ):
     step = pl.program_id(0)
     count = pl.num_programs(0)
@@ -78,7 +79,9 @@
         block_scr[...] = jnp.zeros_like(block_scr)
         ids = lax.broadcasted_iota(jnp.int32, row_to_veh.shape, 0)
         row_to_veh[...] = (ids == row_ref[...]).astype(f32).astype(bf16)
-        crew_scr[:, 0, :] = step_size * exact_dot(dual_ref[...], row_to_veh[...])
+        dual_scr[...] = jnp.zeros_like(dual_scr)
+        dual_scr[:, : dual_ref.shape[1]] = dual_ref[...]
+        crew_scr[:, 0, :] = step_size * exact_dot(dual_scr[...], row_to_veh[...])
         used_scr[48:56] = jnp.zeros_like(used_scr[48:56])
         c = coef_ref[...].astype(f32).T
         coef_t_ref[...] = c
@@ -483,7 +486,7 @@
                 pl.BlockSpec((1, vehicles, n), lambda s, b: (b[2 * s + 1], 0, 0)),
                 pl.BlockSpec((2, n, n), lambda s, *_: (s, 0, 0)),
                 whole(vehicles, n),
-                whole(count, CREW_PAD),
+                whole(count, crews),
                 whole(1, vehicles),
             ],
             out_specs=[vm] * 5,
@@ -491,6 +494,7 @@
                 pltpu.VMEM((16, 1, vehicles), f32),
                 pltpu.VMEM((56, 8, vehicles), f32),
                 pltpu.VMEM((2 * n, 2 * n), bf16),
+                pltpu.VMEM((count, CREW_PAD), f32),
             ],
         ),
         out_shape=[
@@ -511,7 +515,7 @@
         in_hbm(anchor),
         in_hbm(hessian),
         in_hbm(usage_coef),
-        dual,
+        crew_dual,
         crew_row[None, :],
     )
 
@@ -669,7 +673,6 @@
     pack_a, pack_b, spread = lax.optimization_barrier((pack_a, pack_b, sum(spreads)))
     near_a, near_b = gather_near(pack_a, "x"), gather_near(pack_b, "y")
     spread = spread_over_veh(spread)
-    near_b, spread = lax.optimization_barrier((near_b, spread))
     spread_total = sum_over_scen(spread)
     means = gather_far(*near_a, "x") + gather_far(*near_b, "y")
     entries = vehicles * lax.axis_size("veh") * n

time: 226 us -> 224 us (level); the launches traced: 223 us -> 224 us
  waiting for transfers between devices: 75.3 us -> 78.2 us
    ppermute x28, starting transfers between devices: 45 us -> 48.1 us  [shift(): return lax.ppermute(value, 'scen', pairs)]
    ppermute x3, starting transfers between devices: 6.86 us -> 4.25 us  [spread_over_veh(): value = value + lax.ppermute(value, 'veh', veh_pairs(kind))]
  transfers between devices with their start and end apart: 51 -> 51, of which waited for: 34 -> 29; matrix products, arithmetic and copies ran while one was open for 1% -> 1% of each run, Pallas kernels for 3% -> 3%
where the time goes in v5:
time: 224 us
  waiting for transfers between devices  78.2 us (35%)
  starting transfers between devices  74.2 us (33%)
  Pallas kernels  66.5 us (30%)
  local copies, waits for them, and re-layouts  2.47 us (1%)
    ppermute x28, starting transfers between devices, shift(): return lax.ppermute(value, 'scen', pairs)  48.1 us
    ppermute x28, waiting for transfers between devices, shift(): return lax.ppermute(value, 'scen', pairs)  39.2 us
    pallas_call x3, Pallas kernels, shards(): pl.pallas_call(middle_kernel, in_specs=[vm] * 12, out_specs=[vm] * 3, out...  29.6 us
    ppermute x12, starting transfers between devices, usage_exchange(): lax.ppermute(value, 'veh', veh_pairs({z: (z + by) % 4 for z in range(4)}))  18.7 us
    ppermute x12, waiting for transfers between devices, usage_exchange(): lax.ppermute(value, 'veh', veh_pairs({z: (z + by) % 4 for z in range(4)}))  16.5 us
    ppermute x4, waiting for transfers between devices, sum_over_scen(): value = value + lax.ppermute(value, 'scen', scen_pairs(pair, axis))  13.7 us
    pallas_call x1, Pallas kernels, shards(): pl.pallas_call(first_kernel, grid_spec=pltpu.PrefetchScalarGridSpec(num_s...  13 us
    pallas_call x1, Pallas kernels, shards(): pl.pallas_call(last_kernel, grid_spec=pltpu.PrefetchScalarGridSpec(num_sc...  10.4 us
  transfers between devices with their start and end apart: 51, of which 29 were waited for; matrix products, arithmetic and copies ran while one was open for 1% of the time, Pallas kernels for 3%

profile of v5, /device:TPU:0, one launch (start us, length us, event | category | flops | bytes accessed | tf_op | source)
XLA Modules:
  0.0 224.1 jit_solution(16256064195285410294)
XLA Ops:
  2.8 13.0 %first_steps.1 = (f32[16,128,896]{2,1,0:T(8,128)S(1)}, f32[16,128,896]{2,1,0:T(8,128)S(1)}, f32[128,896]{1,0:T(8,128)S(1)}, bf16[384,896]{1,0:T(8,128)(2,1)S(1)}, f32[56,384]{1,0:T(8,128)S(1)}) custom-call(s32[16]{0:T(128)S(1)} %dynamic-slice_bitcast_fusion.bundles, bf16[16,896,128]{2,1,0:T(8,128)(2,1)} %start_ref.1, bf16[16,896,128]{2,1,0:T(8,128)(2,1)} %cost_ref.1, ...), custom_call_target="tpu_custom_call" | custom-call | tf_op jit(solution)/shard_map/first_steps/pallas_call | solution.py:476
  17.2 2.1 collective-permute-start.1
  19.2 3.6 %collective-permute-start.2 = (f32[56,384]{1,0:T(8,128)S(1)}, f32[56,384]{1,0:T(8,128)S(1)}, u32[]{:S(2)}, u32[]{:S(2)}) collective-permute-start(f32[56,384]{1,0:T(8,128)S(1)} %add.78.use_0), channel_id=1, source_target_pairs={{0,4},{1,5},{2,6},{3,7},{4,0},{5,1},{6,2},{7,3},{8,12},{9,13},{10,... | collective-permute-start | bytes 258056 | tf_op jit(solution)/shard_map/ppermute | solution.py:367
  24.2 3.0 %collective-permute-done.2.use_2 = f32[56,384]{1,0:T(8,128)S(1)} collective-permute-done((f32[56,384]{1,0:T(8,128)S(1)}, f32[56,384]{1,0:T(8,128)S(1)}, u32[]{:S(2)}, u32[]{:S(2)}) %collective-permute-start.2) | collective-permute-done | bytes 86048 | tf_op jit(solution)/shard_map/ppermute | solution.py:367
  27.3 9.9 %three_steps.3 = (f32[16,128,896]{2,1,0:T(8,128)S(1)}, f32[48,384]{1,0:T(8,128)S(1)}, f32[16,384]{1,0:T(8,128)S(1)}) custom-call(f32[16,128,896]{2,1,0:T(8,128)S(1)} %get-tuple-element.54.partial_ref, f32[16,128,896]{2,1,0:T(8,128)S(1)} %get-tuple-element.55.linear_ref, bf16[16,128,128]{2,1,0:T(8,128)(2,1)S(1)} %copy-done, ...), custom_call_target="tpu_custom_call", output_to_operand_aliasing={{0}: (0, {})} | custom-call | tf_op jit(solution)/shard_map/three_steps/pallas_call | solution.py:525
  39.8 2.5 %collective-permute-start.6 = (f32[48,384]{1,0:T(8,128)S(1)}, f32[48,384]{1,0:T(8,128)S(1)}, u32[]{:S(2)}, u32[]{:S(2)}) collective-permute-start(f32[48,384]{1,0:T(8,128)S(1)} %add.82.use_0), channel_id=1, source_target_pairs={{0,4},{1,5},{2,6},{3,7},{4,0},{5,1},{6,2},{7,3},{8,12},{9,13},{10,... | collective-permute-start | bytes 221192 | tf_op jit(solution)/shard_map/ppermute | solution.py:367
  44.5 1.6 collective-permute-done.6.use_2
  46.7 9.9 %three_steps.4 = (f32[16,128,896]{2,1,0:T(8,128)S(1)}, f32[48,384]{1,0:T(8,128)S(1)}, f32[16,384]{1,0:T(8,128)S(1)}) custom-call(f32[16,128,896]{2,1,0:T(8,128)S(1)} %get-tuple-element.59.partial_ref, f32[16,128,896]{2,1,0:T(8,128)S(1)} %get-tuple-element.55.linear_ref, bf16[16,128,128]{2,1,0:T(8,128)(2,1)S(1)} %copy-done, ...), custom_call_target="tpu_custom_call", output_to_operand_aliasing={{0}: (0, {})} | custom-call | tf_op jit(solution)/shard_map/three_steps/pallas_call | solution.py:525
  57.9 1.8 collective-permute-start.10
  59.7 2.1 collective-permute-start.11
  61.9 2.0 collective-permute-done.10.use_2
  65.2 2.2 collective-permute-done.9.use_1
  67.4 9.9 %three_steps.5 = (f32[16,128,896]{2,1,0:T(8,128)S(1)}, f32[48,384]{1,0:T(8,128)S(1)}, f32[16,384]{1,0:T(8,128)S(1)}) custom-call(f32[16,128,896]{2,1,0:T(8,128)S(1)} %get-tuple-element.62.partial_ref, f32[16,128,896]{2,1,0:T(8,128)S(1)} %get-tuple-element.55.linear_ref, bf16[16,128,128]{2,1,0:T(8,128)(2,1)S(1)} %copy-done, ...), custom_call_target="tpu_custom_call", output_to_operand_aliasing={{0}: (0, {})} | custom-call | tf_op jit(solution)/shard_map/three_steps/pallas_call | solution.py:525
  78.7 1.9 collective-permute-start.14
  81.9 3.9 %collective-permute-done.13.use_1 = f32[48,384]{1,0:T(8,128)S(1)} collective-permute-done((f32[48,384]{1,0:T(8,128)S(1)}, f32[48,384]{1,0:T(8,128)S(1)}, u32[]{:S(2)}, u32[]{:S(2)}) %collective-permute-start.13) | collective-permute-done | bytes 73760 | tf_op jit(solution)/shard_map/ppermute | solution.py:367
  86.4 10.4 %last_step.1 = (bf16[16,896,128]{2,1,0:T(8,128)(2,1)}, f32[16,896,128]{2,1,0:T(8,128)S(1)}, f32[16,448,128]{2,1,0:T(8,128)S(1)}, f32[16,448,128]{2,1,0:T(8,128)S...) custom-call(s32[2,16]{1,0:T(2,128)S(1)} %pad_add_fusion.slots, ...), custom_call_target="tpu_custom_call" | custom-call | tf_op jit(solution)/shard_map/last_step/pallas_call | solution.py:585
  96.8 1.5 collective-permute-start.26
  98.2 1.8 collective-permute-start.27
  101.5 1.9 collective-permute-start.17
  103.5 6.1 %collective-permute-done.26.up_in = f32[4,224,128]{2,1,0:T(8,128)S(1)} collective-permute-done((f32[4,224,128]{2,1,0:T(8,128)S(1)}, f32[4,224,128]{2,1,0:T(8,128)S(1)}, u32[]{:S(2)}, u32[]{:S(2)}) %collective-permute-start.26) | collective-permute-done | bytes 458784 | tf_op jit(solution)/shard_map/ppermute | solution.py:392
  110.6 1.6 collective-permute-start.28
  112.2 1.7 collective-permute-start.29
  114.9 1.5 collective-permute-start.18
  116.4 1.8 collective-permute-start.19
  118.2 14.3 %collective-permute-done.28.up_in = f32[2,4,224,128]{3,2,1,0:T(8,128)S(1)} collective-permute-done((f32[2,4,224,128]{3,2,1,0:T(8,128)S(1)}, f32[2,4,224,128]{3,2,1,0:T(8,128)S(1)}, u32[]{:S(2)}, u32[]{:S(2)}) %collective-permute-start.28) | collective-permute-done | bytes 917536 | tf_op jit(solution)/shard_map/ppermute | solution.py:392
  133.5 1.5 collective-permute-start.30
  135.0 3.0 %collective-permute-start.31 = (f32[448,128]{1,0:T(8,128)S(1)}, f32[448,128]{1,0:T(8,128)S(1)}, u32[]{:S(2)}, u32[]{:S(2)}) collective-permute-start(f32[448,128]{1,0:T(8,128)S(1)} %get-tuple-element.87), channel_id=1, source_target_pairs={{0,16},{8,24},{16,0},{24,8},{32,48},{40,56},{48,32},{56,40},{64,80... | collective-permute-start | bytes 688136 | tf_op jit(solution)/shard_map/ppermute | solution.py:392
  141.3 3.4 %collective-permute-start.21 = (f32[448,128]{1,0:T(8,128)S(1)}, f32[448,128]{1,0:T(8,128)S(1)}, u32[]{:S(2)}, u32[]{:S(2)}) collective-permute-start(f32[448,128]{1,0:T(8,128)S(1)} %get-tuple-element.77), channel_id=1, source_target_pairs={{0,64},{8,72},{16,80},{24,88},{32,96},{40,104},{48,112},{56,120},{... | collective-permute-start | bytes 688136 | tf_op jit(solution)/shard_map/ppermute | solution.py:392
  144.7 1.5 collective-permute-start.22
  148.0 1.9 collective-permute-start.33
  152.1 1.6 collective-permute-start.25
  153.7 1.7 collective-permute-start.23
  155.4 3.2 %collective-permute-done.33 = f32[448,128]{1,0:T(8,128)S(1)} collective-permute-done((f32[448,128]{1,0:T(8,128)S(1)}, f32[448,128]{1,0:T(8,128)S(1)}, u32[]{:S(2)}, u32[]{:S(2)}) %collective-permute-start.33) | collective-permute-done | bytes 229408 | tf_op jit(solution)/shard_map/ppermute | solution.py:392
  159.9 2.1 collective-permute-done.35
  162.2 4.0 %collective-permute-done.24 = f32[448,128]{1,0:T(8,128)S(1)} collective-permute-done((f32[448,128]{1,0:T(8,128)S(1)}, f32[448,128]{1,0:T(8,128)S(1)}, u32[]{:S(2)}, u32[]{:S(2)}) %collective-permute-start.24) | collective-permute-done | bytes 229408 | tf_op jit(solution)/shard_map/ppermute | solution.py:392
  166.6 3.5 %collective-permute-start.43 = (f32[2,4,224,128]{3,2,1,0:T(8,128)S(1)}, f32[2,4,224,128]{3,2,1,0:T(8,128)S(1)}, u32[]{:S(2)}, u32[]{:S(2)}) collective-permute-start(f32[2,4,224,128]{3,2,1,0:T(8,128)S(1)} %pad_maximum_fusion.refs_0_), channel_id=1, source_target_pairs={{0,24},{8,0},{16,8},{24,16},{32,56},{40,32},{48,40},{56,48},{64,88... | collective-permute-start | bytes 2752520 | tf_op jit(solution)/shard_map/ppermute | solution.py:392
  171.6 3.2 %collective-permute-done.37 = f32[8,128]{1,0:T(8,128)S(1)} collective-permute-done((f32[8,128]{1,0:T(8,128)S(1)}, f32[8,128]{1,0:T(8,128)S(1)}, u32[]{:S(2)}, u32[]{:S(2)}) %collective-permute-start.37) | collective-permute-done | bytes 4128 | tf_op jit(solution)/shard_map/ppermute | solution.py:375
  174.9 3.9 %collective-permute-start.38 = (f32[8,128]{1,0:T(8,128)S(1)}, f32[8,128]{1,0:T(8,128)S(1)}, u32[]{:S(2)}, u32[]{:S(2)}) collective-permute-start(f32[8,128]{1,0:T(8,128)S(1)} %add.92), channel_id=1, source_target_pairs={{0,6},{1,7},{2,4},{3,5},{4,2},{5,3},{6,0},{7,1},{8,14},{9,15},{10,... | collective-permute-start | bytes 12296 | tf_op jit(solution)/shard_map/ppermute | solution.py:375
  178.7 3.2 %collective-permute-start.47 = (f32[2,4,224,128]{3,2,1,0:T(8,128)S(1)}, f32[2,4,224,128]{3,2,1,0:T(8,128)S(1)}, u32[]{:S(2)}, u32[]{:S(2)}) collective-permute-start(f32[2,4,224,128]{3,2,1,0:T(8,128)S(1)} %pad_maximum_fusion.1.refs_5_), channel_id=1, source_target_pairs={{0,96},{8,104},{16,112},{24,120},{32,0},{40,8},{48,16},{56,24},{64... | collective-permute-start | bytes 2752520 | tf_op jit(solution)/shard_map/ppermute | solution.py:392
  182.0 4.3 %collective-permute-done.39 = f32[8,128]{1,0:T(8,128)S(1)} collective-permute-done((f32[8,128]{1,0:T(8,128)S(1)}, f32[8,128]{1,0:T(8,128)S(1)}, u32[]{:S(2)}, u32[]{:S(2)}) %collective-permute-start.39) | collective-permute-done | bytes 4128 | tf_op jit(solution)/shard_map/ppermute | solution.py:382
  188.8 2.2 collective-permute-start.46
  191.0 2.6 %collective-permute-start.49 = (f32[4,224,128]{2,1,0:T(8,128)S(1)}, f32[4,224,128]{2,1,0:T(8,128)S(1)}, u32[]{:S(2)}, u32[]{:S(2)}) collective-permute-start(f32[4,224,128]{2,1,0:T(8,128)S(1)} %slice_bitcast_fusion.1), channel_id=1, source_target_pairs={{0,32},{8,40},{16,48},{24,56},{32,64},{40,72},{48,80},{56,88},{64,... | collective-permute-start | bytes 1376264 | tf_op jit(solution)/shard_map/ppermute | solution.py:392
  193.6 7.2 %collective-permute-done.47.refs_6_ = f32[2,4,224,128]{3,2,1,0:T(8,128)S(1)} collective-permute-done((f32[2,4,224,128]{3,2,1,0:T(8,128)S(1)}, f32[2,4,224,128]{3,2,1,0:T(8,128)S(1)}, u32[]{:S(2)}, u32[]{:S(2)}) %collective-permute-start.47) | collective-permute-done | bytes 917536 | tf_op jit(solution)/shard_map/ppermute | solution.py:392
  200.8 3.8 %collective-permute-start.50 = (f32[4,224,128]{2,1,0:T(8,128)S(1)}, f32[4,224,128]{2,1,0:T(8,128)S(1)}, u32[]{:S(2)}, u32[]{:S(2)}) collective-permute-start(f32[4,224,128]{2,1,0:T(8,128)S(1)} %slice_bitcast_fusion), channel_id=1, source_target_pairs={{0,96},{8,104},{16,112},{24,120},{32,0},{40,8},{48,16},{56,24},{64... | collective-permute-start | bytes 1376264 | tf_op jit(solution)/shard_map/ppermute | solution.py:392
  204.7 6.8 %collective-permute-done.41 = f32[8,128]{1,0:T(8,128)S(1)} collective-permute-done((f32[8,128]{1,0:T(8,128)S(1)}, f32[8,128]{1,0:T(8,128)S(1)}, u32[]{:S(2)}, u32[]{:S(2)}) %collective-permute-start.41) | collective-permute-done | bytes 4128 | tf_op jit(solution)/shard_map/ppermute | solution.py:382
  211.5 1.5 collective-permute-start.42
  213.7 2.6 %collective-permute-done.42 = f32[8,128]{1,0:T(8,128)S(1)} collective-permute-done((f32[8,128]{1,0:T(8,128)S(1)}, f32[8,128]{1,0:T(8,128)S(1)}, u32[]{:S(2)}, u32[]{:S(2)}) %collective-permute-start.42) | collective-permute-done | bytes 4128 | tf_op jit(solution)/shard_map/ppermute | solution.py:382
  216.3 7.8 %new_price.1 = (bf16[16,896,128]{2,1,0:T(8,128)(2,1)}, f32[1,1]{1,0:T(1,128)}) custom-call(s32[2,16]{1,0:T(2,128)S(1)} %pad_add_fusion.slots, f32[16,896,128]{2,1,0:T(8,128)S(1)} %get-tuple-element.69.roster_ref, bf16[16,896,128]{2,1,0:T(8,128)(2,1)} %price_ref.3, f32[8,128]{1,0:T(8,128)S(1)} %add.97.spread_ref, f32[1,256]{1,0:T(1,128)S(1)} %bitcast.36, ...), custom_call_target="tpu_custom_call" | custom-call | tf_op jit(solution)/shard_map/new_price/pallas_call | solution.py:681
  (124 shorter events, 35.0 us)
Async XLA Ops:
  15.8 1.4 collective-permute-start
  17.2 7.0 %collective-permute-start.1 = (f32[56,384]{1,0:T(8,128)S(1)}, f32[56,384]{1,0:T(8,128)S(1)}, u32[]{:S(2)}, u32[]{:S(2)}) collective-permute-start(f32[56,384]{1,0:T(8,128)S(1)} %add.78.use_0), channel_id=1, source_target_pairs={{0,2},{1,3},{2,4},{3,5},{4,6},{5,7},{6,0},{7,1},{8,10},{9,11},{10,... | collective-permute-start | bytes 258056 | tf_op jit(solution)/shard_map/ppermute | solution.py:367
  19.2 8.0 %collective-permute-start.2 = (f32[56,384]{1,0:T(8,128)S(1)}, f32[56,384]{1,0:T(8,128)S(1)}, u32[]{:S(2)}, u32[]{:S(2)}) collective-permute-start(f32[56,384]{1,0:T(8,128)S(1)} %add.78.use_0), channel_id=1, source_target_pairs={{0,4},{1,5},{2,6},{3,7},{4,0},{5,1},{6,2},{7,3},{8,12},{9,13},{10,... | collective-permute-start | bytes 258056 | tf_op jit(solution)/shard_map/ppermute | solution.py:367
  22.8 4.5 %collective-permute-start.3 = (f32[56,384]{1,0:T(8,128)S(1)}, f32[56,384]{1,0:T(8,128)S(1)}, u32[]{:S(2)}, u32[]{:S(2)}) collective-permute-start(f32[56,384]{1,0:T(8,128)S(1)} %add.78.use_0), channel_id=1, source_target_pairs={{0,6},{1,7},{2,0},{3,1},{4,2},{5,3},{6,4},{7,5},{8,14},{9,15},{10,... | collective-permute-start | bytes 258056 | tf_op jit(solution)/shard_map/ppermute | solution.py:367
  38.5 6.0 %collective-permute-start.5 = (f32[48,384]{1,0:T(8,128)S(1)}, f32[48,384]{1,0:T(8,128)S(1)}, u32[]{:S(2)}, u32[]{:S(2)}) collective-permute-start(f32[48,384]{1,0:T(8,128)S(1)} %add.82.use_0), channel_id=1, source_target_pairs={{0,2},{1,3},{2,4},{3,5},{4,6},{5,7},{6,0},{7,1},{8,10},{9,11},{10,... | collective-permute-start | bytes 221192 | tf_op jit(solution)/shard_map/ppermute | solution.py:367
  39.8 6.4 %collective-permute-start.6 = (f32[48,384]{1,0:T(8,128)S(1)}, f32[48,384]{1,0:T(8,128)S(1)}, u32[]{:S(2)}, u32[]{:S(2)}) collective-permute-start(f32[48,384]{1,0:T(8,128)S(1)} %add.82.use_0), channel_id=1, source_target_pairs={{0,4},{1,5},{2,6},{3,7},{4,0},{5,1},{6,2},{7,3},{8,12},{9,13},{10,... | collective-permute-start | bytes 221192 | tf_op jit(solution)/shard_map/ppermute | solution.py:367
  42.3 4.4 %collective-permute-start.7 = (f32[48,384]{1,0:T(8,128)S(1)}, f32[48,384]{1,0:T(8,128)S(1)}, u32[]{:S(2)}, u32[]{:S(2)}) collective-permute-start(f32[48,384]{1,0:T(8,128)S(1)} %add.82.use_0), channel_id=1, source_target_pairs={{0,6},{1,7},{2,0},{3,1},{4,2},{5,3},{6,4},{7,5},{8,14},{9,15},{10,... | collective-permute-start | bytes 221192 | tf_op jit(solution)/shard_map/ppermute | solution.py:367
  57.9 6.0 %collective-permute-start.10 = (f32[48,384]{1,0:T(8,128)S(1)}, f32[48,384]{1,0:T(8,128)S(1)}, u32[]{:S(2)}, u32[]{:S(2)}) collective-permute-start(f32[48,384]{1,0:T(8,128)S(1)} %add.83.use_0), channel_id=1, source_target_pairs={{0,4},{1,5},{2,6},{3,7},{4,0},{5,1},{6,2},{7,3},{8,12},{9,13},{10,... | collective-permute-start | bytes 221192 | tf_op jit(solution)/shard_map/ppermute | solution.py:367
  59.7 5.4 %collective-permute-start.11 = (f32[48,384]{1,0:T(8,128)S(1)}, f32[48,384]{1,0:T(8,128)S(1)}, u32[]{:S(2)}, u32[]{:S(2)}) collective-permute-start(f32[48,384]{1,0:T(8,128)S(1)} %add.83.use_0), channel_id=1, source_target_pairs={{0,6},{1,7},{2,0},{3,1},{4,2},{5,3},{6,4},{7,5},{8,14},{9,15},{10,... | collective-permute-start | bytes 221192 | tf_op jit(solution)/shard_map/ppermute | solution.py:367
  61.8 5.6 %collective-permute-start.9 = (f32[48,384]{1,0:T(8,128)S(1)}, f32[48,384]{1,0:T(8,128)S(1)}, u32[]{:S(2)}, u32[]{:S(2)}) collective-permute-start(f32[48,384]{1,0:T(8,128)S(1)} %add.83.use_0), channel_id=1, source_target_pairs={{0,2},{1,3},{2,4},{3,5},{4,6},{5,7},{6,0},{7,1},{8,10},{9,11},{10,... | collective-permute-start | bytes 221192 | tf_op jit(solution)/shard_map/ppermute | solution.py:367
  77.3 1.3 collective-permute-start.12
  78.6 7.2 %collective-permute-start.13 = (f32[48,384]{1,0:T(8,128)S(1)}, f32[48,384]{1,0:T(8,128)S(1)}, u32[]{:S(2)}, u32[]{:S(2)}) collective-permute-start(f32[48,384]{1,0:T(8,128)S(1)} %add.84.use_0), channel_id=1, source_target_pairs={{0,2},{1,3},{2,4},{3,5},{4,6},{5,7},{6,0},{7,1},{8,10},{9,11},{10,... | collective-permute-start | bytes 221192 | tf_op jit(solution)/shard_map/ppermute | solution.py:367
  78.7 7.1 %collective-permute-start.14 = (f32[48,384]{1,0:T(8,128)S(1)}, f32[48,384]{1,0:T(8,128)S(1)}, u32[]{:S(2)}, u32[]{:S(2)}) collective-permute-start(f32[48,384]{1,0:T(8,128)S(1)} %add.84.use_0), channel_id=1, source_target_pairs={{0,4},{1,5},{2,6},{3,7},{4,0},{5,1},{6,2},{7,3},{8,12},{9,13},{10,... | collective-permute-start | bytes 221192 | tf_op jit(solution)/shard_map/ppermute | solution.py:367
  80.6 5.7 %collective-permute-start.15 = (f32[48,384]{1,0:T(8,128)S(1)}, f32[48,384]{1,0:T(8,128)S(1)}, u32[]{:S(2)}, u32[]{:S(2)}) collective-permute-start(f32[48,384]{1,0:T(8,128)S(1)} %add.84.use_0), channel_id=1, source_target_pairs={{0,6},{1,7},{2,0},{3,1},{4,2},{5,3},{6,4},{7,5},{8,14},{9,15},{10,... | collective-permute-start | bytes 221192 | tf_op jit(solution)/shard_map/ppermute | solution.py:367
  96.8 12.9 %collective-permute-start.26 = (f32[4,224,128]{2,1,0:T(8,128)S(1)}, f32[4,224,128]{2,1,0:T(8,128)S(1)}, u32[]{:S(2)}, u32[]{:S(2)}) collective-permute-start(f32[4,224,128]{2,1,0:T(8,128)S(1)} %get-tuple-element.81), channel_id=1, source_target_pairs={{0,32},{8,40},{16,48},{24,56},{32,64},{40,72},{48,80},{56,88},{64,... | collective-permute-start | bytes 1376264 | tf_op jit(solution)/shard_map/ppermute | solution.py:392
  98.2 11.4 %collective-permute-start.27 = (f32[4,224,128]{2,1,0:T(8,128)S(1)}, f32[4,224,128]{2,1,0:T(8,128)S(1)}, u32[]{:S(2)}, u32[]{:S(2)}) collective-permute-start(f32[4,224,128]{2,1,0:T(8,128)S(1)} %get-tuple-element.82), channel_id=1, source_target_pairs={{0,96},{8,104},{16,112},{24,120},{32,0},{40,8},{48,16},{56,24},{64... | collective-permute-start | bytes 1376264 | tf_op jit(solution)/shard_map/ppermute | solution.py:392
  100.0 13.9 %collective-permute-start.16 = (f32[4,224,128]{2,1,0:T(8,128)S(1)}, f32[4,224,128]{2,1,0:T(8,128)S(1)}, u32[]{:S(2)}, u32[]{:S(2)}) collective-permute-start(f32[4,224,128]{2,1,0:T(8,128)S(1)} %get-tuple-element.71), channel_id=1, source_target_pairs={{0,8},{8,16},{16,24},{24,0},{32,40},{40,48},{48,56},{56,32},{64,72... | collective-permute-start | bytes 1376264 | tf_op jit(solution)/shard_map/ppermute | solution.py:392
  101.5 12.4 %collective-permute-start.17 = (f32[4,224,128]{2,1,0:T(8,128)S(1)}, f32[4,224,128]{2,1,0:T(8,128)S(1)}, u32[]{:S(2)}, u32[]{:S(2)}) collective-permute-start(f32[4,224,128]{2,1,0:T(8,128)S(1)} %get-tuple-element.72), channel_id=1, source_target_pairs={{0,24},{8,0},{16,8},{24,16},{32,56},{40,32},{48,40},{56,48},{64,88... | collective-permute-start | bytes 1376264 | tf_op jit(solution)/shard_map/ppermute | solution.py:392
  110.6 21.8 %collective-permute-start.28 = (f32[2,4,224,128]{3,2,1,0:T(8,128)S(1)}, f32[2,4,224,128]{3,2,1,0:T(8,128)S(1)}, u32[]{:S(2)}, u32[]{:S(2)}) collective-permute-start(f32[2,4,224,128]{3,2,1,0:T(8,128)S(1)} %get-tuple-element.83), channel_id=1, source_target_pairs={{0,32},{8,40},{16,48},{24,56},{32,64},{40,72},{48,80},{56,88},{64,... | collective-permute-start | bytes 2752520 | tf_op jit(solution)/shard_map/ppermute | solution.py:392
  112.2 20.3 %collective-permute-start.29 = (f32[2,4,224,128]{3,2,1,0:T(8,128)S(1)}, f32[2,4,224,128]{3,2,1,0:T(8,128)S(1)}, u32[]{:S(2)}, u32[]{:S(2)}) collective-permute-start(f32[2,4,224,128]{3,2,1,0:T(8,128)S(1)} %get-tuple-element.84), channel_id=1, source_target_pairs={{0,96},{8,104},{16,112},{24,120},{32,0},{40,8},{48,16},{56,24},{64... | collective-permute-start | bytes 2752520 | tf_op jit(solution)/shard_map/ppermute | solution.py:392
  114.9 24.2 %collective-permute-start.18 = (f32[2,4,224,128]{3,2,1,0:T(8,128)S(1)}, f32[2,4,224,128]{3,2,1,0:T(8,128)S(1)}, u32[]{:S(2)}, u32[]{:S(2)}) collective-permute-start(f32[2,4,224,128]{3,2,1,0:T(8,128)S(1)} %get-tuple-element.73), channel_id=1, source_target_pairs={{0,8},{8,16},{16,24},{24,0},{32,40},{40,48},{48,56},{56,32},{64,72... | collective-permute-start | bytes 2752520 | tf_op jit(solution)/shard_map/ppermute | solution.py:392
  116.4 22.7 %collective-permute-start.19 = (f32[2,4,224,128]{3,2,1,0:T(8,128)S(1)}, f32[2,4,224,128]{3,2,1,0:T(8,128)S(1)}, u32[]{:S(2)}, u32[]{:S(2)}) collective-permute-start(f32[2,4,224,128]{3,2,1,0:T(8,128)S(1)} %get-tuple-element.74), channel_id=1, source_target_pairs={{0,24},{8,0},{16,8},{24,16},{32,56},{40,32},{48,40},{56,48},{64,88... | collective-permute-start | bytes 2752520 | tf_op jit(solution)/shard_map/ppermute | solution.py:392
  133.5 11.1 %collective-permute-start.30 = (f32[448,128]{1,0:T(8,128)S(1)}, f32[448,128]{1,0:T(8,128)S(1)}, u32[]{:S(2)}, u32[]{:S(2)}) collective-permute-start(f32[448,128]{1,0:T(8,128)S(1)} %get-tuple-element.86), channel_id=1, source_target_pairs={{0,8},{8,16},{16,24},{24,0},{32,40},{40,48},{48,56},{56,32},{64,72... | collective-permute-start | bytes 688136 | tf_op jit(solution)/shard_map/ppermute | solution.py:392
  135.0 12.2 %collective-permute-start.31 = (f32[448,128]{1,0:T(8,128)S(1)}, f32[448,128]{1,0:T(8,128)S(1)}, u32[]{:S(2)}, u32[]{:S(2)}) collective-permute-start(f32[448,128]{1,0:T(8,128)S(1)} %get-tuple-element.87), channel_id=1, source_target_pairs={{0,16},{8,24},{16,0},{24,8},{32,48},{40,56},{48,32},{56,40},{64,80... | collective-permute-start | bytes 688136 | tf_op jit(solution)/shard_map/ppermute | solution.py:392
  138.0 9.2 %collective-permute-start.32 = (f32[448,128]{1,0:T(8,128)S(1)}, f32[448,128]{1,0:T(8,128)S(1)}, u32[]{:S(2)}, u32[]{:S(2)}) collective-permute-start(f32[448,128]{1,0:T(8,128)S(1)} %get-tuple-element.88), channel_id=1, source_target_pairs={{0,24},{8,0},{16,8},{24,16},{32,56},{40,32},{48,40},{56,48},{64,88... | collective-permute-start | bytes 688136 | tf_op jit(solution)/shard_map/ppermute | solution.py:392
  140.2 10.1 %collective-permute-start.20 = (f32[448,128]{1,0:T(8,128)S(1)}, f32[448,128]{1,0:T(8,128)S(1)}, u32[]{:S(2)}, u32[]{:S(2)}) collective-permute-start(f32[448,128]{1,0:T(8,128)S(1)} %get-tuple-element.76), channel_id=1, source_target_pairs={{0,32},{8,40},{16,48},{24,56},{32,64},{40,72},{48,80},{56,88},{64,... | collective-permute-start | bytes 688136 | tf_op jit(solution)/shard_map/ppermute | solution.py:392
  141.3 10.0 %collective-permute-start.21 = (f32[448,128]{1,0:T(8,128)S(1)}, f32[448,128]{1,0:T(8,128)S(1)}, u32[]{:S(2)}, u32[]{:S(2)}) collective-permute-start(f32[448,128]{1,0:T(8,128)S(1)} %get-tuple-element.77), channel_id=1, source_target_pairs={{0,64},{8,72},{16,80},{24,88},{32,96},{40,104},{48,112},{56,120},{... | collective-permute-start | bytes 688136 | tf_op jit(solution)/shard_map/ppermute | solution.py:392
  144.7 6.6 %collective-permute-start.22 = (f32[448,128]{1,0:T(8,128)S(1)}, f32[448,128]{1,0:T(8,128)S(1)}, u32[]{:S(2)}, u32[]{:S(2)}) collective-permute-start(f32[448,128]{1,0:T(8,128)S(1)} %get-tuple-element.78), channel_id=1, source_target_pairs={{0,96},{8,104},{16,112},{24,120},{32,0},{40,8},{48,16},{56,24},{64... | collective-permute-start | bytes 688136 | tf_op jit(solution)/shard_map/ppermute | solution.py:392
  148.0 10.6 %collective-permute-start.33 = (f32[448,128]{1,0:T(8,128)S(1)}, f32[448,128]{1,0:T(8,128)S(1)}, u32[]{:S(2)}, u32[]{:S(2)}) collective-permute-start(f32[448,128]{1,0:T(8,128)S(1)} %get-tuple-element.89), channel_id=1, source_target_pairs={{0,24},{8,0},{16,8},{24,16},{32,56},{40,32},{48,40},{56,48},{64,88... | collective-permute-start | bytes 688136 | tf_op jit(solution)/shard_map/ppermute | solution.py:392
  149.9 10.0 %collective-permute-start.34 = (f32[448,128]{1,0:T(8,128)S(1)}, f32[448,128]{1,0:T(8,128)S(1)}, u32[]{:S(2)}, u32[]{:S(2)}) collective-permute-start(f32[448,128]{1,0:T(8,128)S(1)} %get-tuple-element.89), channel_id=1, source_target_pairs={{0,16},{8,24},{16,0},{24,8},{32,48},{40,56},{48,32},{56,40},{64,80... | collective-permute-start | bytes 688136 | tf_op jit(solution)/shard_map/ppermute | solution.py:392
  150.3 11.8 %collective-permute-start.35 = (f32[448,128]{1,0:T(8,128)S(1)}, f32[448,128]{1,0:T(8,128)S(1)}, u32[]{:S(2)}, u32[]{:S(2)}) collective-permute-start(f32[448,128]{1,0:T(8,128)S(1)} %get-tuple-element.89), channel_id=1, source_target_pairs={{0,8},{8,16},{16,24},{24,0},{32,40},{40,48},{48,56},{56,32},{64,72... | collective-permute-start | bytes 688136 | tf_op jit(solution)/shard_map/ppermute | solution.py:392
  152.1 10.0 %collective-permute-start.25 = (f32[448,128]{1,0:T(8,128)S(1)}, f32[448,128]{1,0:T(8,128)S(1)}, u32[]{:S(2)}, u32[]{:S(2)}) collective-permute-start(f32[448,128]{1,0:T(8,128)S(1)} %get-tuple-element.79), channel_id=1, source_target_pairs={{0,32},{8,40},{16,48},{24,56},{32,64},{40,72},{48,80},{56,88},{64,... | collective-permute-start | bytes 688136 | tf_op jit(solution)/shard_map/ppermute | solution.py:392
  153.7 8.5 %collective-permute-start.23 = (f32[448,128]{1,0:T(8,128)S(1)}, f32[448,128]{1,0:T(8,128)S(1)}, u32[]{:S(2)}, u32[]{:S(2)}) collective-permute-start(f32[448,128]{1,0:T(8,128)S(1)} %get-tuple-element.79), channel_id=1, source_target_pairs={{0,96},{8,104},{16,112},{24,120},{32,0},{40,8},{48,16},{56,24},{64... | collective-permute-start | bytes 688136 | tf_op jit(solution)/shard_map/ppermute | solution.py:392
  158.6 7.5 %collective-permute-start.24 = (f32[448,128]{1,0:T(8,128)S(1)}, f32[448,128]{1,0:T(8,128)S(1)}, u32[]{:S(2)}, u32[]{:S(2)}) collective-permute-start(f32[448,128]{1,0:T(8,128)S(1)} %get-tuple-element.79), channel_id=1, source_target_pairs={{0,64},{8,72},{16,80},{24,88},{32,96},{40,104},{48,112},{56,120},{... | collective-permute-start | bytes 688136 | tf_op jit(solution)/shard_map/ppermute | solution.py:392
  166.2 21.3 %collective-permute-start.44 = (f32[2,4,224,128]{3,2,1,0:T(8,128)S(1)}, f32[2,4,224,128]{3,2,1,0:T(8,128)S(1)}, u32[]{:S(2)}, u32[]{:S(2)}) collective-permute-start(f32[2,4,224,128]{3,2,1,0:T(8,128)S(1)} %pad_maximum_fusion.refs_0_), channel_id=1, source_target_pairs={{0,8},{8,16},{16,24},{24,0},{32,40},{40,48},{48,56},{56,32},{64,72... | collective-permute-start | bytes 2752520 | tf_op jit(solution)/shard_map/ppermute | solution.py:392
  166.6 22.2 %collective-permute-start.43 = (f32[2,4,224,128]{3,2,1,0:T(8,128)S(1)}, f32[2,4,224,128]{3,2,1,0:T(8,128)S(1)}, u32[]{:S(2)}, u32[]{:S(2)}) collective-permute-start(f32[2,4,224,128]{3,2,1,0:T(8,128)S(1)} %pad_maximum_fusion.refs_0_), channel_id=1, source_target_pairs={{0,24},{8,0},{16,8},{24,16},{32,56},{40,32},{48,40},{56,48},{64,88... | collective-permute-start | bytes 2752520 | tf_op jit(solution)/shard_map/ppermute | solution.py:392
  170.1 20.9 %collective-permute-start.48 = (f32[2,4,224,128]{3,2,1,0:T(8,128)S(1)}, f32[2,4,224,128]{3,2,1,0:T(8,128)S(1)}, u32[]{:S(2)}, u32[]{:S(2)}) collective-permute-start(f32[2,4,224,128]{3,2,1,0:T(8,128)S(1)} %pad_maximum_fusion.1.refs_5_), channel_id=1, source_target_pairs={{0,32},{8,40},{16,48},{24,56},{32,64},{40,72},{48,80},{56,88},{64,... | collective-permute-start | bytes 2752520 | tf_op jit(solution)/shard_map/ppermute | solution.py:392
  171.2 3.6 %collective-permute-start.37 = (f32[8,128]{1,0:T(8,128)S(1)}, f32[8,128]{1,0:T(8,128)S(1)}, u32[]{:S(2)}, u32[]{:S(2)}) collective-permute-start(f32[8,128]{1,0:T(8,128)S(1)} %add.91), channel_id=1, source_target_pairs={{0,2},{1,3},{2,0},{3,1},{4,6},{5,7},{6,4},{7,5},{8,10},{9,11},{10,... | collective-permute-start | bytes 12296 | tf_op jit(solution)/shard_map/ppermute | solution.py:375
  174.9 7.1 %collective-permute-start.38 = (f32[8,128]{1,0:T(8,128)S(1)}, f32[8,128]{1,0:T(8,128)S(1)}, u32[]{:S(2)}, u32[]{:S(2)}) collective-permute-start(f32[8,128]{1,0:T(8,128)S(1)} %add.92), channel_id=1, source_target_pairs={{0,6},{1,7},{2,4},{3,5},{4,2},{5,3},{6,0},{7,1},{8,14},{9,15},{10,... | collective-permute-start | bytes 12296 | tf_op jit(solution)/shard_map/ppermute | solution.py:375
  178.7 22.0 %collective-permute-start.47 = (f32[2,4,224,128]{3,2,1,0:T(8,128)S(1)}, f32[2,4,224,128]{3,2,1,0:T(8,128)S(1)}, u32[]{:S(2)}, u32[]{:S(2)}) collective-permute-start(f32[2,4,224,128]{3,2,1,0:T(8,128)S(1)} %pad_maximum_fusion.1.refs_5_), channel_id=1, source_target_pairs={{0,96},{8,104},{16,112},{24,120},{32,0},{40,8},{48,16},{56,24},{64... | collective-permute-start | bytes 2752520 | tf_op jit(solution)/shard_map/ppermute | solution.py:392
  182.0 4.3 %collective-permute-start.39 = (f32[8,128]{1,0:T(8,128)S(1)}, f32[8,128]{1,0:T(8,128)S(1)}, u32[]{:S(2)}, u32[]{:S(2)}) collective-permute-start(f32[8,128]{1,0:T(8,128)S(1)} %add.93), channel_id=1, source_target_pairs={{0,8},{8,0},{16,24},{24,16},{32,40},{40,32},{48,56},{56,48},{64,72... | collective-permute-start | bytes 12296 | tf_op jit(solution)/shard_map/ppermute | solution.py:382
  186.3 18.3 %collective-permute-start.40 = (f32[8,128]{1,0:T(8,128)S(1)}, f32[8,128]{1,0:T(8,128)S(1)}, u32[]{:S(2)}, u32[]{:S(2)}) collective-permute-start(f32[8,128]{1,0:T(8,128)S(1)} %add.94), channel_id=1, source_target_pairs={{0,24},{8,16},{16,8},{24,0},{32,56},{40,48},{48,40},{56,32},{64,88... | collective-permute-start | bytes 12296 | tf_op jit(solution)/shard_map/ppermute | solution.py:382
  187.6 28.8 %collective-permute-start.45 = (f32[4,224,128]{2,1,0:T(8,128)S(1)}, f32[4,224,128]{2,1,0:T(8,128)S(1)}, u32[]{:S(2)}, u32[]{:S(2)}) collective-permute-start(f32[4,224,128]{2,1,0:T(8,128)S(1)} %slice_bitcast_fusion.3), channel_id=1, source_target_pairs={{0,8},{8,16},{16,24},{24,0},{32,40},{40,48},{48,56},{56,32},{64,72... | collective-permute-start | bytes 1376264 | tf_op jit(solution)/shard_map/ppermute | solution.py:392
  188.8 27.6 %collective-permute-start.46 = (f32[4,224,128]{2,1,0:T(8,128)S(1)}, f32[4,224,128]{2,1,0:T(8,128)S(1)}, u32[]{:S(2)}, u32[]{:S(2)}) collective-permute-start(f32[4,224,128]{2,1,0:T(8,128)S(1)} %slice_bitcast_fusion.2), channel_id=1, source_target_pairs={{0,24},{8,0},{16,8},{24,16},{32,56},{40,32},{48,40},{56,48},{64,88... | collective-permute-start | bytes 1376264 | tf_op jit(solution)/shard_map/ppermute | solution.py:392
  191.0 25.3 %collective-permute-start.49 = (f32[4,224,128]{2,1,0:T(8,128)S(1)}, f32[4,224,128]{2,1,0:T(8,128)S(1)}, u32[]{:S(2)}, u32[]{:S(2)}) collective-permute-start(f32[4,224,128]{2,1,0:T(8,128)S(1)} %slice_bitcast_fusion.1), channel_id=1, source_target_pairs={{0,32},{8,40},{16,48},{24,56},{32,64},{40,72},{48,80},{56,88},{64,... | collective-permute-start | bytes 1376264 | tf_op jit(solution)/shard_map/ppermute | solution.py:392
  200.8 15.5 %collective-permute-start.50 = (f32[4,224,128]{2,1,0:T(8,128)S(1)}, f32[4,224,128]{2,1,0:T(8,128)S(1)}, u32[]{:S(2)}, u32[]{:S(2)}) collective-permute-start(f32[4,224,128]{2,1,0:T(8,128)S(1)} %slice_bitcast_fusion), channel_id=1, source_target_pairs={{0,96},{8,104},{16,112},{24,120},{32,0},{40,8},{48,16},{56,24},{64... | collective-permute-start | bytes 1376264 | tf_op jit(solution)/shard_map/ppermute | solution.py:392
  204.6 6.9 %collective-permute-start.41 = (f32[8,128]{1,0:T(8,128)S(1)}, f32[8,128]{1,0:T(8,128)S(1)}, u32[]{:S(2)}, u32[]{:S(2)}) collective-permute-start(f32[8,128]{1,0:T(8,128)S(1)} %add.95), channel_id=1, source_target_pairs={{0,32},{8,40},{16,48},{24,56},{32,0},{40,8},{48,16},{56,24},{64,96... | collective-permute-start | bytes 12296 | tf_op jit(solution)/shard_map/ppermute | solution.py:382
  211.5 4.8 %collective-permute-start.42 = (f32[8,128]{1,0:T(8,128)S(1)}, f32[8,128]{1,0:T(8,128)S(1)}, u32[]{:S(2)}, u32[]{:S(2)}) collective-permute-start(f32[8,128]{1,0:T(8,128)S(1)} %add.96), channel_id=1, source_target_pairs={{0,96},{8,104},{16,112},{24,120},{32,64},{40,72},{48,80},{56,88},{... | collective-permute-start | bytes 12296 | tf_op jit(solution)/shard_map/ppermute | solution.py:382
  (11 other events, 131.5 us)

commit v6 on v5

--- a/solution.py
+++ b/solution.py
@@ -310,8 +310,14 @@
         total, more = merge_into(total, weight, part[...], line[4 - by])
         spread += more
         weight = weight + line[4 - by]
-    mean_ref[...] = total / jnp.full((8, 128), weight, f32)[0:1]
+    mean_ref[: own.shape[0], :] = total / jnp.full((8, 128), weight, f32)[0:1]
     spread_ref[...] = spread
+
+
+def finish_last_kernel(weights, own, in_1, in_2, in_3, *refs):
+    others, mean_ref, spread_ref = refs[:-2], refs[-2], refs[-1]
+    finish_kernel(weights, own, in_1, in_2, in_3, mean_ref, spread_ref)
+    mean_ref[own.shape[0] :, :] = sum((other[...] for other in others), spread_ref[...])
 
 
 def price_kernel(slots, roster_ref, price_ref, spread_ref, weight_ref, *refs):
@@ -376,10 +382,9 @@
     return value
 
 
-def sum_over_scen(value):
-    for axis in ("x", "y"):
-        for pair in (PAIR_A, PAIR_B):
-            value = value + lax.ppermute(value, "scen", scen_pairs(pair, axis))
+def spread_over_x(value):
+    for pair in (PAIR_A, PAIR_B):
+        value = value + lax.ppermute(value, "scen", scen_pairs(pair, "x"))
     return value
 
 
@@ -663,17 +668,18 @@
     moved = [
         (m[0], *[shift(m[by], side[1], by) for by in (1, 2, 3)]) for side, m in zip(sides, moved)
     ]
-    moved = [
-        local_call(finish_kernel, side[2], m, [flat], "finish") for side, m in zip(sides, moved)
-    ]
-    spreads += [m[1] for m in moved]
-    own_a, own_b = moved[0][0], moved[1][0]
+    own_b, spread = local_call(finish_kernel, sides[1][2], moved[1], [flat], "finish")
+    own_a = local_call(
+        finish_last_kernel, sides[0][2], (*moved[0], *spreads, spread), [(half + 8, n)], "finish"
+    )[0]
     row_a, row_b = gather_row(own_a, "y"), gather_row(own_b, "x")
+    spread = summed(*[row_a[k][half:] for k in range(4)])
+    row_a = {k: row_a[k][:half] for k in range(4)}
     pack_a, pack_b = gather_pack(row_a), gather_pack(row_b)
-    pack_a, pack_b, spread = lax.optimization_barrier((pack_a, pack_b, sum(spreads)))
+    pack_a, pack_b, spread = lax.optimization_barrier((pack_a, pack_b, spread))
     near_a, near_b = gather_near(pack_a, "x"), gather_near(pack_b, "y")
     spread = spread_over_veh(spread)
-    spread_total = sum_over_scen(spread)
+    spread_total = spread_over_x(spread)
     means = gather_far(*near_a, "x") + gather_far(*near_b, "y")
     entries = vehicles * lax.axis_size("veh") * n
 
@@ -701,7 +707,7 @@
         *[in_vmem(m) for m in means],
     )
 
-    own_mean = jnp.concatenate([own_a, own_b], axis=0)
+    own_mean = jnp.concatenate([own_a[:half], own_b], axis=0)
     return (plan, new_price, own_mean.astype(bf16)[None], dual[:, :crews], gap[0, 0])
 
 

time: 224 us -> 216 us (0.964)
  waiting for transfers between devices: 78.2 us -> 69 us
    ppermute x4 -> x2, waiting for transfers between devices: 13.7 us -> 5.74 us  [spread_over_x(): value = value + lax.ppermute(value, 'scen', scen_pairs(pair, 'x'))]
  transfers between devices with their start and end apart: 51 -> 49, of which waited for: 29 -> 30; matrix products, arithmetic and copies ran while one was open for 1% -> 1% of each run, Pallas kernels for 3% -> 3%
where the time goes in v6:
time: 216 us; the launch traced here: 215 us
  starting transfers between devices  73 us (34%)
  waiting for transfers between devices  69 us (32%)
  Pallas kernels  67.1 us (31%)
  local copies, waits for them, and re-layouts  3.15 us (1%)
    ppermute x28, starting transfers between devices, shift(): return lax.ppermute(value, 'scen', pairs)  47.9 us
    ppermute x28, waiting for transfers between devices, shift(): return lax.ppermute(value, 'scen', pairs)  39.1 us
    pallas_call x3, Pallas kernels, shards(): pl.pallas_call(middle_kernel, in_specs=[vm] * 12, out_specs=[vm] * 3, out...  29.6 us
    ppermute x12, starting transfers between devices, usage_exchange(): lax.ppermute(value, 'veh', veh_pairs({z: (z + by) % 4 for z in range(4)}))  18.7 us
    ppermute x12, waiting for transfers between devices, usage_exchange(): lax.ppermute(value, 'veh', veh_pairs({z: (z + by) % 4 for z in range(4)}))  16.5 us
    pallas_call x1, Pallas kernels, shards(): pl.pallas_call(first_kernel, grid_spec=pltpu.PrefetchScalarGridSpec(num_s...  13 us
    pallas_call x1, Pallas kernels, shards(): pl.pallas_call(last_kernel, grid_spec=pltpu.PrefetchScalarGridSpec(num_sc...  10.4 us
    pallas_call x1, Pallas kernels, shards(): pl.pallas_call(price_kernel, grid_spec=pltpu.PrefetchScalarGridSpec(num_s...  7.7 us
  transfers between devices with their start and end apart: 49, of which 30 were waited for; matrix products, arithmetic and copies ran while one was open for 1% of the time, Pallas kernels for 3%

profile of v6, /device:TPU:0, one launch (start us, length us, event | category | flops | bytes accessed | tf_op | source)
XLA Modules:
  0.0 215.0 jit_solution(16327748848242117700)
XLA Ops:
  2.8 13.0 %first_steps.1 = (f32[16,128,896]{2,1,0:T(8,128)S(1)}, f32[16,128,896]{2,1,0:T(8,128)S(1)}, f32[128,896]{1,0:T(8,128)S(1)}, bf16[384,896]{1,0:T(8,128)(2,1)S(1)}, f32[56,384]{1,0:T(8,128)S(1)}) custom-call(s32[16]{0:T(128)S(1)} %dynamic-slice_bitcast_fusion.bundles, bf16[16,896,128]{2,1,0:T(8,128)(2,1)} %start_ref.1, bf16[16,896,128]{2,1,0:T(8,128)(2,1)} %cost_ref.1, ...), custom_call_target="tpu_custom_call" | custom-call | tf_op jit(solution)/shard_map/first_steps/pallas_call | solution.py:481
  17.2 2.1 collective-permute-start.1
  19.2 3.6 %collective-permute-start.2 = (f32[56,384]{1,0:T(8,128)S(1)}, f32[56,384]{1,0:T(8,128)S(1)}, u32[]{:S(2)}, u32[]{:S(2)}) collective-permute-start(f32[56,384]{1,0:T(8,128)S(1)} %add.63.use_0), channel_id=1, source_target_pairs={{0,4},{1,5},{2,6},{3,7},{4,0},{5,1},{6,2},{7,3},{8,12},{9,13},{10,... | collective-permute-start | bytes 258056 | tf_op jit(solution)/shard_map/ppermute | solution.py:373
  24.2 3.0 %collective-permute-done.2.use_2 = f32[56,384]{1,0:T(8,128)S(1)} collective-permute-done((f32[56,384]{1,0:T(8,128)S(1)}, f32[56,384]{1,0:T(8,128)S(1)}, u32[]{:S(2)}, u32[]{:S(2)}) %collective-permute-start.2) | collective-permute-done | bytes 86048 | tf_op jit(solution)/shard_map/ppermute | solution.py:373
  27.3 9.9 %three_steps.3 = (f32[16,128,896]{2,1,0:T(8,128)S(1)}, f32[48,384]{1,0:T(8,128)S(1)}, f32[16,384]{1,0:T(8,128)S(1)}) custom-call(f32[16,128,896]{2,1,0:T(8,128)S(1)} %get-tuple-element.53.partial_ref, f32[16,128,896]{2,1,0:T(8,128)S(1)} %get-tuple-element.54.linear_ref, bf16[16,128,128]{2,1,0:T(8,128)(2,1)S(1)} %copy-done, ...), custom_call_target="tpu_custom_call", output_to_operand_aliasing={{0}: (0, {})} | custom-call | tf_op jit(solution)/shard_map/three_steps/pallas_call | solution.py:530
  39.8 2.5 %collective-permute-start.6 = (f32[48,384]{1,0:T(8,128)S(1)}, f32[48,384]{1,0:T(8,128)S(1)}, u32[]{:S(2)}, u32[]{:S(2)}) collective-permute-start(f32[48,384]{1,0:T(8,128)S(1)} %add.67.use_0), channel_id=1, source_target_pairs={{0,4},{1,5},{2,6},{3,7},{4,0},{5,1},{6,2},{7,3},{8,12},{9,13},{10,... | collective-permute-start | bytes 221192 | tf_op jit(solution)/shard_map/ppermute | solution.py:373
  44.5 1.6 collective-permute-done.6.use_2
  46.7 9.9 %three_steps.4 = (f32[16,128,896]{2,1,0:T(8,128)S(1)}, f32[48,384]{1,0:T(8,128)S(1)}, f32[16,384]{1,0:T(8,128)S(1)}) custom-call(f32[16,128,896]{2,1,0:T(8,128)S(1)} %get-tuple-element.58.partial_ref, f32[16,128,896]{2,1,0:T(8,128)S(1)} %get-tuple-element.54.linear_ref, bf16[16,128,128]{2,1,0:T(8,128)(2,1)S(1)} %copy-done, ...), custom_call_target="tpu_custom_call", output_to_operand_aliasing={{0}: (0, {})} | custom-call | tf_op jit(solution)/shard_map/three_steps/pallas_call | solution.py:530
  57.9 1.8 collective-permute-start.10
  59.7 2.1 collective-permute-start.11
  61.9 2.0 collective-permute-done.10.use_2
  65.2 2.2 %collective-permute-done.9.use_1 = f32[48,384]{1,0:T(8,128)S(1)} collective-permute-done((f32[48,384]{1,0:T(8,128)S(1)}, f32[48,384]{1,0:T(8,128)S(1)}, u32[]{:S(2)}, u32[]{:S(2)}) %collective-permute-start.9) | collective-permute-done | bytes 73760 | tf_op jit(solution)/shard_map/ppermute | solution.py:373
  67.4 9.9 %three_steps.5 = (f32[16,128,896]{2,1,0:T(8,128)S(1)}, f32[48,384]{1,0:T(8,128)S(1)}, f32[16,384]{1,0:T(8,128)S(1)}) custom-call(f32[16,128,896]{2,1,0:T(8,128)S(1)} %get-tuple-element.61.partial_ref, f32[16,128,896]{2,1,0:T(8,128)S(1)} %get-tuple-element.54.linear_ref, bf16[16,128,128]{2,1,0:T(8,128)(2,1)S(1)} %copy-done, ...), custom_call_target="tpu_custom_call", output_to_operand_aliasing={{0}: (0, {})} | custom-call | tf_op jit(solution)/shard_map/three_steps/pallas_call | solution.py:530
  78.7 1.9 collective-permute-start.14
  81.9 3.9 %collective-permute-done.13.use_1 = f32[48,384]{1,0:T(8,128)S(1)} collective-permute-done((f32[48,384]{1,0:T(8,128)S(1)}, f32[48,384]{1,0:T(8,128)S(1)}, u32[]{:S(2)}, u32[]{:S(2)}) %collective-permute-start.13) | collective-permute-done | bytes 73760 | tf_op jit(solution)/shard_map/ppermute | solution.py:373
  86.4 10.4 %last_step.1 = (bf16[16,896,128]{2,1,0:T(8,128)(2,1)}, f32[16,896,128]{2,1,0:T(8,128)S(1)}, f32[16,448,128]{2,1,0:T(8,128)S(1)}, f32[16,448,128]{2,1,0:T(8,128)S...) custom-call(s32[2,16]{1,0:T(2,128)S(1)} %pad_add_fusion.slots, ...), custom_call_target="tpu_custom_call" | custom-call | tf_op jit(solution)/shard_map/last_step/pallas_call | solution.py:590
  97.4 1.7 collective-permute-start.23
  99.0 1.6 collective-permute-start.24
  100.6 1.5 collective-permute-start.16
  102.1 1.7 collective-permute-start.17
  104.0 6.1 %collective-permute-done.23.up_in = f32[4,224,128]{2,1,0:T(8,128)S(1)} collective-permute-done((f32[4,224,128]{2,1,0:T(8,128)S(1)}, f32[4,224,128]{2,1,0:T(8,128)S(1)}, u32[]{:S(2)}, u32[]{:S(2)}) %collective-permute-start.23) | collective-permute-done | bytes 458784 | tf_op jit(solution)/shard_map/ppermute | solution.py:397
  111.2 1.6 collective-permute-start.25
  112.8 1.7 collective-permute-start.26
  115.5 1.5 collective-permute-start.18
  117.0 1.8 collective-permute-start.19
  118.8 14.0 %collective-permute-done.25.up_in = f32[2,4,224,128]{3,2,1,0:T(8,128)S(1)} collective-permute-done((f32[2,4,224,128]{3,2,1,0:T(8,128)S(1)}, f32[2,4,224,128]{3,2,1,0:T(8,128)S(1)}, u32[]{:S(2)}, u32[]{:S(2)}) %collective-permute-start.25) | collective-permute-done | bytes 917536 | tf_op jit(solution)/shard_map/ppermute | solution.py:397
  133.8 1.6 collective-permute-start.27
  135.5 2.8 %collective-permute-start.28 = (f32[448,128]{1,0:T(8,128)S(1)}, f32[448,128]{1,0:T(8,128)S(1)}, u32[]{:S(2)}, u32[]{:S(2)}) collective-permute-start(f32[448,128]{1,0:T(8,128)S(1)} %get-tuple-element.90), channel_id=1, source_target_pairs={{0,16},{8,24},{16,0},{24,8},{32,48},{40,56},{48,32},{56,40},{64,80... | collective-permute-start | bytes 688136 | tf_op jit(solution)/shard_map/ppermute | solution.py:397
  141.8 3.3 %collective-permute-start.21 = (f32[448,128]{1,0:T(8,128)S(1)}, f32[448,128]{1,0:T(8,128)S(1)}, u32[]{:S(2)}, u32[]{:S(2)}) collective-permute-start(f32[448,128]{1,0:T(8,128)S(1)} %get-tuple-element.76), channel_id=1, source_target_pairs={{0,64},{8,72},{16,80},{24,88},{32,96},{40,104},{48,112},{56,120},{... | collective-permute-start | bytes 688136 | tf_op jit(solution)/shard_map/ppermute | solution.py:397
  148.3 1.9 collective-permute-start.33
  151.6 1.5 finish.3
  153.1 1.7 collective-permute-start.32
  154.8 1.5 collective-permute-start.30
  156.3 2.5 %collective-permute-done.33 = f32[448,128]{1,0:T(8,128)S(1)} collective-permute-done((f32[448,128]{1,0:T(8,128)S(1)}, f32[448,128]{1,0:T(8,128)S(1)}, u32[]{:S(2)}, u32[]{:S(2)}) %collective-permute-start.33) | collective-permute-done | bytes 229408 | tf_op jit(solution)/shard_map/ppermute | solution.py:397
  160.1 2.4 %collective-permute-done.35 = f32[448,128]{1,0:T(8,128)S(1)} collective-permute-done((f32[448,128]{1,0:T(8,128)S(1)}, f32[448,128]{1,0:T(8,128)S(1)}, u32[]{:S(2)}, u32[]{:S(2)}) %collective-permute-start.35) | collective-permute-done | bytes 229408 | tf_op jit(solution)/shard_map/ppermute | solution.py:397
  162.8 3.6 %collective-permute-done.31 = f32[456,128]{1,0:T(8,128)S(1)} collective-permute-done((f32[456,128]{1,0:T(8,128)S(1)}, f32[456,128]{1,0:T(8,128)S(1)}, u32[]{:S(2)}, u32[]{:S(2)}) %collective-permute-start.31) | collective-permute-done | bytes 233504 | tf_op jit(solution)/shard_map/ppermute | solution.py:397
  167.6 2.7 %collective-permute-start.41 = (f32[2,4,224,128]{3,2,1,0:T(8,128)S(1)}, f32[2,4,224,128]{3,2,1,0:T(8,128)S(1)}, u32[]{:S(2)}, u32[]{:S(2)}) collective-permute-start(f32[2,4,224,128]{3,2,1,0:T(8,128)S(1)} %pad_maximum_fusion.refs_0_), channel_id=1, source_target_pairs={{0,24},{8,0},{16,8},{24,16},{32,56},{40,32},{48,40},{56,48},{64,88... | collective-permute-start | bytes 2752520 | tf_op jit(solution)/shard_map/ppermute | solution.py:397
  171.0 2.6 %collective-permute-start.45 = (f32[2,4,224,128]{3,2,1,0:T(8,128)S(1)}, f32[2,4,224,128]{3,2,1,0:T(8,128)S(1)}, u32[]{:S(2)}, u32[]{:S(2)}) collective-permute-start(f32[2,4,224,128]{3,2,1,0:T(8,128)S(1)} %pad_maximum_fusion.1.refs_5_), channel_id=1, source_target_pairs={{0,96},{8,104},{16,112},{24,120},{32,0},{40,8},{48,16},{56,24},{64... | collective-permute-start | bytes 2752520 | tf_op jit(solution)/shard_map/ppermute | solution.py:397
  173.9 3.2 %collective-permute-done.37 = f32[8,128]{1,0:T(8,128)S(1)} collective-permute-done((f32[8,128]{1,0:T(8,128)S(1)}, f32[8,128]{1,0:T(8,128)S(1)}, u32[]{:S(2)}, u32[]{:S(2)}) %collective-permute-start.37) | collective-permute-done | bytes 4128 | tf_op jit(solution)/shard_map/ppermute | solution.py:381
  177.2 3.7 %collective-permute-start.38 = (f32[8,128]{1,0:T(8,128)S(1)}, f32[8,128]{1,0:T(8,128)S(1)}, u32[]{:S(2)}, u32[]{:S(2)}) collective-permute-start(f32[8,128]{1,0:T(8,128)S(1)} %add.74), channel_id=1, source_target_pairs={{0,6},{1,7},{2,4},{3,5},{4,2},{5,3},{6,0},{7,1},{8,14},{9,15},{10,... | collective-permute-start | bytes 12296 | tf_op jit(solution)/shard_map/ppermute | solution.py:381
  180.9 6.5 %collective-permute-done.42.refs_2_ = f32[2,4,224,128]{3,2,1,0:T(8,128)S(1)} collective-permute-done((f32[2,4,224,128]{3,2,1,0:T(8,128)S(1)}, f32[2,4,224,128]{3,2,1,0:T(8,128)S(1)}, u32[]{:S(2)}, u32[]{:S(2)}) %collective-permute-start.42) | collective-permute-done | bytes 917536 | tf_op jit(solution)/shard_map/ppermute | solution.py:397
  188.2 2.7 %collective-permute-start.44 = (f32[4,224,128]{2,1,0:T(8,128)S(1)}, f32[4,224,128]{2,1,0:T(8,128)S(1)}, u32[]{:S(2)}, u32[]{:S(2)}) collective-permute-start(f32[4,224,128]{2,1,0:T(8,128)S(1)} %slice_bitcast_fusion.2), channel_id=1, source_target_pairs={{0,24},{8,0},{16,8},{24,16},{32,56},{40,32},{48,40},{56,48},{64,88... | collective-permute-start | bytes 1376264 | tf_op jit(solution)/shard_map/ppermute | solution.py:397
  190.9 2.4 %collective-permute-start.47 = (f32[4,224,128]{2,1,0:T(8,128)S(1)}, f32[4,224,128]{2,1,0:T(8,128)S(1)}, u32[]{:S(2)}, u32[]{:S(2)}) collective-permute-start(f32[4,224,128]{2,1,0:T(8,128)S(1)} %slice_bitcast_fusion.1), channel_id=1, source_target_pairs={{0,32},{8,40},{16,48},{24,56},{32,64},{40,72},{48,80},{56,88},{64,... | collective-permute-start | bytes 1376264 | tf_op jit(solution)/shard_map/ppermute | solution.py:397
  193.9 3.8 %collective-permute-start.48 = (f32[4,224,128]{2,1,0:T(8,128)S(1)}, f32[4,224,128]{2,1,0:T(8,128)S(1)}, u32[]{:S(2)}, u32[]{:S(2)}) collective-permute-start(f32[4,224,128]{2,1,0:T(8,128)S(1)} %slice_bitcast_fusion), channel_id=1, source_target_pairs={{0,96},{8,104},{16,112},{24,120},{32,0},{40,8},{48,16},{56,24},{64... | collective-permute-start | bytes 1376264 | tf_op jit(solution)/shard_map/ppermute | solution.py:397
  197.8 3.6 %collective-permute-done.39 = f32[8,128]{1,0:T(8,128)S(1)} collective-permute-done((f32[8,128]{1,0:T(8,128)S(1)}, f32[8,128]{1,0:T(8,128)S(1)}, u32[]{:S(2)}, u32[]{:S(2)}) %collective-permute-start.39) | collective-permute-done | bytes 4128 | tf_op jit(solution)/shard_map/ppermute | solution.py:387
  201.4 1.9 collective-permute-start.40
  204.0 2.2 %collective-permute-done.40 = f32[8,128]{1,0:T(8,128)S(1)} collective-permute-done((f32[8,128]{1,0:T(8,128)S(1)}, f32[8,128]{1,0:T(8,128)S(1)}, u32[]{:S(2)}, u32[]{:S(2)}) %collective-permute-start.40) | collective-permute-done | bytes 4128 | tf_op jit(solution)/shard_map/ppermute | solution.py:387
  207.3 7.7 %new_price.1 = (bf16[16,896,128]{2,1,0:T(8,128)(2,1)}, f32[1,1]{1,0:T(1,128)}) custom-call(s32[2,16]{1,0:T(2,128)S(1)} %pad_add_fusion.slots, f32[16,896,128]{2,1,0:T(8,128)S(1)} %get-tuple-element.68.roster_ref, bf16[16,896,128]{2,1,0:T(8,128)(2,1)} %price_ref.3, f32[8,128]{1,0:T(8,128)S(1)} %add.77.spread_ref, f32[1,256]{1,0:T(1,128)S(1)} %bitcast.35, ...), custom_call_target="tpu_custom_call" | custom-call | tf_op jit(solution)/shard_map/new_price/pallas_call | solution.py:687
  (122 shorter events, 35.3 us)
Async XLA Ops:
  15.8 1.4 collective-permute-start
  17.2 7.0 %collective-permute-start.1 = (f32[56,384]{1,0:T(8,128)S(1)}, f32[56,384]{1,0:T(8,128)S(1)}, u32[]{:S(2)}, u32[]{:S(2)}) collective-permute-start(f32[56,384]{1,0:T(8,128)S(1)} %add.63.use_0), channel_id=1, source_target_pairs={{0,2},{1,3},{2,4},{3,5},{4,6},{5,7},{6,0},{7,1},{8,10},{9,11},{10,... | collective-permute-start | bytes 258056 | tf_op jit(solution)/shard_map/ppermute | solution.py:373
  19.2 8.0 %collective-permute-start.2 = (f32[56,384]{1,0:T(8,128)S(1)}, f32[56,384]{1,0:T(8,128)S(1)}, u32[]{:S(2)}, u32[]{:S(2)}) collective-permute-start(f32[56,384]{1,0:T(8,128)S(1)} %add.63.use_0), channel_id=1, source_target_pairs={{0,4},{1,5},{2,6},{3,7},{4,0},{5,1},{6,2},{7,3},{8,12},{9,13},{10,... | collective-permute-start | bytes 258056 | tf_op jit(solution)/shard_map/ppermute | solution.py:373
  22.8 4.5 %collective-permute-start.3 = (f32[56,384]{1,0:T(8,128)S(1)}, f32[56,384]{1,0:T(8,128)S(1)}, u32[]{:S(2)}, u32[]{:S(2)}) collective-permute-start(f32[56,384]{1,0:T(8,128)S(1)} %add.63.use_0), channel_id=1, source_target_pairs={{0,6},{1,7},{2,0},{3,1},{4,2},{5,3},{6,4},{7,5},{8,14},{9,15},{10,... | collective-permute-start | bytes 258056 | tf_op jit(solution)/shard_map/ppermute | solution.py:373
  37.2 1.3 collective-permute-start.4
  38.5 6.0 %collective-permute-start.5 = (f32[48,384]{1,0:T(8,128)S(1)}, f32[48,384]{1,0:T(8,128)S(1)}, u32[]{:S(2)}, u32[]{:S(2)}) collective-permute-start(f32[48,384]{1,0:T(8,128)S(1)} %add.67.use_0), channel_id=1, source_target_pairs={{0,2},{1,3},{2,4},{3,5},{4,6},{5,7},{6,0},{7,1},{8,10},{9,11},{10,... | collective-permute-start | bytes 221192 | tf_op jit(solution)/shard_map/ppermute | solution.py:373
  39.8 6.4 %collective-permute-start.6 = (f32[48,384]{1,0:T(8,128)S(1)}, f32[48,384]{1,0:T(8,128)S(1)}, u32[]{:S(2)}, u32[]{:S(2)}) collective-permute-start(f32[48,384]{1,0:T(8,128)S(1)} %add.67.use_0), channel_id=1, source_target_pairs={{0,4},{1,5},{2,6},{3,7},{4,0},{5,1},{6,2},{7,3},{8,12},{9,13},{10,... | collective-permute-start | bytes 221192 | tf_op jit(solution)/shard_map/ppermute | solution.py:373
  42.3 4.4 %collective-permute-start.7 = (f32[48,384]{1,0:T(8,128)S(1)}, f32[48,384]{1,0:T(8,128)S(1)}, u32[]{:S(2)}, u32[]{:S(2)}) collective-permute-start(f32[48,384]{1,0:T(8,128)S(1)} %add.67.use_0), channel_id=1, source_target_pairs={{0,6},{1,7},{2,0},{3,1},{4,2},{5,3},{6,4},{7,5},{8,14},{9,15},{10,... | collective-permute-start | bytes 221192 | tf_op jit(solution)/shard_map/ppermute | solution.py:373
  57.9 6.0 %collective-permute-start.10 = (f32[48,384]{1,0:T(8,128)S(1)}, f32[48,384]{1,0:T(8,128)S(1)}, u32[]{:S(2)}, u32[]{:S(2)}) collective-permute-start(f32[48,384]{1,0:T(8,128)S(1)} %add.68.use_0), channel_id=1, source_target_pairs={{0,4},{1,5},{2,6},{3,7},{4,0},{5,1},{6,2},{7,3},{8,12},{9,13},{10,... | collective-permute-start | bytes 221192 | tf_op jit(solution)/shard_map/ppermute | solution.py:373
  59.7 5.4 %collective-permute-start.11 = (f32[48,384]{1,0:T(8,128)S(1)}, f32[48,384]{1,0:T(8,128)S(1)}, u32[]{:S(2)}, u32[]{:S(2)}) collective-permute-start(f32[48,384]{1,0:T(8,128)S(1)} %add.68.use_0), channel_id=1, source_target_pairs={{0,6},{1,7},{2,0},{3,1},{4,2},{5,3},{6,4},{7,5},{8,14},{9,15},{10,... | collective-permute-start | bytes 221192 | tf_op jit(solution)/shard_map/ppermute | solution.py:373
  61.8 5.6 %collective-permute-start.9 = (f32[48,384]{1,0:T(8,128)S(1)}, f32[48,384]{1,0:T(8,128)S(1)}, u32[]{:S(2)}, u32[]{:S(2)}) collective-permute-start(f32[48,384]{1,0:T(8,128)S(1)} %add.68.use_0), channel_id=1, source_target_pairs={{0,2},{1,3},{2,4},{3,5},{4,6},{5,7},{6,0},{7,1},{8,10},{9,11},{10,... | collective-permute-start | bytes 221192 | tf_op jit(solution)/shard_map/ppermute | solution.py:373
  77.3 1.3 collective-permute-start.12
  78.6 7.2 %collective-permute-start.13 = (f32[48,384]{1,0:T(8,128)S(1)}, f32[48,384]{1,0:T(8,128)S(1)}, u32[]{:S(2)}, u32[]{:S(2)}) collective-permute-start(f32[48,384]{1,0:T(8,128)S(1)} %add.69.use_0), channel_id=1, source_target_pairs={{0,2},{1,3},{2,4},{3,5},{4,6},{5,7},{6,0},{7,1},{8,10},{9,11},{10,... | collective-permute-start | bytes 221192 | tf_op jit(solution)/shard_map/ppermute | solution.py:373
  78.7 7.1 %collective-permute-start.14 = (f32[48,384]{1,0:T(8,128)S(1)}, f32[48,384]{1,0:T(8,128)S(1)}, u32[]{:S(2)}, u32[]{:S(2)}) collective-permute-start(f32[48,384]{1,0:T(8,128)S(1)} %add.69.use_0), channel_id=1, source_target_pairs={{0,4},{1,5},{2,6},{3,7},{4,0},{5,1},{6,2},{7,3},{8,12},{9,13},{10,... | collective-permute-start | bytes 221192 | tf_op jit(solution)/shard_map/ppermute | solution.py:373
  80.6 5.7 %collective-permute-start.15 = (f32[48,384]{1,0:T(8,128)S(1)}, f32[48,384]{1,0:T(8,128)S(1)}, u32[]{:S(2)}, u32[]{:S(2)}) collective-permute-start(f32[48,384]{1,0:T(8,128)S(1)} %add.69.use_0), channel_id=1, source_target_pairs={{0,6},{1,7},{2,0},{3,1},{4,2},{5,3},{6,4},{7,5},{8,14},{9,15},{10,... | collective-permute-start | bytes 221192 | tf_op jit(solution)/shard_map/ppermute | solution.py:373
  97.4 12.7 %collective-permute-start.23 = (f32[4,224,128]{2,1,0:T(8,128)S(1)}, f32[4,224,128]{2,1,0:T(8,128)S(1)}, u32[]{:S(2)}, u32[]{:S(2)}) collective-permute-start(f32[4,224,128]{2,1,0:T(8,128)S(1)} %get-tuple-element.81), channel_id=1, source_target_pairs={{0,32},{8,40},{16,48},{24,56},{32,64},{40,72},{48,80},{56,88},{64,... | collective-permute-start | bytes 1376264 | tf_op jit(solution)/shard_map/ppermute | solution.py:397
  99.0 11.2 %collective-permute-start.24 = (f32[4,224,128]{2,1,0:T(8,128)S(1)}, f32[4,224,128]{2,1,0:T(8,128)S(1)}, u32[]{:S(2)}, u32[]{:S(2)}) collective-permute-start(f32[4,224,128]{2,1,0:T(8,128)S(1)} %get-tuple-element.82), channel_id=1, source_target_pairs={{0,96},{8,104},{16,112},{24,120},{32,0},{40,8},{48,16},{56,24},{64... | collective-permute-start | bytes 1376264 | tf_op jit(solution)/shard_map/ppermute | solution.py:397
  100.6 13.9 %collective-permute-start.16 = (f32[4,224,128]{2,1,0:T(8,128)S(1)}, f32[4,224,128]{2,1,0:T(8,128)S(1)}, u32[]{:S(2)}, u32[]{:S(2)}) collective-permute-start(f32[4,224,128]{2,1,0:T(8,128)S(1)} %get-tuple-element.70), channel_id=1, source_target_pairs={{0,8},{8,16},{16,24},{24,0},{32,40},{40,48},{48,56},{56,32},{64,72... | collective-permute-start | bytes 1376264 | tf_op jit(solution)/shard_map/ppermute | solution.py:397
  102.1 12.4 %collective-permute-start.17 = (f32[4,224,128]{2,1,0:T(8,128)S(1)}, f32[4,224,128]{2,1,0:T(8,128)S(1)}, u32[]{:S(2)}, u32[]{:S(2)}) collective-permute-start(f32[4,224,128]{2,1,0:T(8,128)S(1)} %get-tuple-element.71), channel_id=1, source_target_pairs={{0,24},{8,0},{16,8},{24,16},{32,56},{40,32},{48,40},{56,48},{64,88... | collective-permute-start | bytes 1376264 | tf_op jit(solution)/shard_map/ppermute | solution.py:397
  111.2 21.5 %collective-permute-start.25 = (f32[2,4,224,128]{3,2,1,0:T(8,128)S(1)}, f32[2,4,224,128]{3,2,1,0:T(8,128)S(1)}, u32[]{:S(2)}, u32[]{:S(2)}) collective-permute-start(f32[2,4,224,128]{3,2,1,0:T(8,128)S(1)} %get-tuple-element.85), channel_id=1, source_target_pairs={{0,32},{8,40},{16,48},{24,56},{32,64},{40,72},{48,80},{56,88},{64,... | collective-permute-start | bytes 2752520 | tf_op jit(solution)/shard_map/ppermute | solution.py:397
  112.8 20.0 %collective-permute-start.26 = (f32[2,4,224,128]{3,2,1,0:T(8,128)S(1)}, f32[2,4,224,128]{3,2,1,0:T(8,128)S(1)}, u32[]{:S(2)}, u32[]{:S(2)}) collective-permute-start(f32[2,4,224,128]{3,2,1,0:T(8,128)S(1)} %get-tuple-element.86), channel_id=1, source_target_pairs={{0,96},{8,104},{16,112},{24,120},{32,0},{40,8},{48,16},{56,24},{64... | collective-permute-start | bytes 2752520 | tf_op jit(solution)/shard_map/ppermute | solution.py:397
  115.5 24.0 %collective-permute-start.18 = (f32[2,4,224,128]{3,2,1,0:T(8,128)S(1)}, f32[2,4,224,128]{3,2,1,0:T(8,128)S(1)}, u32[]{:S(2)}, u32[]{:S(2)}) collective-permute-start(f32[2,4,224,128]{3,2,1,0:T(8,128)S(1)} %get-tuple-element.72), channel_id=1, source_target_pairs={{0,8},{8,16},{16,24},{24,0},{32,40},{40,48},{48,56},{56,32},{64,72... | collective-permute-start | bytes 2752520 | tf_op jit(solution)/shard_map/ppermute | solution.py:397
  117.0 22.5 %collective-permute-start.19 = (f32[2,4,224,128]{3,2,1,0:T(8,128)S(1)}, f32[2,4,224,128]{3,2,1,0:T(8,128)S(1)}, u32[]{:S(2)}, u32[]{:S(2)}) collective-permute-start(f32[2,4,224,128]{3,2,1,0:T(8,128)S(1)} %get-tuple-element.73), channel_id=1, source_target_pairs={{0,24},{8,0},{16,8},{24,16},{32,56},{40,32},{48,40},{56,48},{64,88... | collective-permute-start | bytes 2752520 | tf_op jit(solution)/shard_map/ppermute | solution.py:397
  133.8 11.2 %collective-permute-start.27 = (f32[448,128]{1,0:T(8,128)S(1)}, f32[448,128]{1,0:T(8,128)S(1)}, u32[]{:S(2)}, u32[]{:S(2)}) collective-permute-start(f32[448,128]{1,0:T(8,128)S(1)} %get-tuple-element.89), channel_id=1, source_target_pairs={{0,8},{8,16},{16,24},{24,0},{32,40},{40,48},{48,56},{56,32},{64,72... | collective-permute-start | bytes 688136 | tf_op jit(solution)/shard_map/ppermute | solution.py:397
  135.5 11.9 %collective-permute-start.28 = (f32[448,128]{1,0:T(8,128)S(1)}, f32[448,128]{1,0:T(8,128)S(1)}, u32[]{:S(2)}, u32[]{:S(2)}) collective-permute-start(f32[448,128]{1,0:T(8,128)S(1)} %get-tuple-element.90), channel_id=1, source_target_pairs={{0,16},{8,24},{16,0},{24,8},{32,48},{40,56},{48,32},{56,40},{64,80... | collective-permute-start | bytes 688136 | tf_op jit(solution)/shard_map/ppermute | solution.py:397
  138.3 9.1 %collective-permute-start.29 = (f32[448,128]{1,0:T(8,128)S(1)}, f32[448,128]{1,0:T(8,128)S(1)}, u32[]{:S(2)}, u32[]{:S(2)}) collective-permute-start(f32[448,128]{1,0:T(8,128)S(1)} %get-tuple-element.91), channel_id=1, source_target_pairs={{0,24},{8,0},{16,8},{24,16},{32,56},{40,32},{48,40},{56,48},{64,88... | collective-permute-start | bytes 688136 | tf_op jit(solution)/shard_map/ppermute | solution.py:397
  140.6 10.1 %collective-permute-start.20 = (f32[448,128]{1,0:T(8,128)S(1)}, f32[448,128]{1,0:T(8,128)S(1)}, u32[]{:S(2)}, u32[]{:S(2)}) collective-permute-start(f32[448,128]{1,0:T(8,128)S(1)} %get-tuple-element.75), channel_id=1, source_target_pairs={{0,32},{8,40},{16,48},{24,56},{32,64},{40,72},{48,80},{56,88},{64,... | collective-permute-start | bytes 688136 | tf_op jit(solution)/shard_map/ppermute | solution.py:397
  141.8 9.8 %collective-permute-start.21 = (f32[448,128]{1,0:T(8,128)S(1)}, f32[448,128]{1,0:T(8,128)S(1)}, u32[]{:S(2)}, u32[]{:S(2)}) collective-permute-start(f32[448,128]{1,0:T(8,128)S(1)} %get-tuple-element.76), channel_id=1, source_target_pairs={{0,64},{8,72},{16,80},{24,88},{32,96},{40,104},{48,112},{56,120},{... | collective-permute-start | bytes 688136 | tf_op jit(solution)/shard_map/ppermute | solution.py:397
  145.1 6.5 %collective-permute-start.22 = (f32[448,128]{1,0:T(8,128)S(1)}, f32[448,128]{1,0:T(8,128)S(1)}, u32[]{:S(2)}, u32[]{:S(2)}) collective-permute-start(f32[448,128]{1,0:T(8,128)S(1)} %get-tuple-element.77), channel_id=1, source_target_pairs={{0,96},{8,104},{16,112},{24,120},{32,0},{40,8},{48,16},{56,24},{64... | collective-permute-start | bytes 688136 | tf_op jit(solution)/shard_map/ppermute | solution.py:397
  148.3 10.6 %collective-permute-start.33 = (f32[448,128]{1,0:T(8,128)S(1)}, f32[448,128]{1,0:T(8,128)S(1)}, u32[]{:S(2)}, u32[]{:S(2)}) collective-permute-start(f32[448,128]{1,0:T(8,128)S(1)} %get-tuple-element.94), channel_id=1, source_target_pairs={{0,24},{8,0},{16,8},{24,16},{32,56},{40,32},{48,40},{56,48},{64,88... | collective-permute-start | bytes 688136 | tf_op jit(solution)/shard_map/ppermute | solution.py:397
  150.2 9.9 %collective-permute-start.34 = (f32[448,128]{1,0:T(8,128)S(1)}, f32[448,128]{1,0:T(8,128)S(1)}, u32[]{:S(2)}, u32[]{:S(2)}) collective-permute-start(f32[448,128]{1,0:T(8,128)S(1)} %get-tuple-element.94), channel_id=1, source_target_pairs={{0,16},{8,24},{16,0},{24,8},{32,48},{40,56},{48,32},{56,40},{64,80... | collective-permute-start | bytes 688136 | tf_op jit(solution)/shard_map/ppermute | solution.py:397
  150.7 11.8 %collective-permute-start.35 = (f32[448,128]{1,0:T(8,128)S(1)}, f32[448,128]{1,0:T(8,128)S(1)}, u32[]{:S(2)}, u32[]{:S(2)}) collective-permute-start(f32[448,128]{1,0:T(8,128)S(1)} %get-tuple-element.94), channel_id=1, source_target_pairs={{0,8},{8,16},{16,24},{24,0},{32,40},{40,48},{48,56},{56,32},{64,72... | collective-permute-start | bytes 688136 | tf_op jit(solution)/shard_map/ppermute | solution.py:397
  153.1 9.5 %collective-permute-start.32 = (f32[456,128]{1,0:T(8,128)S(1)}, f32[456,128]{1,0:T(8,128)S(1)}, u32[]{:S(2)}, u32[]{:S(2)}) collective-permute-start(f32[456,128]{1,0:T(8,128)S(1)} %get-tuple-element.93), channel_id=1, source_target_pairs={{0,32},{8,40},{16,48},{24,56},{32,64},{40,72},{48,80},{56,88},{64,... | collective-permute-start | bytes 700424 | tf_op jit(solution)/shard_map/ppermute | solution.py:397
  154.8 8.0 %collective-permute-start.30 = (f32[456,128]{1,0:T(8,128)S(1)}, f32[456,128]{1,0:T(8,128)S(1)}, u32[]{:S(2)}, u32[]{:S(2)}) collective-permute-start(f32[456,128]{1,0:T(8,128)S(1)} %get-tuple-element.93), channel_id=1, source_target_pairs={{0,96},{8,104},{16,112},{24,120},{32,0},{40,8},{48,16},{56,24},{64... | collective-permute-start | bytes 700424 | tf_op jit(solution)/shard_map/ppermute | solution.py:397
  158.8 7.6 %collective-permute-start.31 = (f32[456,128]{1,0:T(8,128)S(1)}, f32[456,128]{1,0:T(8,128)S(1)}, u32[]{:S(2)}, u32[]{:S(2)}) collective-permute-start(f32[456,128]{1,0:T(8,128)S(1)} %get-tuple-element.93), channel_id=1, source_target_pairs={{0,64},{8,72},{16,80},{24,88},{32,96},{40,104},{48,112},{56,120},{... | collective-permute-start | bytes 700424 | tf_op jit(solution)/shard_map/ppermute | solution.py:397
  166.5 20.9 %collective-permute-start.42 = (f32[2,4,224,128]{3,2,1,0:T(8,128)S(1)}, f32[2,4,224,128]{3,2,1,0:T(8,128)S(1)}, u32[]{:S(2)}, u32[]{:S(2)}) collective-permute-start(f32[2,4,224,128]{3,2,1,0:T(8,128)S(1)} %pad_maximum_fusion.refs_0_), channel_id=1, source_target_pairs={{0,8},{8,16},{16,24},{24,0},{32,40},{40,48},{48,56},{56,32},{64,72... | collective-permute-start | bytes 2752520 | tf_op jit(solution)/shard_map/ppermute | solution.py:397
  167.6 20.5 %collective-permute-start.41 = (f32[2,4,224,128]{3,2,1,0:T(8,128)S(1)}, f32[2,4,224,128]{3,2,1,0:T(8,128)S(1)}, u32[]{:S(2)}, u32[]{:S(2)}) collective-permute-start(f32[2,4,224,128]{3,2,1,0:T(8,128)S(1)} %pad_maximum_fusion.refs_0_), channel_id=1, source_target_pairs={{0,24},{8,0},{16,8},{24,16},{32,56},{40,32},{48,40},{56,48},{64,88... | collective-permute-start | bytes 2752520 | tf_op jit(solution)/shard_map/ppermute | solution.py:397
  170.3 20.6 %collective-permute-start.46 = (f32[2,4,224,128]{3,2,1,0:T(8,128)S(1)}, f32[2,4,224,128]{3,2,1,0:T(8,128)S(1)}, u32[]{:S(2)}, u32[]{:S(2)}) collective-permute-start(f32[2,4,224,128]{3,2,1,0:T(8,128)S(1)} %pad_maximum_fusion.1.refs_5_), channel_id=1, source_target_pairs={{0,32},{8,40},{16,48},{24,56},{32,64},{40,72},{48,80},{56,88},{64,... | collective-permute-start | bytes 2752520 | tf_op jit(solution)/shard_map/ppermute | solution.py:397
  171.0 2.6 %collective-permute-start.36 = (f32[8,128]{1,0:T(8,128)S(1)}, f32[8,128]{1,0:T(8,128)S(1)}, u32[]{:S(2)}, u32[]{:S(2)}) collective-permute-start(f32[8,128]{1,0:T(8,128)S(1)} %fusion.2), channel_id=1, source_target_pairs={{0,1},{1,0},{2,3},{3,2},{4,5},{5,4},{6,7},{7,6},{8,9},{9,8},{10,11... | collective-permute-start | bytes 12296 | tf_op jit(solution)/shard_map/ppermute | solution.py:381
  171.0 22.9 %collective-permute-start.45 = (f32[2,4,224,128]{3,2,1,0:T(8,128)S(1)}, f32[2,4,224,128]{3,2,1,0:T(8,128)S(1)}, u32[]{:S(2)}, u32[]{:S(2)}) collective-permute-start(f32[2,4,224,128]{3,2,1,0:T(8,128)S(1)} %pad_maximum_fusion.1.refs_5_), channel_id=1, source_target_pairs={{0,96},{8,104},{16,112},{24,120},{32,0},{40,8},{48,16},{56,24},{64... | collective-permute-start | bytes 2752520 | tf_op jit(solution)/shard_map/ppermute | solution.py:397
  173.6 3.6 %collective-permute-start.37 = (f32[8,128]{1,0:T(8,128)S(1)}, f32[8,128]{1,0:T(8,128)S(1)}, u32[]{:S(2)}, u32[]{:S(2)}) collective-permute-start(f32[8,128]{1,0:T(8,128)S(1)} %add.73), channel_id=1, source_target_pairs={{0,2},{1,3},{2,0},{3,1},{4,6},{5,7},{6,4},{7,5},{8,10},{9,11},{10,... | collective-permute-start | bytes 12296 | tf_op jit(solution)/shard_map/ppermute | solution.py:381
  177.2 20.5 %collective-permute-start.38 = (f32[8,128]{1,0:T(8,128)S(1)}, f32[8,128]{1,0:T(8,128)S(1)}, u32[]{:S(2)}, u32[]{:S(2)}) collective-permute-start(f32[8,128]{1,0:T(8,128)S(1)} %add.74), channel_id=1, source_target_pairs={{0,6},{1,7},{2,4},{3,5},{4,2},{5,3},{6,0},{7,1},{8,14},{9,15},{10,... | collective-permute-start | bytes 12296 | tf_op jit(solution)/shard_map/ppermute | solution.py:381
  187.4 18.7 %collective-permute-start.43 = (f32[4,224,128]{2,1,0:T(8,128)S(1)}, f32[4,224,128]{2,1,0:T(8,128)S(1)}, u32[]{:S(2)}, u32[]{:S(2)}) collective-permute-start(f32[4,224,128]{2,1,0:T(8,128)S(1)} %slice_bitcast_fusion.3), channel_id=1, source_target_pairs={{0,8},{8,16},{16,24},{24,0},{32,40},{40,48},{48,56},{56,32},{64,72... | collective-permute-start | bytes 1376264 | tf_op jit(solution)/shard_map/ppermute | solution.py:397
  188.2 18.0 %collective-permute-start.44 = (f32[4,224,128]{2,1,0:T(8,128)S(1)}, f32[4,224,128]{2,1,0:T(8,128)S(1)}, u32[]{:S(2)}, u32[]{:S(2)}) collective-permute-start(f32[4,224,128]{2,1,0:T(8,128)S(1)} %slice_bitcast_fusion.2), channel_id=1, source_target_pairs={{0,24},{8,0},{16,8},{24,16},{32,56},{40,32},{48,40},{56,48},{64,88... | collective-permute-start | bytes 1376264 | tf_op jit(solution)/shard_map/ppermute | solution.py:397
  190.9 15.3 %collective-permute-start.47 = (f32[4,224,128]{2,1,0:T(8,128)S(1)}, f32[4,224,128]{2,1,0:T(8,128)S(1)}, u32[]{:S(2)}, u32[]{:S(2)}) collective-permute-start(f32[4,224,128]{2,1,0:T(8,128)S(1)} %slice_bitcast_fusion.1), channel_id=1, source_target_pairs={{0,32},{8,40},{16,48},{24,56},{32,64},{40,72},{48,80},{56,88},{64,... | collective-permute-start | bytes 1376264 | tf_op jit(solution)/shard_map/ppermute | solution.py:397
  193.9 13.4 %collective-permute-start.48 = (f32[4,224,128]{2,1,0:T(8,128)S(1)}, f32[4,224,128]{2,1,0:T(8,128)S(1)}, u32[]{:S(2)}, u32[]{:S(2)}) collective-permute-start(f32[4,224,128]{2,1,0:T(8,128)S(1)} %slice_bitcast_fusion), channel_id=1, source_target_pairs={{0,96},{8,104},{16,112},{24,120},{32,0},{40,8},{48,16},{56,24},{64... | collective-permute-start | bytes 1376264 | tf_op jit(solution)/shard_map/ppermute | solution.py:397
  197.7 3.7 %collective-permute-start.39 = (f32[8,128]{1,0:T(8,128)S(1)}, f32[8,128]{1,0:T(8,128)S(1)}, u32[]{:S(2)}, u32[]{:S(2)}) collective-permute-start(f32[8,128]{1,0:T(8,128)S(1)} %add.75), channel_id=1, source_target_pairs={{0,8},{8,0},{16,24},{24,16},{32,40},{40,32},{48,56},{56,48},{64,72... | collective-permute-start | bytes 12296 | tf_op jit(solution)/shard_map/ppermute | solution.py:387
  201.4 4.8 %collective-permute-start.40 = (f32[8,128]{1,0:T(8,128)S(1)}, f32[8,128]{1,0:T(8,128)S(1)}, u32[]{:S(2)}, u32[]{:S(2)}) collective-permute-start(f32[8,128]{1,0:T(8,128)S(1)} %add.76), channel_id=1, source_target_pairs={{0,24},{8,16},{16,8},{24,0},{32,56},{40,48},{48,40},{56,32},{64,88... | collective-permute-start | bytes 12296 | tf_op jit(solution)/shard_map/ppermute | solution.py:387
  (9 other events, 111.5 us)

commit v7 on v6

--- a/solution.py
+++ b/solution.py
@@ -683,14 +683,15 @@
     means = gather_far(*near_a, "x") + gather_far(*near_b, "y")
     entries = vehicles * lax.axis_size("veh") * n
 
-    each = 2
+    each = 4
+    four_block = pl.BlockSpec((each, vehicles, n), lambda s, *_: (s, 0, 0))
     new_price, gap = pl.pallas_call(
         price_kernel,
         grid_spec=pltpu.PrefetchScalarGridSpec(
             num_scalar_prefetch=1,
             grid=(count // each,),
-            in_specs=[vm, pair_block] + [vm] * 12,
-            out_specs=[pair_block, whole(1, 1)],
+            in_specs=[vm, four_block] + [vm] * 12,
+            out_specs=[four_block, whole(1, 1)],
         ),
         out_shape=[
             jax.ShapeDtypeStruct((count, vehicles, n), bf16),

time: 216 us -> 215 us (level)
  waiting for transfers between devices: 69 us -> 72.1 us
  starting transfers between devices: 73 us -> 70.4 us
    ppermute x28, waiting for transfers between devices: 39.1 us -> 42.2 us  [shift(): return lax.ppermute(value, 'scen', pairs)]
    ppermute x28, starting transfers between devices: 47.9 us -> 45.5 us  [shift(): return lax.ppermute(value, 'scen', pairs)]
where the time goes in v7:
time: 215 us; the launch traced here: 214 us
  waiting for transfers between devices  72.1 us (34%)
  starting transfers between devices  70.4 us (33%)
  Pallas kernels  65.5 us (30%)
  local copies, waits for them, and re-layouts  3.15 us (1%)
    ppermute x28, starting transfers between devices, shift(): return lax.ppermute(value, 'scen', pairs)  45.5 us
    ppermute x28, waiting for transfers between devices, shift(): return lax.ppermute(value, 'scen', pairs)  42.2 us
    pallas_call x3, Pallas kernels, shards(): pl.pallas_call(middle_kernel, in_specs=[vm] * 12, out_specs=[vm] * 3, out...  29.6 us
    ppermute x12, starting transfers between devices, usage_exchange(): lax.ppermute(value, 'veh', veh_pairs({z: (z + by) % 4 for z in range(4)}))  18.7 us
    ppermute x12, waiting for transfers between devices, usage_exchange(): lax.ppermute(value, 'veh', veh_pairs({z: (z + by) % 4 for z in range(4)}))  16.5 us
    pallas_call x1, Pallas kernels, shards(): pl.pallas_call(first_kernel, grid_spec=pltpu.PrefetchScalarGridSpec(num_s...  13.1 us
    pallas_call x1, Pallas kernels, shards(): pl.pallas_call(last_kernel, grid_spec=pltpu.PrefetchScalarGridSpec(num_sc...  10.4 us
    pallas_call x6, Pallas kernels, local_call(): pl.pallas_call(body, in_specs=[pl.BlockSpec(memory_space=pltpu.SMEM)] + [...  6.42 us
  transfers between devices with their start and end apart: 49, of which 30 were waited for; matrix products, arithmetic and copies ran while one was open for 1% of the time, Pallas kernels for 3%

profile of v7, /device:TPU:0, one launch (start us, length us, event | category | flops | bytes accessed | tf_op | source)
XLA Modules:
  0.0 214.0 jit_solution(10126934113398376845)
XLA Ops:
  2.8 13.1 %first_steps.1 = (f32[16,128,896]{2,1,0:T(8,128)S(1)}, f32[16,128,896]{2,1,0:T(8,128)S(1)}, f32[128,896]{1,0:T(8,128)S(1)}, bf16[384,896]{1,0:T(8,128)(2,1)S(1)}, f32[56,384]{1,0:T(8,128)S(1)}) custom-call(s32[16]{0:T(128)S(1)} %dynamic-slice_bitcast_fusion.bundles, bf16[16,896,128]{2,1,0:T(8,128)(2,1)} %start_ref.1, bf16[16,896,128]{2,1,0:T(8,128)(2,1)} %cost_ref.1, ...), custom_call_target="tpu_custom_call" | custom-call | tf_op jit(solution)/shard_map/first_steps/pallas_call | solution.py:481
  17.3 2.1 collective-permute-start.1
  19.4 3.6 %collective-permute-start.2 = (f32[56,384]{1,0:T(8,128)S(1)}, f32[56,384]{1,0:T(8,128)S(1)}, u32[]{:S(2)}, u32[]{:S(2)}) collective-permute-start(f32[56,384]{1,0:T(8,128)S(1)} %add.63.use_0), channel_id=1, source_target_pairs={{0,4},{1,5},{2,6},{3,7},{4,0},{5,1},{6,2},{7,3},{8,12},{9,13},{10,... | collective-permute-start | bytes 258056 | tf_op jit(solution)/shard_map/ppermute | solution.py:373
  24.3 3.0 %collective-permute-done.2.use_2 = f32[56,384]{1,0:T(8,128)S(1)} collective-permute-done((f32[56,384]{1,0:T(8,128)S(1)}, f32[56,384]{1,0:T(8,128)S(1)}, u32[]{:S(2)}, u32[]{:S(2)}) %collective-permute-start.2) | collective-permute-done | bytes 86048 | tf_op jit(solution)/shard_map/ppermute | solution.py:373
  27.4 9.9 %three_steps.3 = (f32[16,128,896]{2,1,0:T(8,128)S(1)}, f32[48,384]{1,0:T(8,128)S(1)}, f32[16,384]{1,0:T(8,128)S(1)}) custom-call(f32[16,128,896]{2,1,0:T(8,128)S(1)} %get-tuple-element.53.partial_ref, f32[16,128,896]{2,1,0:T(8,128)S(1)} %get-tuple-element.54.linear_ref, bf16[16,128,128]{2,1,0:T(8,128)(2,1)S(1)} %copy-done, ...), custom_call_target="tpu_custom_call", output_to_operand_aliasing={{0}: (0, {})} | custom-call | tf_op jit(solution)/shard_map/three_steps/pallas_call | solution.py:530
  39.9 2.5 %collective-permute-start.6 = (f32[48,384]{1,0:T(8,128)S(1)}, f32[48,384]{1,0:T(8,128)S(1)}, u32[]{:S(2)}, u32[]{:S(2)}) collective-permute-start(f32[48,384]{1,0:T(8,128)S(1)} %add.67.use_0), channel_id=1, source_target_pairs={{0,4},{1,5},{2,6},{3,7},{4,0},{5,1},{6,2},{7,3},{8,12},{9,13},{10,... | collective-permute-start | bytes 221192 | tf_op jit(solution)/shard_map/ppermute | solution.py:373
  44.7 1.6 collective-permute-done.6.use_2
  46.8 9.9 %three_steps.4 = (f32[16,128,896]{2,1,0:T(8,128)S(1)}, f32[48,384]{1,0:T(8,128)S(1)}, f32[16,384]{1,0:T(8,128)S(1)}) custom-call(f32[16,128,896]{2,1,0:T(8,128)S(1)} %get-tuple-element.58.partial_ref, f32[16,128,896]{2,1,0:T(8,128)S(1)} %get-tuple-element.54.linear_ref, bf16[16,128,128]{2,1,0:T(8,128)(2,1)S(1)} %copy-done, ...), custom_call_target="tpu_custom_call", output_to_operand_aliasing={{0}: (0, {})} | custom-call | tf_op jit(solution)/shard_map/three_steps/pallas_call | solution.py:530
  58.0 1.8 collective-permute-start.10
  59.9 2.1 collective-permute-start.11
  62.0 2.0 collective-permute-done.10.use_2
  65.3 2.2 %collective-permute-done.9.use_1 = f32[48,384]{1,0:T(8,128)S(1)} collective-permute-done((f32[48,384]{1,0:T(8,128)S(1)}, f32[48,384]{1,0:T(8,128)S(1)}, u32[]{:S(2)}, u32[]{:S(2)}) %collective-permute-start.9) | collective-permute-done | bytes 73760 | tf_op jit(solution)/shard_map/ppermute | solution.py:373
  67.5 9.9 %three_steps.5 = (f32[16,128,896]{2,1,0:T(8,128)S(1)}, f32[48,384]{1,0:T(8,128)S(1)}, f32[16,384]{1,0:T(8,128)S(1)}) custom-call(f32[16,128,896]{2,1,0:T(8,128)S(1)} %get-tuple-element.61.partial_ref, f32[16,128,896]{2,1,0:T(8,128)S(1)} %get-tuple-element.54.linear_ref, bf16[16,128,128]{2,1,0:T(8,128)(2,1)S(1)} %copy-done, ...), custom_call_target="tpu_custom_call", output_to_operand_aliasing={{0}: (0, {})} | custom-call | tf_op jit(solution)/shard_map/three_steps/pallas_call | solution.py:530
  78.8 1.9 collective-permute-start.14
  82.0 3.9 %collective-permute-done.13.use_1 = f32[48,384]{1,0:T(8,128)S(1)} collective-permute-done((f32[48,384]{1,0:T(8,128)S(1)}, f32[48,384]{1,0:T(8,128)S(1)}, u32[]{:S(2)}, u32[]{:S(2)}) %collective-permute-start.13) | collective-permute-done | bytes 73760 | tf_op jit(solution)/shard_map/ppermute | solution.py:373
  86.5 10.4 %last_step.1 = (bf16[16,896,128]{2,1,0:T(8,128)(2,1)}, f32[16,896,128]{2,1,0:T(8,128)S(1)}, f32[16,448,128]{2,1,0:T(8,128)S(1)}, f32[16,448,128]{2,1,0:T(8,128)S...) custom-call(s32[2,16]{1,0:T(2,128)S(1)} %pad_add_fusion.slots, ...), custom_call_target="tpu_custom_call" | custom-call | tf_op jit(solution)/shard_map/last_step/pallas_call | solution.py:590
  97.5 1.4 collective-permute-start.23
  98.9 1.8 collective-permute-start.24
  102.1 1.9 collective-permute-start.17
  104.2 6.1 %collective-permute-done.23.up_in = f32[4,224,128]{2,1,0:T(8,128)S(1)} collective-permute-done((f32[4,224,128]{2,1,0:T(8,128)S(1)}, f32[4,224,128]{2,1,0:T(8,128)S(1)}, u32[]{:S(2)}, u32[]{:S(2)}) %collective-permute-start.23) | collective-permute-done | bytes 458784 | tf_op jit(solution)/shard_map/ppermute | solution.py:397
  112.7 1.9 collective-permute-start.26
  115.5 1.7 collective-permute-start.18
  117.3 1.6 collective-permute-start.19
  118.8 14.2 %collective-permute-done.25.up_in = f32[2,4,224,128]{3,2,1,0:T(8,128)S(1)} collective-permute-done((f32[2,4,224,128]{3,2,1,0:T(8,128)S(1)}, f32[2,4,224,128]{3,2,1,0:T(8,128)S(1)}, u32[]{:S(2)}, u32[]{:S(2)}) %collective-permute-start.25) | collective-permute-done | bytes 917536 | tf_op jit(solution)/shard_map/ppermute | solution.py:397
  134.1 1.8 collective-permute-start.27
  135.9 2.2 %collective-permute-start.28 = (f32[448,128]{1,0:T(8,128)S(1)}, f32[448,128]{1,0:T(8,128)S(1)}, u32[]{:S(2)}, u32[]{:S(2)}) collective-permute-start(f32[448,128]{1,0:T(8,128)S(1)} %get-tuple-element.90), channel_id=1, source_target_pairs={{0,16},{8,24},{16,0},{24,8},{32,48},{40,56},{48,32},{56,40},{64,80... | collective-permute-start | bytes 688136 | tf_op jit(solution)/shard_map/ppermute | solution.py:397
  138.1 1.7 collective-permute-start.29
  141.9 3.5 %collective-permute-start.21 = (f32[448,128]{1,0:T(8,128)S(1)}, f32[448,128]{1,0:T(8,128)S(1)}, u32[]{:S(2)}, u32[]{:S(2)}) collective-permute-start(f32[448,128]{1,0:T(8,128)S(1)} %get-tuple-element.76), channel_id=1, source_target_pairs={{0,64},{8,72},{16,80},{24,88},{32,96},{40,104},{48,112},{56,120},{... | collective-permute-start | bytes 688136 | tf_op jit(solution)/shard_map/ppermute | solution.py:397
  148.1 2.4 %collective-permute-start.33 = (f32[448,128]{1,0:T(8,128)S(1)}, f32[448,128]{1,0:T(8,128)S(1)}, u32[]{:S(2)}, u32[]{:S(2)}) collective-permute-start(f32[448,128]{1,0:T(8,128)S(1)} %get-tuple-element.94), channel_id=1, source_target_pairs={{0,24},{8,0},{16,8},{24,16},{32,56},{40,32},{48,40},{56,48},{64,88... | collective-permute-start | bytes 688136 | tf_op jit(solution)/shard_map/ppermute | solution.py:397
  152.0 1.5 finish.3
  153.5 1.5 collective-permute-start.32
  155.0 1.8 collective-permute-start.30
  156.8 2.3 %collective-permute-done.33 = f32[448,128]{1,0:T(8,128)S(1)} collective-permute-done((f32[448,128]{1,0:T(8,128)S(1)}, f32[448,128]{1,0:T(8,128)S(1)}, u32[]{:S(2)}, u32[]{:S(2)}) %collective-permute-start.33) | collective-permute-done | bytes 229408 | tf_op jit(solution)/shard_map/ppermute | solution.py:397
  160.4 2.4 %collective-permute-done.35 = f32[448,128]{1,0:T(8,128)S(1)} collective-permute-done((f32[448,128]{1,0:T(8,128)S(1)}, f32[448,128]{1,0:T(8,128)S(1)}, u32[]{:S(2)}, u32[]{:S(2)}) %collective-permute-start.35) | collective-permute-done | bytes 229408 | tf_op jit(solution)/shard_map/ppermute | solution.py:397
  162.9 1.4 collective-permute-done.30
  164.3 2.6 %collective-permute-done.31 = f32[456,128]{1,0:T(8,128)S(1)} collective-permute-done((f32[456,128]{1,0:T(8,128)S(1)}, f32[456,128]{1,0:T(8,128)S(1)}, u32[]{:S(2)}, u32[]{:S(2)}) %collective-permute-start.31) | collective-permute-done | bytes 233504 | tf_op jit(solution)/shard_map/ppermute | solution.py:397
  167.9 3.1 %collective-permute-start.41 = (f32[2,4,224,128]{3,2,1,0:T(8,128)S(1)}, f32[2,4,224,128]{3,2,1,0:T(8,128)S(1)}, u32[]{:S(2)}, u32[]{:S(2)}) collective-permute-start(f32[2,4,224,128]{3,2,1,0:T(8,128)S(1)} %pad_maximum_fusion.refs_0_), channel_id=1, source_target_pairs={{0,24},{8,0},{16,8},{24,16},{32,56},{40,32},{48,40},{56,48},{64,88... | collective-permute-start | bytes 2752520 | tf_op jit(solution)/shard_map/ppermute | solution.py:397
  171.0 3.2 %collective-permute-start.45 = (f32[2,4,224,128]{3,2,1,0:T(8,128)S(1)}, f32[2,4,224,128]{3,2,1,0:T(8,128)S(1)}, u32[]{:S(2)}, u32[]{:S(2)}) collective-permute-start(f32[2,4,224,128]{3,2,1,0:T(8,128)S(1)} %pad_maximum_fusion.1.refs_5_), channel_id=1, source_target_pairs={{0,96},{8,104},{16,112},{24,120},{32,0},{40,8},{48,16},{56,24},{64... | collective-permute-start | bytes 2752520 | tf_op jit(solution)/shard_map/ppermute | solution.py:397
  174.6 3.2 %collective-permute-done.37 = f32[8,128]{1,0:T(8,128)S(1)} collective-permute-done((f32[8,128]{1,0:T(8,128)S(1)}, f32[8,128]{1,0:T(8,128)S(1)}, u32[]{:S(2)}, u32[]{:S(2)}) %collective-permute-start.37) | collective-permute-done | bytes 4128 | tf_op jit(solution)/shard_map/ppermute | solution.py:381
  177.8 3.5 %collective-permute-start.38 = (f32[8,128]{1,0:T(8,128)S(1)}, f32[8,128]{1,0:T(8,128)S(1)}, u32[]{:S(2)}, u32[]{:S(2)}) collective-permute-start(f32[8,128]{1,0:T(8,128)S(1)} %add.74), channel_id=1, source_target_pairs={{0,6},{1,7},{2,4},{3,5},{4,2},{5,3},{6,0},{7,1},{8,14},{9,15},{10,... | collective-permute-start | bytes 12296 | tf_op jit(solution)/shard_map/ppermute | solution.py:381
  181.3 8.1 %collective-permute-done.42.refs_2_ = f32[2,4,224,128]{3,2,1,0:T(8,128)S(1)} collective-permute-done((f32[2,4,224,128]{3,2,1,0:T(8,128)S(1)}, f32[2,4,224,128]{3,2,1,0:T(8,128)S(1)}, u32[]{:S(2)}, u32[]{:S(2)}) %collective-permute-start.42) | collective-permute-done | bytes 917536 | tf_op jit(solution)/shard_map/ppermute | solution.py:397
  189.5 3.3 %collective-permute-start.44 = (f32[4,224,128]{2,1,0:T(8,128)S(1)}, f32[4,224,128]{2,1,0:T(8,128)S(1)}, u32[]{:S(2)}, u32[]{:S(2)}) collective-permute-start(f32[4,224,128]{2,1,0:T(8,128)S(1)} %slice_bitcast_fusion.2), channel_id=1, source_target_pairs={{0,24},{8,0},{16,8},{24,16},{32,56},{40,32},{48,40},{56,48},{64,88... | collective-permute-start | bytes 1376264 | tf_op jit(solution)/shard_map/ppermute | solution.py:397
  192.9 1.6 collective-permute-done.45.refs_6_
  194.5 3.8 %collective-permute-start.48 = (f32[4,224,128]{2,1,0:T(8,128)S(1)}, f32[4,224,128]{2,1,0:T(8,128)S(1)}, u32[]{:S(2)}, u32[]{:S(2)}) collective-permute-start(f32[4,224,128]{2,1,0:T(8,128)S(1)} %slice_bitcast_fusion), channel_id=1, source_target_pairs={{0,96},{8,104},{16,112},{24,120},{32,0},{40,8},{48,16},{56,24},{64... | collective-permute-start | bytes 1376264 | tf_op jit(solution)/shard_map/ppermute | solution.py:397
  198.4 3.6 %collective-permute-done.39 = f32[8,128]{1,0:T(8,128)S(1)} collective-permute-done((f32[8,128]{1,0:T(8,128)S(1)}, f32[8,128]{1,0:T(8,128)S(1)}, u32[]{:S(2)}, u32[]{:S(2)}) %collective-permute-start.39) | collective-permute-done | bytes 4128 | tf_op jit(solution)/shard_map/ppermute | solution.py:387
  202.0 1.9 collective-permute-start.40
  204.7 2.2 %collective-permute-done.40 = f32[8,128]{1,0:T(8,128)S(1)} collective-permute-done((f32[8,128]{1,0:T(8,128)S(1)}, f32[8,128]{1,0:T(8,128)S(1)}, u32[]{:S(2)}, u32[]{:S(2)}) %collective-permute-start.40) | collective-permute-done | bytes 4128 | tf_op jit(solution)/shard_map/ppermute | solution.py:387
  208.0 6.0 %new_price.1 = (bf16[16,896,128]{2,1,0:T(8,128)(2,1)}, f32[1,1]{1,0:T(1,128)}) custom-call(s32[2,16]{1,0:T(2,128)S(1)} %pad_add_fusion.slots, f32[16,896,128]{2,1,0:T(8,128)S(1)} %get-tuple-element.68.roster_ref, bf16[16,896,128]{2,1,0:T(8,128)(2,1)} %price_ref.3, f32[8,128]{1,0:T(8,128)S(1)} %add.77.spread_ref, f32[1,256]{1,0:T(1,128)S(1)} %bitcast.35, ...), custom_call_target="tpu_custom_call" | custom-call | tf_op jit(solution)/shard_map/new_price/pallas_call | solution.py:688
  (122 shorter events, 34.2 us)
Async XLA Ops:
  15.9 1.4 collective-permute-start
  17.3 7.0 %collective-permute-start.1 = (f32[56,384]{1,0:T(8,128)S(1)}, f32[56,384]{1,0:T(8,128)S(1)}, u32[]{:S(2)}, u32[]{:S(2)}) collective-permute-start(f32[56,384]{1,0:T(8,128)S(1)} %add.63.use_0), channel_id=1, source_target_pairs={{0,2},{1,3},{2,4},{3,5},{4,6},{5,7},{6,0},{7,1},{8,10},{9,11},{10,... | collective-permute-start | bytes 258056 | tf_op jit(solution)/shard_map/ppermute | solution.py:373
  19.4 8.0 %collective-permute-start.2 = (f32[56,384]{1,0:T(8,128)S(1)}, f32[56,384]{1,0:T(8,128)S(1)}, u32[]{:S(2)}, u32[]{:S(2)}) collective-permute-start(f32[56,384]{1,0:T(8,128)S(1)} %add.63.use_0), channel_id=1, source_target_pairs={{0,4},{1,5},{2,6},{3,7},{4,0},{5,1},{6,2},{7,3},{8,12},{9,13},{10,... | collective-permute-start | bytes 258056 | tf_op jit(solution)/shard_map/ppermute | solution.py:373
  22.9 4.5 %collective-permute-start.3 = (f32[56,384]{1,0:T(8,128)S(1)}, f32[56,384]{1,0:T(8,128)S(1)}, u32[]{:S(2)}, u32[]{:S(2)}) collective-permute-start(f32[56,384]{1,0:T(8,128)S(1)} %add.63.use_0), channel_id=1, source_target_pairs={{0,6},{1,7},{2,0},{3,1},{4,2},{5,3},{6,4},{7,5},{8,14},{9,15},{10,... | collective-permute-start | bytes 258056 | tf_op jit(solution)/shard_map/ppermute | solution.py:373
  37.3 1.3 collective-permute-start.4
  38.7 6.0 %collective-permute-start.5 = (f32[48,384]{1,0:T(8,128)S(1)}, f32[48,384]{1,0:T(8,128)S(1)}, u32[]{:S(2)}, u32[]{:S(2)}) collective-permute-start(f32[48,384]{1,0:T(8,128)S(1)} %add.67.use_0), channel_id=1, source_target_pairs={{0,2},{1,3},{2,4},{3,5},{4,6},{5,7},{6,0},{7,1},{8,10},{9,11},{10,... | collective-permute-start | bytes 221192 | tf_op jit(solution)/shard_map/ppermute | solution.py:373
  39.9 6.4 %collective-permute-start.6 = (f32[48,384]{1,0:T(8,128)S(1)}, f32[48,384]{1,0:T(8,128)S(1)}, u32[]{:S(2)}, u32[]{:S(2)}) collective-permute-start(f32[48,384]{1,0:T(8,128)S(1)} %add.67.use_0), channel_id=1, source_target_pairs={{0,4},{1,5},{2,6},{3,7},{4,0},{5,1},{6,2},{7,3},{8,12},{9,13},{10,... | collective-permute-start | bytes 221192 | tf_op jit(solution)/shard_map/ppermute | solution.py:373
  42.4 4.4 %collective-permute-start.7 = (f32[48,384]{1,0:T(8,128)S(1)}, f32[48,384]{1,0:T(8,128)S(1)}, u32[]{:S(2)}, u32[]{:S(2)}) collective-permute-start(f32[48,384]{1,0:T(8,128)S(1)} %add.67.use_0), channel_id=1, source_target_pairs={{0,6},{1,7},{2,0},{3,1},{4,2},{5,3},{6,4},{7,5},{8,14},{9,15},{10,... | collective-permute-start | bytes 221192 | tf_op jit(solution)/shard_map/ppermute | solution.py:373
  56.7 1.3 collective-permute-start.8
  58.0 6.0 %collective-permute-start.10 = (f32[48,384]{1,0:T(8,128)S(1)}, f32[48,384]{1,0:T(8,128)S(1)}, u32[]{:S(2)}, u32[]{:S(2)}) collective-permute-start(f32[48,384]{1,0:T(8,128)S(1)} %add.68.use_0), channel_id=1, source_target_pairs={{0,4},{1,5},{2,6},{3,7},{4,0},{5,1},{6,2},{7,3},{8,12},{9,13},{10,... | collective-permute-start | bytes 221192 | tf_op jit(solution)/shard_map/ppermute | solution.py:373
  59.9 5.4 %collective-permute-start.11 = (f32[48,384]{1,0:T(8,128)S(1)}, f32[48,384]{1,0:T(8,128)S(1)}, u32[]{:S(2)}, u32[]{:S(2)}) collective-permute-start(f32[48,384]{1,0:T(8,128)S(1)} %add.68.use_0), channel_id=1, source_target_pairs={{0,6},{1,7},{2,0},{3,1},{4,2},{5,3},{6,4},{7,5},{8,14},{9,15},{10,... | collective-permute-start | bytes 221192 | tf_op jit(solution)/shard_map/ppermute | solution.py:373
  61.9 5.6 %collective-permute-start.9 = (f32[48,384]{1,0:T(8,128)S(1)}, f32[48,384]{1,0:T(8,128)S(1)}, u32[]{:S(2)}, u32[]{:S(2)}) collective-permute-start(f32[48,384]{1,0:T(8,128)S(1)} %add.68.use_0), channel_id=1, source_target_pairs={{0,2},{1,3},{2,4},{3,5},{4,6},{5,7},{6,0},{7,1},{8,10},{9,11},{10,... | collective-permute-start | bytes 221192 | tf_op jit(solution)/shard_map/ppermute | solution.py:373
  78.7 7.2 %collective-permute-start.13 = (f32[48,384]{1,0:T(8,128)S(1)}, f32[48,384]{1,0:T(8,128)S(1)}, u32[]{:S(2)}, u32[]{:S(2)}) collective-permute-start(f32[48,384]{1,0:T(8,128)S(1)} %add.69.use_0), channel_id=1, source_target_pairs={{0,2},{1,3},{2,4},{3,5},{4,6},{5,7},{6,0},{7,1},{8,10},{9,11},{10,... | collective-permute-start | bytes 221192 | tf_op jit(solution)/shard_map/ppermute | solution.py:373
  78.8 7.1 %collective-permute-start.14 = (f32[48,384]{1,0:T(8,128)S(1)}, f32[48,384]{1,0:T(8,128)S(1)}, u32[]{:S(2)}, u32[]{:S(2)}) collective-permute-start(f32[48,384]{1,0:T(8,128)S(1)} %add.69.use_0), channel_id=1, source_target_pairs={{0,4},{1,5},{2,6},{3,7},{4,0},{5,1},{6,2},{7,3},{8,12},{9,13},{10,... | collective-permute-start | bytes 221192 | tf_op jit(solution)/shard_map/ppermute | solution.py:373
  80.7 5.7 %collective-permute-start.15 = (f32[48,384]{1,0:T(8,128)S(1)}, f32[48,384]{1,0:T(8,128)S(1)}, u32[]{:S(2)}, u32[]{:S(2)}) collective-permute-start(f32[48,384]{1,0:T(8,128)S(1)} %add.69.use_0), channel_id=1, source_target_pairs={{0,6},{1,7},{2,0},{3,1},{4,2},{5,3},{6,4},{7,5},{8,14},{9,15},{10,... | collective-permute-start | bytes 221192 | tf_op jit(solution)/shard_map/ppermute | solution.py:373
  97.5 12.8 %collective-permute-start.23 = (f32[4,224,128]{2,1,0:T(8,128)S(1)}, f32[4,224,128]{2,1,0:T(8,128)S(1)}, u32[]{:S(2)}, u32[]{:S(2)}) collective-permute-start(f32[4,224,128]{2,1,0:T(8,128)S(1)} %get-tuple-element.81), channel_id=1, source_target_pairs={{0,32},{8,40},{16,48},{24,56},{32,64},{40,72},{48,80},{56,88},{64,... | collective-permute-start | bytes 1376264 | tf_op jit(solution)/shard_map/ppermute | solution.py:397
  98.9 11.4 %collective-permute-start.24 = (f32[4,224,128]{2,1,0:T(8,128)S(1)}, f32[4,224,128]{2,1,0:T(8,128)S(1)}, u32[]{:S(2)}, u32[]{:S(2)}) collective-permute-start(f32[4,224,128]{2,1,0:T(8,128)S(1)} %get-tuple-element.82), channel_id=1, source_target_pairs={{0,96},{8,104},{16,112},{24,120},{32,0},{40,8},{48,16},{56,24},{64... | collective-permute-start | bytes 1376264 | tf_op jit(solution)/shard_map/ppermute | solution.py:397
  100.7 13.8 %collective-permute-start.16 = (f32[4,224,128]{2,1,0:T(8,128)S(1)}, f32[4,224,128]{2,1,0:T(8,128)S(1)}, u32[]{:S(2)}, u32[]{:S(2)}) collective-permute-start(f32[4,224,128]{2,1,0:T(8,128)S(1)} %get-tuple-element.70), channel_id=1, source_target_pairs={{0,8},{8,16},{16,24},{24,0},{32,40},{40,48},{48,56},{56,32},{64,72... | collective-permute-start | bytes 1376264 | tf_op jit(solution)/shard_map/ppermute | solution.py:397
  102.1 12.5 %collective-permute-start.17 = (f32[4,224,128]{2,1,0:T(8,128)S(1)}, f32[4,224,128]{2,1,0:T(8,128)S(1)}, u32[]{:S(2)}, u32[]{:S(2)}) collective-permute-start(f32[4,224,128]{2,1,0:T(8,128)S(1)} %get-tuple-element.71), channel_id=1, source_target_pairs={{0,24},{8,0},{16,8},{24,16},{32,56},{40,32},{48,40},{56,48},{64,88... | collective-permute-start | bytes 1376264 | tf_op jit(solution)/shard_map/ppermute | solution.py:397
  111.3 21.8 %collective-permute-start.25 = (f32[2,4,224,128]{3,2,1,0:T(8,128)S(1)}, f32[2,4,224,128]{3,2,1,0:T(8,128)S(1)}, u32[]{:S(2)}, u32[]{:S(2)}) collective-permute-start(f32[2,4,224,128]{3,2,1,0:T(8,128)S(1)} %get-tuple-element.85), channel_id=1, source_target_pairs={{0,32},{8,40},{16,48},{24,56},{32,64},{40,72},{48,80},{56,88},{64,... | collective-permute-start | bytes 2752520 | tf_op jit(solution)/shard_map/ppermute | solution.py:397
  112.7 20.4 %collective-permute-start.26 = (f32[2,4,224,128]{3,2,1,0:T(8,128)S(1)}, f32[2,4,224,128]{3,2,1,0:T(8,128)S(1)}, u32[]{:S(2)}, u32[]{:S(2)}) collective-permute-start(f32[2,4,224,128]{3,2,1,0:T(8,128)S(1)} %get-tuple-element.86), channel_id=1, source_target_pairs={{0,96},{8,104},{16,112},{24,120},{32,0},{40,8},{48,16},{56,24},{64... | collective-permute-start | bytes 2752520 | tf_op jit(solution)/shard_map/ppermute | solution.py:397
  115.5 24.2 %collective-permute-start.18 = (f32[2,4,224,128]{3,2,1,0:T(8,128)S(1)}, f32[2,4,224,128]{3,2,1,0:T(8,128)S(1)}, u32[]{:S(2)}, u32[]{:S(2)}) collective-permute-start(f32[2,4,224,128]{3,2,1,0:T(8,128)S(1)} %get-tuple-element.72), channel_id=1, source_target_pairs={{0,8},{8,16},{16,24},{24,0},{32,40},{40,48},{48,56},{56,32},{64,72... | collective-permute-start | bytes 2752520 | tf_op jit(solution)/shard_map/ppermute | solution.py:397
  117.3 22.5 %collective-permute-start.19 = (f32[2,4,224,128]{3,2,1,0:T(8,128)S(1)}, f32[2,4,224,128]{3,2,1,0:T(8,128)S(1)}, u32[]{:S(2)}, u32[]{:S(2)}) collective-permute-start(f32[2,4,224,128]{3,2,1,0:T(8,128)S(1)} %get-tuple-element.73), channel_id=1, source_target_pairs={{0,24},{8,0},{16,8},{24,16},{32,56},{40,32},{48,40},{56,48},{64,88... | collective-permute-start | bytes 2752520 | tf_op jit(solution)/shard_map/ppermute | solution.py:397
  134.1 11.2 %collective-permute-start.27 = (f32[448,128]{1,0:T(8,128)S(1)}, f32[448,128]{1,0:T(8,128)S(1)}, u32[]{:S(2)}, u32[]{:S(2)}) collective-permute-start(f32[448,128]{1,0:T(8,128)S(1)} %get-tuple-element.89), channel_id=1, source_target_pairs={{0,8},{8,16},{16,24},{24,0},{32,40},{40,48},{48,56},{56,32},{64,72... | collective-permute-start | bytes 688136 | tf_op jit(solution)/shard_map/ppermute | solution.py:397
  135.9 11.3 %collective-permute-start.28 = (f32[448,128]{1,0:T(8,128)S(1)}, f32[448,128]{1,0:T(8,128)S(1)}, u32[]{:S(2)}, u32[]{:S(2)}) collective-permute-start(f32[448,128]{1,0:T(8,128)S(1)} %get-tuple-element.90), channel_id=1, source_target_pairs={{0,16},{8,24},{16,0},{24,8},{32,48},{40,56},{48,32},{56,40},{64,80... | collective-permute-start | bytes 688136 | tf_op jit(solution)/shard_map/ppermute | solution.py:397
  138.1 9.1 %collective-permute-start.29 = (f32[448,128]{1,0:T(8,128)S(1)}, f32[448,128]{1,0:T(8,128)S(1)}, u32[]{:S(2)}, u32[]{:S(2)}) collective-permute-start(f32[448,128]{1,0:T(8,128)S(1)} %get-tuple-element.91), channel_id=1, source_target_pairs={{0,24},{8,0},{16,8},{24,16},{32,56},{40,32},{48,40},{56,48},{64,88... | collective-permute-start | bytes 688136 | tf_op jit(solution)/shard_map/ppermute | solution.py:397
  140.9 10.1 %collective-permute-start.20 = (f32[448,128]{1,0:T(8,128)S(1)}, f32[448,128]{1,0:T(8,128)S(1)}, u32[]{:S(2)}, u32[]{:S(2)}) collective-permute-start(f32[448,128]{1,0:T(8,128)S(1)} %get-tuple-element.75), channel_id=1, source_target_pairs={{0,32},{8,40},{16,48},{24,56},{32,64},{40,72},{48,80},{56,88},{64,... | collective-permute-start | bytes 688136 | tf_op jit(solution)/shard_map/ppermute | solution.py:397
  141.9 10.1 %collective-permute-start.21 = (f32[448,128]{1,0:T(8,128)S(1)}, f32[448,128]{1,0:T(8,128)S(1)}, u32[]{:S(2)}, u32[]{:S(2)}) collective-permute-start(f32[448,128]{1,0:T(8,128)S(1)} %get-tuple-element.76), channel_id=1, source_target_pairs={{0,64},{8,72},{16,80},{24,88},{32,96},{40,104},{48,112},{56,120},{... | collective-permute-start | bytes 688136 | tf_op jit(solution)/shard_map/ppermute | solution.py:397
  145.3 6.7 %collective-permute-start.22 = (f32[448,128]{1,0:T(8,128)S(1)}, f32[448,128]{1,0:T(8,128)S(1)}, u32[]{:S(2)}, u32[]{:S(2)}) collective-permute-start(f32[448,128]{1,0:T(8,128)S(1)} %get-tuple-element.77), channel_id=1, source_target_pairs={{0,96},{8,104},{16,112},{24,120},{32,0},{40,8},{48,16},{56,24},{64... | collective-permute-start | bytes 688136 | tf_op jit(solution)/shard_map/ppermute | solution.py:397
  148.1 11.0 %collective-permute-start.33 = (f32[448,128]{1,0:T(8,128)S(1)}, f32[448,128]{1,0:T(8,128)S(1)}, u32[]{:S(2)}, u32[]{:S(2)}) collective-permute-start(f32[448,128]{1,0:T(8,128)S(1)} %get-tuple-element.94), channel_id=1, source_target_pairs={{0,24},{8,0},{16,8},{24,16},{32,56},{40,32},{48,40},{56,48},{64,88... | collective-permute-start | bytes 688136 | tf_op jit(solution)/shard_map/ppermute | solution.py:397
  150.4 9.9 %collective-permute-start.34 = (f32[448,128]{1,0:T(8,128)S(1)}, f32[448,128]{1,0:T(8,128)S(1)}, u32[]{:S(2)}, u32[]{:S(2)}) collective-permute-start(f32[448,128]{1,0:T(8,128)S(1)} %get-tuple-element.94), channel_id=1, source_target_pairs={{0,16},{8,24},{16,0},{24,8},{32,48},{40,56},{48,32},{56,40},{64,80... | collective-permute-start | bytes 688136 | tf_op jit(solution)/shard_map/ppermute | solution.py:397
  151.0 11.8 %collective-permute-start.35 = (f32[448,128]{1,0:T(8,128)S(1)}, f32[448,128]{1,0:T(8,128)S(1)}, u32[]{:S(2)}, u32[]{:S(2)}) collective-permute-start(f32[448,128]{1,0:T(8,128)S(1)} %get-tuple-element.94), channel_id=1, source_target_pairs={{0,8},{8,16},{16,24},{24,0},{32,40},{40,48},{48,56},{56,32},{64,72... | collective-permute-start | bytes 688136 | tf_op jit(solution)/shard_map/ppermute | solution.py:397
  153.5 9.3 %collective-permute-start.32 = (f32[456,128]{1,0:T(8,128)S(1)}, f32[456,128]{1,0:T(8,128)S(1)}, u32[]{:S(2)}, u32[]{:S(2)}) collective-permute-start(f32[456,128]{1,0:T(8,128)S(1)} %get-tuple-element.93), channel_id=1, source_target_pairs={{0,32},{8,40},{16,48},{24,56},{32,64},{40,72},{48,80},{56,88},{64,... | collective-permute-start | bytes 700424 | tf_op jit(solution)/shard_map/ppermute | solution.py:397
  155.0 9.3 %collective-permute-start.30 = (f32[456,128]{1,0:T(8,128)S(1)}, f32[456,128]{1,0:T(8,128)S(1)}, u32[]{:S(2)}, u32[]{:S(2)}) collective-permute-start(f32[456,128]{1,0:T(8,128)S(1)} %get-tuple-element.93), channel_id=1, source_target_pairs={{0,96},{8,104},{16,112},{24,120},{32,0},{40,8},{48,16},{56,24},{64... | collective-permute-start | bytes 700424 | tf_op jit(solution)/shard_map/ppermute | solution.py:397
  159.0 7.8 %collective-permute-start.31 = (f32[456,128]{1,0:T(8,128)S(1)}, f32[456,128]{1,0:T(8,128)S(1)}, u32[]{:S(2)}, u32[]{:S(2)}) collective-permute-start(f32[456,128]{1,0:T(8,128)S(1)} %get-tuple-element.93), channel_id=1, source_target_pairs={{0,64},{8,72},{16,80},{24,88},{32,96},{40,104},{48,112},{56,120},{... | collective-permute-start | bytes 700424 | tf_op jit(solution)/shard_map/ppermute | solution.py:397
  167.0 22.4 %collective-permute-start.42 = (f32[2,4,224,128]{3,2,1,0:T(8,128)S(1)}, f32[2,4,224,128]{3,2,1,0:T(8,128)S(1)}, u32[]{:S(2)}, u32[]{:S(2)}) collective-permute-start(f32[2,4,224,128]{3,2,1,0:T(8,128)S(1)} %pad_maximum_fusion.refs_0_), channel_id=1, source_target_pairs={{0,8},{8,16},{16,24},{24,0},{32,40},{40,48},{48,56},{56,32},{64,72... | collective-permute-start | bytes 2752520 | tf_op jit(solution)/shard_map/ppermute | solution.py:397
  167.9 21.6 %collective-permute-start.41 = (f32[2,4,224,128]{3,2,1,0:T(8,128)S(1)}, f32[2,4,224,128]{3,2,1,0:T(8,128)S(1)}, u32[]{:S(2)}, u32[]{:S(2)}) collective-permute-start(f32[2,4,224,128]{3,2,1,0:T(8,128)S(1)} %pad_maximum_fusion.refs_0_), channel_id=1, source_target_pairs={{0,24},{8,0},{16,8},{24,16},{32,56},{40,32},{48,40},{56,48},{64,88... | collective-permute-start | bytes 2752520 | tf_op jit(solution)/shard_map/ppermute | solution.py:397
  171.0 21.8 %collective-permute-start.46 = (f32[2,4,224,128]{3,2,1,0:T(8,128)S(1)}, f32[2,4,224,128]{3,2,1,0:T(8,128)S(1)}, u32[]{:S(2)}, u32[]{:S(2)}) collective-permute-start(f32[2,4,224,128]{3,2,1,0:T(8,128)S(1)} %pad_maximum_fusion.1.refs_5_), channel_id=1, source_target_pairs={{0,32},{8,40},{16,48},{24,56},{32,64},{40,72},{48,80},{56,88},{64,... | collective-permute-start | bytes 2752520 | tf_op jit(solution)/shard_map/ppermute | solution.py:397
  171.0 3.2 %collective-permute-start.36 = (f32[8,128]{1,0:T(8,128)S(1)}, f32[8,128]{1,0:T(8,128)S(1)}, u32[]{:S(2)}, u32[]{:S(2)}) collective-permute-start(f32[8,128]{1,0:T(8,128)S(1)} %fusion.2), channel_id=1, source_target_pairs={{0,1},{1,0},{2,3},{3,2},{4,5},{5,4},{6,7},{7,6},{8,9},{9,8},{10,11... | collective-permute-start | bytes 12296 | tf_op jit(solution)/shard_map/ppermute | solution.py:381
  171.0 23.5 %collective-permute-start.45 = (f32[2,4,224,128]{3,2,1,0:T(8,128)S(1)}, f32[2,4,224,128]{3,2,1,0:T(8,128)S(1)}, u32[]{:S(2)}, u32[]{:S(2)}) collective-permute-start(f32[2,4,224,128]{3,2,1,0:T(8,128)S(1)} %pad_maximum_fusion.1.refs_5_), channel_id=1, source_target_pairs={{0,96},{8,104},{16,112},{24,120},{32,0},{40,8},{48,16},{56,24},{64... | collective-permute-start | bytes 2752520 | tf_op jit(solution)/shard_map/ppermute | solution.py:397
  174.2 3.6 %collective-permute-start.37 = (f32[8,128]{1,0:T(8,128)S(1)}, f32[8,128]{1,0:T(8,128)S(1)}, u32[]{:S(2)}, u32[]{:S(2)}) collective-permute-start(f32[8,128]{1,0:T(8,128)S(1)} %add.73), channel_id=1, source_target_pairs={{0,2},{1,3},{2,0},{3,1},{4,6},{5,7},{6,4},{7,5},{8,10},{9,11},{10,... | collective-permute-start | bytes 12296 | tf_op jit(solution)/shard_map/ppermute | solution.py:381
  177.8 20.5 %collective-permute-start.38 = (f32[8,128]{1,0:T(8,128)S(1)}, f32[8,128]{1,0:T(8,128)S(1)}, u32[]{:S(2)}, u32[]{:S(2)}) collective-permute-start(f32[8,128]{1,0:T(8,128)S(1)} %add.74), channel_id=1, source_target_pairs={{0,6},{1,7},{2,4},{3,5},{4,2},{5,3},{6,0},{7,1},{8,14},{9,15},{10,... | collective-permute-start | bytes 12296 | tf_op jit(solution)/shard_map/ppermute | solution.py:381
  189.4 17.4 %collective-permute-start.43 = (f32[4,224,128]{2,1,0:T(8,128)S(1)}, f32[4,224,128]{2,1,0:T(8,128)S(1)}, u32[]{:S(2)}, u32[]{:S(2)}) collective-permute-start(f32[4,224,128]{2,1,0:T(8,128)S(1)} %slice_bitcast_fusion.3), channel_id=1, source_target_pairs={{0,8},{8,16},{16,24},{24,0},{32,40},{40,48},{48,56},{56,32},{64,72... | collective-permute-start | bytes 1376264 | tf_op jit(solution)/shard_map/ppermute | solution.py:397
  189.5 17.3 %collective-permute-start.44 = (f32[4,224,128]{2,1,0:T(8,128)S(1)}, f32[4,224,128]{2,1,0:T(8,128)S(1)}, u32[]{:S(2)}, u32[]{:S(2)}) collective-permute-start(f32[4,224,128]{2,1,0:T(8,128)S(1)} %slice_bitcast_fusion.2), channel_id=1, source_target_pairs={{0,24},{8,0},{16,8},{24,16},{32,56},{40,32},{48,40},{56,48},{64,88... | collective-permute-start | bytes 1376264 | tf_op jit(solution)/shard_map/ppermute | solution.py:397
  192.9 14.0 %collective-permute-start.47 = (f32[4,224,128]{2,1,0:T(8,128)S(1)}, f32[4,224,128]{2,1,0:T(8,128)S(1)}, u32[]{:S(2)}, u32[]{:S(2)}) collective-permute-start(f32[4,224,128]{2,1,0:T(8,128)S(1)} %slice_bitcast_fusion.1), channel_id=1, source_target_pairs={{0,32},{8,40},{16,48},{24,56},{32,64},{40,72},{48,80},{56,88},{64,... | collective-permute-start | bytes 1376264 | tf_op jit(solution)/shard_map/ppermute | solution.py:397
  194.5 13.4 %collective-permute-start.48 = (f32[4,224,128]{2,1,0:T(8,128)S(1)}, f32[4,224,128]{2,1,0:T(8,128)S(1)}, u32[]{:S(2)}, u32[]{:S(2)}) collective-permute-start(f32[4,224,128]{2,1,0:T(8,128)S(1)} %slice_bitcast_fusion), channel_id=1, source_target_pairs={{0,96},{8,104},{16,112},{24,120},{32,0},{40,8},{48,16},{56,24},{64... | collective-permute-start | bytes 1376264 | tf_op jit(solution)/shard_map/ppermute | solution.py:397
  198.3 3.7 %collective-permute-start.39 = (f32[8,128]{1,0:T(8,128)S(1)}, f32[8,128]{1,0:T(8,128)S(1)}, u32[]{:S(2)}, u32[]{:S(2)}) collective-permute-start(f32[8,128]{1,0:T(8,128)S(1)} %add.75), channel_id=1, source_target_pairs={{0,8},{8,0},{16,24},{24,16},{32,40},{40,32},{48,56},{56,48},{64,72... | collective-permute-start | bytes 12296 | tf_op jit(solution)/shard_map/ppermute | solution.py:387
  202.0 4.8 %collective-permute-start.40 = (f32[8,128]{1,0:T(8,128)S(1)}, f32[8,128]{1,0:T(8,128)S(1)}, u32[]{:S(2)}, u32[]{:S(2)}) collective-permute-start(f32[8,128]{1,0:T(8,128)S(1)} %add.76), channel_id=1, source_target_pairs={{0,24},{8,16},{16,8},{24,0},{32,56},{40,48},{48,40},{56,32},{64,88... | collective-permute-start | bytes 12296 | tf_op jit(solution)/shard_map/ppermute | solution.py:387
  (9 other events, 112.1 us)
